TPU v7x, 512 devices: a whole 4x4x16 slice. The times are simulated.
512 devices in a mesh: slab: 8 (over y, core), pair: 64 (over x, z).
Axes of the slice: x: 4, y: 4, z: 16, core: 2. Of those that a mesh axis runs over, the one named last changes fastest.
Arguments:
- amplitudes: bfloat16 [1024, 16384], P('pair', 'slab'), may hold values from -6 to 6
- integrals: bfloat16 [16384, 65536], P('slab', 'pair'), may hold values from -0.125 to 0.125
- contract_irrep: int32 [16384], replicated, may hold values from 0 to 7, as said below
- outer_irrep: int32 [65536], replicated, may hold values from 0 to 7, as said below
- block_map: int32 [8, 8], replicated, may hold values from 0 to 1, as said below
Outputs:
- ladder: float32 [1024, 65536], P('slab', 'pair')
Inputs may be any that keep to these rules, and one draw needn't show every extreme that they name: `contract_irrep`: each irrep label occupies exactly one contiguous run of contracted virtual pairs, whose length is a positive multiple of 64. `outer_irrep`: each irrep label occupies exactly one contiguous run of outer virtual pairs, whose length is a positive multiple of 64. Each row and each column of block_map holds exactly one 1.
All inputs are finite; a program needn't handle non-finite values.
Results may differ from a plain program's by a relative error of at most 0.0003.
Values may be sent and summed in bfloat16 or wider, within the bound.
No kernel may reach another device: no remote copies, remote signals or barrier semaphores. Data moves between devices by JAX's collectives and lax.ppermute only.
A program may use at most 64 MiB of HBM per device.

v0:
```python
import jax
import jax.numpy as jnp
from jax import lax
from jax.sharding import PartitionSpec as P


def body(amplitudes, integrals, contract_irrep, outer_irrep, block_map):
    row_count = integrals.shape[0]
    col_count = integrals.shape[1]
    row_labels = lax.dynamic_slice_in_dim(
        contract_irrep, lax.axis_index("slab") * row_count, row_count, 0
    )
    col_labels = lax.dynamic_slice_in_dim(
        outer_irrep, lax.axis_index("pair") * col_count, col_count, 0
    )
    levels = jnp.arange(block_map.shape[0], dtype=jnp.int32)
    row_hot = (row_labels[:, None] == levels[None, :]).astype(jnp.bfloat16)
    col_hot = (col_labels[None, :] == levels[:, None]).astype(jnp.bfloat16)
    row_map = jnp.dot(
        row_hot, block_map.astype(jnp.bfloat16), preferred_element_type=jnp.float32
    ).astype(jnp.bfloat16)
    keep_mask = jnp.dot(row_map, col_hot, preferred_element_type=jnp.bfloat16)
    blocked = jnp.where(keep_mask > 0.5, integrals, jnp.zeros_like(integrals))
    partial_value = jnp.dot(
        lax.all_gather(amplitudes, "pair", axis=0, tiled=True),
        blocked,
        preferred_element_type=jnp.float32,
    )
    summed = lax.psum(partial_value, "slab")
    own_rows = summed.shape[0] // lax.axis_size("slab")
    return lax.dynamic_slice_in_dim(summed, lax.axis_index("slab") * own_rows, own_rows, 0)


def solution(mesh):
    in_specs = (P("pair", "slab"), P("slab", "pair"), P(), P(), P())
    out_specs = P("slab", "pair")
    return jax.shard_map(body, mesh=mesh, in_specs=in_specs, out_specs=out_specs, check_vma=False)
```

profile of v0, /device:TPU:1, one launch (start us, length us, event | category | flops | bytes accessed | tf_op | source)
XLA Modules:
  0.0 263.1 jit_solution(6869850255132488543)
XLA Ops:
  6.5 0.0 all-gather.2.cloned.1.call-start
  6.5 0.7 all-gather.2.cloned.1.call-update
  7.3 0.0 all-reduce.2.cloned.1.call-start
  7.3 0.7 dynamic_slice.10
  8.0 0.7 dynamic_slice.9
  8.7 1.1 convolution_convert_fusion
  9.8 144.2 %all-gather.2.cloned.1.call-done = bf16[1024,2048]{1,0:T(8,128)(2,1)} async-done(((bf16[16,2048]{1,0:T(8,128)(2,1)}), bf16[1024,2048]{1,0:T(8,128)(2,1)}) %all-gather.2.cloned.1.call-update) | async-done | bytes 4194320 | tf_op jit(solution)/shard_map/all_gather | solution.py:25
  154.1 11.0 %fusion.1 = f32[1024,1024]{0,1:T(8,128)} fusion(bf16[1024,2048]{1,0:T(8,128)(2,1)} %all-gather.2.cloned.1.call-done, bf16[2048,1024]{1,0:T(8,128)(2,1)} %param.6, bf16[2048,8]{1,0:T(8,128)(2,1)S(1)} %convolution_convert_fusion, s32[1024]{0:T(1024)S(1)} %dynamic_slice.10), kind=kOutput, calls=%fused_computation.3 | convolution fusion | flops 4332724224 | bytes 12619776 | tf_op jit(solution)/shard_map/dot_general | solution.py:24
  165.0 0.0 all-reduce.2.cloned.1.call-update
  165.1 89.1 %all-reduce.2.cloned.1.call-done = f32[1024,1024]{0,1:T(8,128)} async-done(((f32[1024,1024]{0,1:T(8,128)}), f32[1024,1024]{0,1:T(8,128)}) %all-reduce.2.cloned.1.call-update) | async-done | bytes 4194320 | tf_op jit(solution)/shard_map/psum | solution.py:29
  254.1 1.1 constant_dynamic-slice_fusion
  255.2 1.0 copy.6
Async XLA Ops:
  6.5 147.5 %all-gather.2.cloned.1.call-start = ((), (), s32[]{:S(2)}) async-start(), calls=%async_computation | async-start | bytes 4259840 | tf_op jit(solution)/shard_map/all_gather | solution.py:25
  7.3 246.9 %all-reduce.2.cloned.1.call-start = ((), (), s32[]{:S(2)}) async-start(), calls=%async_computation.1 | async-start | bytes 8388608 | tf_op jit(solution)/shard_map/psum | solution.py:29
Sparse Core Ops, SparseCore 0:
  10.3 143.7 all-gather.1
  165.2 88.9 all-reduce.1
where the time goes:
time: 264 us; the launch traced here: 263 us
  waiting for transfers between devices  234 us (89%)
  between operations  13.4 us (5%)
  matrix products  12.1 us (5%)
  local copies, waits for them, and re-layouts  3.46 us (1%)
    all_gather x1, waiting for transfers between devices, body(): lax.all_gather(amplitudes, 'pair', axis=0, tiled=True)  144 us
    psum x1, waiting for transfers between devices, body(): summed = lax.psum(partial_value, 'slab')  89.1 us
    dot_general x1, matrix products, body(): jnp.dot(lax.all_gather(amplitudes, 'pair', axis=0, tiled=True), blocked,...  11 us
  transfers between devices with their start and end apart: 2, of which 2 were waited for; matrix products, arithmetic and copies ran while one was open for 1% of the time, Pallas kernels for 0%

commit v1 on v0

v1 whole, which is shorter than its diff:
```python
import jax
import jax.numpy as jnp
from jax import lax
from jax.sharding import Mesh, PartitionSpec as P

Y, CORE, X, Z = 4, 2, 4, 16
HALF = Z // CORE


def blocked_integrals(integrals, contract_irrep, outer_irrep, block_map):
    rows, cols = integrals.shape
    slab = lax.axis_index("y") * CORE + lax.axis_index("core")
    pair = lax.axis_index("x") * Z + lax.axis_index("z")
    row_labels = lax.dynamic_slice_in_dim(contract_irrep, slab * rows, rows, 0)
    col_labels = lax.dynamic_slice_in_dim(outer_irrep, pair * cols, cols, 0)
    levels = jnp.arange(block_map.shape[0], dtype=jnp.int32)
    partner = jnp.sum(block_map * levels[None, :], axis=1)
    row_partner = jnp.sum(
        jnp.where(row_labels[:, None] == levels[None, :], partner[None, :], 0), axis=1
    )
    keep = row_partner[:, None] == col_labels[None, :]
    return jnp.where(keep, integrals, jnp.zeros_like(integrals))


def over_z(value, step):
    return lax.ppermute(value, "z", [(i, (i + step) % Z) for i in range(Z)])


def apart(value, axis, size, step):
    pairs = []
    for core in range(CORE):
        for i in range(size):
            to = (i + (step if core == 0 else -step)) % size
            pairs.append((core * size + i, core * size + to))
    return lax.ppermute(value, ("core", axis), pairs)


def spread(value, offset):
    pairs = []
    for y in range(Y):
        for k in range(CORE):
            for x in range(X):
                for z in range(Z):
                    source = HALF * k + (z + offset) % HALF
                    sender = z // HALF
                    pairs.append(
                        (
                            ((y * CORE + sender) * X + (x + y) % X) * Z + source,
                            ((y * CORE + k) * X + x) * Z + z,
                        )
                    )
    return lax.ppermute(value, ("y", "core", "x", "z"), pairs)


def hand_in(value, t):
    pairs = []
    for y in range(Y):
        for core in range(CORE):
            for x in range(X):
                to = (x + y - t) % Y if core == 0 else (x + y + t) % Y
                pairs.append(((y * CORE + core) * X + x, (to * CORE + core) * X + x))
    return lax.ppermute(value, ("y", "core", "x"), pairs)


def body(amplitudes, integrals, contract_irrep, outer_irrep, block_map):
    core, z = lax.axis_index("core"), lax.axis_index("z")
    rows, depth = amplitudes.shape
    swap = [(0, 1), (1, 0)]

    other = lax.ppermute(amplitudes, "core", swap)
    own = jnp.concatenate(
        [jnp.where(core == 0, amplitudes, other), jnp.where(core == 0, other, amplitudes)], axis=1
    )

    first = spread(own, 0)
    second = spread(own, 4)
    blocked = blocked_integrals(integrals, contract_irrep, outer_irrep, block_map)
    blocked_other = lax.ppermute(blocked, "core", swap)

    here = jnp.concatenate([first, second])
    turned = jnp.concatenate(
        [jnp.where(core == 0, first, second), jnp.where(core == 0, second, first)]
    )
    below = over_z(here, 1)
    above = over_z(here, -1)
    far = apart(turned, "z", Z, 2)

    pieces = [here, below, above, far]
    received = []
    for t in range(X):
        if t:
            pieces = [apart(piece, "x", X, 1) for piece in pieces]
        h, b, a, f = pieces
        block = jnp.concatenate(
            [f[:rows], b[:rows], h[:rows], a[:rows], f[rows:], b[rows:], h[rows:], a[rows:]]
        )
        mine = lax.dynamic_slice_in_dim(block, core * depth, depth, 1)
        theirs = lax.dynamic_slice_in_dim(block, (1 - core) * depth, depth, 1)
        partial = jnp.dot(mine, blocked, preferred_element_type=jnp.float32) + jnp.dot(
            theirs, blocked_other, preferred_element_type=jnp.float32
        )
        received.append(hand_in(partial, t))
    total = (received[0] + received[1]) + (received[2] + received[3])
    return jnp.roll(total, (z + HALF - 2) % HALF * rows, axis=0)


def solution(mesh):
    grid = Mesh(mesh.devices.reshape(Y, CORE, X, Z), ("y", "core", "x", "z"))
    slab, pair = ("y", "core"), ("x", "z")
    in_specs = (P(pair, slab), P(slab, pair), P(), P(), P())
    return jax.shard_map(
        body, mesh=grid, in_specs=in_specs, out_specs=P(slab, pair), check_vma=False
    )
```

time: 264 us -> 153 us (0.58)
  waiting for transfers between devices: 234 us -> 35.6 us
  starting transfers between devices: 0.04 us -> 80 us
  between operations: 13.4 us -> 0.7 us
  matrix products: 12.1 us -> 24.2 us
  other arithmetic: 0 us -> 8.02 us
    all_gather x1 -> x0, waiting for transfers between devices: 144 us -> none  [body(): lax.all_gather(amplitudes, 'pair', axis=0, tiled=True)]
    psum x1 -> x0, waiting for transfers between devices: 89.1 us -> none  [body(): summed = lax.psum(partial_value, 'slab')]
    ppermute x0 -> x23, starting transfers between devices: none -> 80 us  [the longest x13 36.3 us: apart(): return lax.ppermute(value, ('core', axis), pairs)]
    ppermute x0 -> x23, waiting for transfers between devices: none -> 35.6 us  [the longest x4 19.3 us: hand_in(): return lax.ppermute(value, ('y', 'core', 'x'), pairs)]
    dot_general x2 -> x8, matrix products: 12.1 us -> 24.2 us  [the longest x4 12.6 us: body(): jnp.dot(mine, blocked, preferred_element_type=jnp.float32)]
    select_n x0 -> x3, other arithmetic: none -> 5 us  [the longest x1 4.1 us: blocked_integrals(): return jnp.where(keep, integrals, jnp.zeros_like(integrals))]
  transfers between devices with their start and end apart: 2 -> 23, of which waited for: 2 -> 7; matrix products, arithmetic and copies ran while one was open for 1% -> 4% of each run, Pallas kernels for 0% -> 0%
where the time goes in v1:
time: 153 us; the launch traced here: 150 us
  starting transfers between devices  80 us (52%)
  waiting for transfers between devices  35.6 us (23%)
  matrix products  24.2 us (16%)
  other arithmetic  8.02 us (5%)
  local copies, waits for them, and re-layouts  1.75 us (1%)
    ppermute x13, starting transfers between devices, apart(): return lax.ppermute(value, ('core', axis), pairs)  36.3 us
    ppermute x4, waiting for transfers between devices, hand_in(): return lax.ppermute(value, ('y', 'core', 'x'), pairs)  19.3 us
    ppermute x4, starting transfers between devices, hand_in(): return lax.ppermute(value, ('y', 'core', 'x'), pairs)  14.9 us
    dot_general x4, matrix products, body(): jnp.dot(mine, blocked, preferred_element_type=jnp.float32)  12.6 us
    ppermute x2, starting transfers between devices, spread(): return lax.ppermute(value, ('y', 'core', 'x', 'z'), pairs)  12.2 us
    dot_general x4, matrix products, body(): jnp.dot(theirs, blocked_other, preferred_element_type=jnp.float32)  11.6 us
    ppermute x2, waiting for transfers between devices, spread(): return lax.ppermute(value, ('y', 'core', 'x', 'z'), pairs)  10.3 us
    ppermute x1, starting transfers between devices, body(): other = lax.ppermute(amplitudes, 'core', swap)  8.77 us
  transfers between devices with their start and end apart: 23, of which 7 were waited for; matrix products, arithmetic and copies ran while one was open for 4% of the time, Pallas kernels for 0%

profile of v1, /device:TPU:1, one launch (start us, length us, event | category | flops | bytes accessed | tf_op | source)
XLA Modules:
  0.0 150.3 jit_solution(5740602687880809215)
XLA Ops:
  0.0 8.8 %collective-permute-start = (bf16[16,2048]{1,0:T(8,128)(2,1)}, bf16[16,2048]{1,0:T(8,128)(2,1)S(1)}, u32[]{:S(2)}, u32[]{:S(2)}) collective-permute-start(bf16[16,2048]{1,0:T(8,128)(2,1)} %param.5), channel_id=1, source_target_pairs={{0,64},{64,0},{1,65},{65,1},{2,66},{66,2},{3,67},{67,3},{4,68},{68... | collective-permute-start | bytes 196616 | tf_op jit(solution)/shard_map/ppermute | solution.py:70
  8.8 1.1 collective-permute-done
  9.9 0.9 broadcast_select_fusion.3
  10.7 10.3 %collective-permute-start.1 = (bf16[16,4096]{1,0:T(8,128)(2,1)S(1)}, bf16[16,4096]{1,0:T(8,128)(2,1)S(1)}, u32[]{:S(2)}, u32[]{:S(2)}) collective-permute-start(bf16[16,4096]{1,0:T(8,128)(2,1)S(1)} %pad_maximum_fusion.1), channel_id=1, source_target_pairs={{0,0},{1,1},{2,2},{3,3},{4,4},{5,5},{6,6},{7,7},{64,8},{65,9},{66,... | collective-permute-start | bytes 393224 | tf_op jit(solution)/shard_map/ppermute | solution.py:52
  21.1 0.8 multiply_reduce_fusion
  21.9 0.7 dynamic_slice.36
  22.6 0.7 dynamic_slice.35
  23.3 0.1 select_reduce_fusion
  23.4 1.9 %collective-permute-start.2 = (bf16[16,4096]{1,0:T(8,128)(2,1)S(1)}, bf16[16,4096]{1,0:T(8,128)(2,1)S(1)}, u32[]{:S(2)}, u32[]{:S(2)}) collective-permute-start(bf16[16,4096]{1,0:T(8,128)(2,1)S(1)} %pad_maximum_fusion.1), channel_id=1, source_target_pairs={{4,0},{5,1},{6,2},{7,3},{0,4},{1,5},{2,6},{3,7},{68,8},{69,9},{70,... | collective-permute-start | bytes 393224 | tf_op jit(solution)/shard_map/ppermute | solution.py:52
  25.3 0.6 collective-permute-done.1
  25.9 9.7 %collective-permute-done.2 = bf16[16,4096]{1,0:T(8,128)(2,1)S(1)} collective-permute-done((bf16[16,4096]{1,0:T(8,128)(2,1)S(1)}, bf16[16,4096]{1,0:T(8,128)(2,1)S(1)}, u32[]{:S(2)}, u32[]{:S(2)}) %collective-permute-start.2) | collective-permute-done | bytes 131104 | tf_op jit(solution)/shard_map/ppermute | solution.py:52
  35.7 1.9 %collective-permute-start.3 = (bf16[32,4096]{1,0:T(8,128)(2,1)S(1)}, bf16[32,4096]{1,0:T(8,128)(2,1)S(1)}, u32[]{:S(2)}, u32[]{:S(2)}) collective-permute-start(bf16[32,4096]{1,0:T(8,128)(2,1)S(1)} %pad_maximum_fusion), channel_id=1, source_target_pairs={{0,2},{1,3},{2,4},{3,5},{4,6},{5,7},{6,8},{7,9},{8,10},{9,11},{10,... | collective-permute-start | bytes 786440 | tf_op jit(solution)/shard_map/ppermute | solution.py:35
  37.6 4.1 %compare_select_fusion = bf16[2048,1024]{1,0:T(8,128)(2,1)} fusion(bf16[2048,1024]{1,0:T(8,128)(2,1)} %param.6, s32[1024]{0:T(1024)S(1)} %dynamic_slice.36, s32[2048]{0:T(1024)S(1)} %select_reduce_fusion), kind=kLoop, calls=%fused_computation | loop fusion | flops 4194304 | bytes 8400896 | tf_op jit(solution)/shard_map/jit(_where)/select_n | solution.py:22
  41.7 1.9 %collective-permute-start.6 = (bf16[2048,1024]{1,0:T(8,128)(2,1)}, bf16[2048,1024]{1,0:T(8,128)(2,1)}, u32[]{:S(2)}, u32[]{:S(2)}) collective-permute-start(bf16[2048,1024]{1,0:T(8,128)(2,1)} %compare_select_fusion), channel_id=1, source_target_pairs={{0,64},{64,0},{1,65},{65,1},{2,66},{66,2},{3,67},{67,3},{4,68},{68... | collective-permute-start | bytes 12582920 | tf_op jit(solution)/shard_map/ppermute | solution.py:78
  43.6 4.1 %collective-permute-start.10 = (bf16[32,4096]{1,0:T(8,128)(2,1)S(1)}, bf16[32,4096]{1,0:T(8,128)(2,1)S(1)}, u32[]{:S(2)}, u32[]{:S(2)}) collective-permute-start(bf16[32,4096]{1,0:T(8,128)(2,1)S(1)} %get-tuple-element.7), channel_id=1, source_target_pairs={{0,16},{16,32},{32,48},{48,0},{64,112},{80,64},{96,80},{112,96},{1... | collective-permute-start | bytes 786440 | tf_op jit(solution)/shard_map/ppermute | solution.py:35
  47.7 1.9 %collective-permute-start.5 = (bf16[32,4096]{1,0:T(8,128)(2,1)S(1)}, bf16[32,4096]{1,0:T(8,128)(2,1)S(1)}, u32[]{:S(2)}, u32[]{:S(2)}) collective-permute-start(bf16[32,4096]{1,0:T(8,128)(2,1)S(1)} %get-tuple-element.7), channel_id=1, source_target_pairs={{0,15},{1,0},{2,1},{3,2},{4,3},{5,4},{6,5},{7,6},{8,7},{9,8},{10,9... | collective-permute-start | bytes 786440 | tf_op jit(solution)/shard_map/ppermute | solution.py:26
  49.7 4.0 %collective-permute-start.4 = (bf16[32,4096]{1,0:T(8,128)(2,1)S(1)}, bf16[32,4096]{1,0:T(8,128)(2,1)S(1)}, u32[]{:S(2)}, u32[]{:S(2)}) collective-permute-start(bf16[32,4096]{1,0:T(8,128)(2,1)S(1)} %get-tuple-element.7), channel_id=1, source_target_pairs={{0,1},{1,2},{2,3},{3,4},{4,5},{5,6},{6,7},{7,8},{8,9},{9,10},{10,1... | collective-permute-start | bytes 786440 | tf_op jit(solution)/shard_map/ppermute | solution.py:26
  53.7 0.0 collective-permute-done.3
  53.7 2.5 %collective-permute-start.8 = (bf16[32,4096]{1,0:T(8,128)(2,1)S(1)}, bf16[32,4096]{1,0:T(8,128)(2,1)S(1)}, u32[]{:S(2)}, u32[]{:S(2)}) collective-permute-start(bf16[32,4096]{1,0:T(8,128)(2,1)S(1)} %collective-permute-done.3), channel_id=1, source_target_pairs={{0,16},{16,32},{32,48},{48,0},{64,112},{80,64},{96,80},{112,96},{1... | collective-permute-start | bytes 786440 | tf_op jit(solution)/shard_map/ppermute | solution.py:35
  56.2 0.0 collective-permute-done.10
  56.2 2.2 %collective-permute-start.15 = (bf16[32,4096]{1,0:T(8,128)(2,1)S(1)}, bf16[32,4096]{1,0:T(8,128)(2,1)S(1)}, u32[]{:S(2)}, u32[]{:S(2)}) collective-permute-start(bf16[32,4096]{1,0:T(8,128)(2,1)S(1)} %collective-permute-done.10), channel_id=1, source_target_pairs={{0,16},{16,32},{32,48},{48,0},{64,112},{80,64},{96,80},{112,96},{1... | collective-permute-start | bytes 786440 | tf_op jit(solution)/shard_map/ppermute | solution.py:35
  58.4 0.0 collective-permute-done.5
  58.4 2.5 %collective-permute-start.11 = (bf16[32,4096]{1,0:T(8,128)(2,1)S(1)}, bf16[32,4096]{1,0:T(8,128)(2,1)S(1)}, u32[]{:S(2)}, u32[]{:S(2)}) collective-permute-start(bf16[32,4096]{1,0:T(8,128)(2,1)S(1)} %collective-permute-done.5), channel_id=1, source_target_pairs={{0,16},{16,32},{32,48},{48,0},{64,112},{80,64},{96,80},{112,96},{1... | collective-permute-start | bytes 786440 | tf_op jit(solution)/shard_map/ppermute | solution.py:35
  60.9 0.2 collective-permute-done.4
  61.1 3.9 %collective-permute-start.9 = (bf16[32,4096]{1,0:T(8,128)(2,1)S(1)}, bf16[32,4096]{1,0:T(8,128)(2,1)S(1)}, u32[]{:S(2)}, u32[]{:S(2)}) collective-permute-start(bf16[32,4096]{1,0:T(8,128)(2,1)S(1)} %collective-permute-done.4), channel_id=1, source_target_pairs={{0,16},{16,32},{32,48},{48,0},{64,112},{80,64},{96,80},{112,96},{1... | collective-permute-start | bytes 786440 | tf_op jit(solution)/shard_map/ppermute | solution.py:35
  65.1 0.0 collective-permute-done.8
  65.1 2.5 %collective-permute-start.13 = (bf16[32,4096]{1,0:T(8,128)(2,1)S(1)}, bf16[32,4096]{1,0:T(8,128)(2,1)S(1)}, u32[]{:S(2)}, u32[]{:S(2)}) collective-permute-start(bf16[32,4096]{1,0:T(8,128)(2,1)S(1)} %collective-permute-done.8), channel_id=1, source_target_pairs={{0,16},{16,32},{32,48},{48,0},{64,112},{80,64},{96,80},{112,96},{1... | collective-permute-start | bytes 786440 | tf_op jit(solution)/shard_map/ppermute | solution.py:35
  67.6 0.0 collective-permute-done.15
  67.6 2.2 %collective-permute-start.20 = (bf16[32,4096]{1,0:T(8,128)(2,1)S(1)}, bf16[32,4096]{1,0:T(8,128)(2,1)S(1)}, u32[]{:S(2)}, u32[]{:S(2)}) collective-permute-start(bf16[32,4096]{1,0:T(8,128)(2,1)S(1)} %collective-permute-done.15), channel_id=1, source_target_pairs={{0,16},{16,32},{32,48},{48,0},{64,112},{80,64},{96,80},{112,96},{1... | collective-permute-start | bytes 786440 | tf_op jit(solution)/shard_map/ppermute | solution.py:35
  69.8 0.0 collective-permute-done.11
  69.8 2.7 %collective-permute-start.16 = (bf16[32,4096]{1,0:T(8,128)(2,1)S(1)}, bf16[32,4096]{1,0:T(8,128)(2,1)S(1)}, u32[]{:S(2)}, u32[]{:S(2)}) collective-permute-start(bf16[32,4096]{1,0:T(8,128)(2,1)S(1)} %collective-permute-done.11), channel_id=1, source_target_pairs={{0,16},{16,32},{32,48},{48,0},{64,112},{80,64},{96,80},{112,96},{1... | collective-permute-start | bytes 786440 | tf_op jit(solution)/shard_map/ppermute | solution.py:35
  72.4 0.0 collective-permute-done.9
  72.5 3.9 %collective-permute-start.14 = (bf16[32,4096]{1,0:T(8,128)(2,1)S(1)}, bf16[32,4096]{1,0:T(8,128)(2,1)S(1)}, u32[]{:S(2)}, u32[]{:S(2)}) collective-permute-start(bf16[32,4096]{1,0:T(8,128)(2,1)S(1)} %collective-permute-done.9), channel_id=1, source_target_pairs={{0,16},{16,32},{32,48},{48,0},{64,112},{80,64},{96,80},{112,96},{1... | collective-permute-start | bytes 786440 | tf_op jit(solution)/shard_map/ppermute | solution.py:35
  76.5 0.0 collective-permute-done.13
  76.5 2.5 %collective-permute-start.18 = (bf16[32,4096]{1,0:T(8,128)(2,1)S(1)}, bf16[32,4096]{1,0:T(8,128)(2,1)S(1)}, u32[]{:S(2)}, u32[]{:S(2)}) collective-permute-start(bf16[32,4096]{1,0:T(8,128)(2,1)S(1)} %collective-permute-done.13), channel_id=1, source_target_pairs={{0,16},{16,32},{32,48},{48,0},{64,112},{80,64},{96,80},{112,96},{1... | collective-permute-start | bytes 786440 | tf_op jit(solution)/shard_map/ppermute | solution.py:35
  79.0 0.0 collective-permute-done.16
  79.0 2.7 %collective-permute-start.21 = (bf16[32,4096]{1,0:T(8,128)(2,1)S(1)}, bf16[32,4096]{1,0:T(8,128)(2,1)S(1)}, u32[]{:S(2)}, u32[]{:S(2)}) collective-permute-start(bf16[32,4096]{1,0:T(8,128)(2,1)S(1)} %collective-permute-done.16), channel_id=1, source_target_pairs={{0,16},{16,32},{32,48},{48,0},{64,112},{80,64},{96,80},{112,96},{1... | collective-permute-start | bytes 786440 | tf_op jit(solution)/shard_map/ppermute | solution.py:35
  81.7 0.0 collective-permute-done.14
  81.7 2.9 %collective-permute-start.19 = (bf16[32,4096]{1,0:T(8,128)(2,1)S(1)}, bf16[32,4096]{1,0:T(8,128)(2,1)S(1)}, u32[]{:S(2)}, u32[]{:S(2)}) collective-permute-start(bf16[32,4096]{1,0:T(8,128)(2,1)S(1)} %collective-permute-done.14), channel_id=1, source_target_pairs={{0,16},{16,32},{32,48},{48,0},{64,112},{80,64},{96,80},{112,96},{1... | collective-permute-start | bytes 786440 | tf_op jit(solution)/shard_map/ppermute | solution.py:35
  84.8 0.0 collective-permute-done.18
  84.8 4.7 %collective-permute-done.19 = bf16[32,4096]{1,0:T(8,128)(2,1)S(1)} collective-permute-done((bf16[32,4096]{1,0:T(8,128)(2,1)S(1)}, bf16[32,4096]{1,0:T(8,128)(2,1)S(1)}, u32[]{:S(2)}, u32[]{:S(2)}) %collective-permute-start.19) | collective-permute-done | bytes 262176 | tf_op jit(solution)/shard_map/ppermute | solution.py:35
  89.5 0.0 collective-permute-done.20
  89.6 0.0 collective-permute-done.21
  89.7 0.0 collective-permute-done.6
  89.7 2.9 %fusion.1 = f32[128,1024]{1,0:T(8,128)S(1)} fusion(bf16[2048,1024]{1,0:T(8,128)(2,1)} %collective-permute-done.6, bf16[128,4096]{1,0:T(8,128)(2,1)S(1)} %slice_dynamic-update-slice_fusion, s32[]{:T(128)S(6)} %select_n.80), kind=kOutput, calls=%fused_computation.9 | convolution fusion | flops 536870912 | bytes 5242884 | tf_op jit(solution)/shard_map/dot_general | solution.py:99
  92.6 2.9 %convolution_add_fusion = f32[128,1024]{1,0:T(8,128)S(1)} fusion(f32[128,1024]{1,0:T(8,128)S(1)} %fusion.1, bf16[2048,1024]{1,0:T(8,128)(2,1)} %compare_select_fusion, bf16[128,4096]{1,0:T(8,128)(2,1)S(1)} %slice_dynamic-update-slice_fusion, s32[]{:T(128)S(6)} %select_n.75), kind=kOutput, calls=%fused_computation.1 | convolution fusion | flops 537001984 | bytes 5767172 | tf_op jit(solution)/shard_map/dot_general | solution.py:99
  95.5 2.9 %fusion.4 = f32[128,1024]{1,0:T(8,128)S(1)} fusion(bf16[2048,1024]{1,0:T(8,128)(2,1)} %collective-permute-done.6, bf16[128,4096]{1,0:T(8,128)(2,1)S(1)} %slice_dynamic-update-slice_fusion.8, s32[]{:T(128)S(6)} %select_n.80), kind=kOutput, calls=%fused_computation.12 | convolution fusion | flops 536870912 | bytes 5242884 | tf_op jit(solution)/shard_map/dot_general | solution.py:99
  98.5 2.9 %convolution_add_fusion.1 = f32[128,1024]{1,0:T(8,128)S(1)} fusion(f32[128,1024]{1,0:T(8,128)S(1)} %fusion.4, bf16[2048,1024]{1,0:T(8,128)(2,1)} %compare_select_fusion, bf16[128,4096]{1,0:T(8,128)(2,1)S(1)} %slice_dynamic-update-slice_fusion.8, s32[]{:T(128)S(6)} %select_n.75), kind=kOutput, calls=%fused_computation.2 | convolution fusion | flops 537001984 | bytes 5767172 | tf_op jit(solution)/shard_map/dot_general | solution.py:99
  101.4 2.9 %fusion.10 = f32[128,1024]{1,0:T(8,128)S(1)} fusion(bf16[2048,1024]{1,0:T(8,128)(2,1)} %collective-permute-done.6, bf16[128,4096]{1,0:T(8,128)(2,1)S(1)} %slice_dynamic-update-slice_fusion.24, s32[]{:T(128)S(6)} %select_n.80), kind=kOutput, calls=%fused_computation.18 | convolution fusion | flops 536870912 | bytes 5242884 | tf_op jit(solution)/shard_map/dot_general | solution.py:99
  104.3 2.9 %convolution_add_fusion.3 = f32[128,1024]{1,0:T(8,128)S(1)} fusion(f32[128,1024]{1,0:T(8,128)S(1)} %fusion.10, bf16[2048,1024]{1,0:T(8,128)(2,1)} %compare_select_fusion, bf16[128,4096]{1,0:T(8,128)(2,1)S(1)} %slice_dynamic-update-slice_fusion.24, s32[]{:T(128)S(6)} %select_n.75), kind=kOutput, calls=%fused_computation.4 | convolution fusion | flops 537001984 | bytes 5767172 | tf_op jit(solution)/shard_map/dot_general | solution.py:99
  107.3 2.9 %fusion.7 = f32[128,1024]{1,0:T(8,128)S(1)} fusion(bf16[2048,1024]{1,0:T(8,128)(2,1)} %collective-permute-done.6, bf16[128,4096]{1,0:T(8,128)(2,1)S(1)} %slice_dynamic-update-slice_fusion.16, s32[]{:T(128)S(6)} %select_n.80), kind=kOutput, calls=%fused_computation.15 | convolution fusion | flops 536870912 | bytes 5242884 | tf_op jit(solution)/shard_map/dot_general | solution.py:99
  110.2 3.7 %convolution_add_fusion.2 = f32[128,1024]{1,0:T(8,128)} fusion(f32[128,1024]{1,0:T(8,128)S(1)} %fusion.7, bf16[2048,1024]{1,0:T(8,128)(2,1)} %compare_select_fusion, bf16[128,4096]{1,0:T(8,128)(2,1)S(1)} %slice_dynamic-update-slice_fusion.16, s32[]{:T(128)S(6)} %select_n.75), kind=kOutput, calls=%fused_computation.3 | convolution fusion | flops 537001984 | bytes 5767172 | tf_op jit(solution)/shard_map/dot_general | solution.py:99
  113.9 5.8 %collective-permute-start.12 = (f32[128,1024]{1,0:T(8,128)}, f32[128,1024]{1,0:T(8,128)S(1)}, u32[]{:S(2)}, u32[]{:S(2)}) collective-permute-start(f32[128,1024]{1,0:T(8,128)} %convolution_add_fusion.2), channel_id=1, source_target_pairs={{0,384},{16,16},{32,160},{48,304},{64,192},{80,336},{96,480},{112,... | collective-permute-start | bytes 1572872 | tf_op jit(solution)/shard_map/ppermute | solution.py:62
  119.7 0.7 collective-permute-start.7
  120.4 4.4 %collective-permute-start.17 = (f32[128,1024]{1,0:T(8,128)S(1)}, f32[128,1024]{1,0:T(8,128)S(1)}, u32[]{:S(2)}, u32[]{:S(2)}) collective-permute-start(f32[128,1024]{1,0:T(8,128)S(1)} %convolution_add_fusion.1), channel_id=1, source_target_pairs={{0,256},{16,400},{32,32},{48,176},{64,320},{80,464},{96,96},{112,2... | collective-permute-start | bytes 1572872 | tf_op jit(solution)/shard_map/ppermute | solution.py:62
  124.9 4.0 %collective-permute-start.22 = (f32[128,1024]{1,0:T(8,128)S(1)}, f32[128,1024]{1,0:T(8,128)}, u32[]{:S(2)}, u32[]{:S(2)}) collective-permute-start(f32[128,1024]{1,0:T(8,128)S(1)} %convolution_add_fusion), channel_id=1, source_target_pairs={{0,128},{16,272},{32,416},{48,48},{64,448},{80,80},{96,224},{112,3... | collective-permute-start | bytes 1572872 | tf_op jit(solution)/shard_map/ppermute | solution.py:62
  128.9 0.0 collective-permute-done.12
  128.9 0.0 collective-permute-done.7
  128.9 6.8 %collective-permute-done.17 = f32[128,1024]{1,0:T(8,128)S(1)} collective-permute-done((f32[128,1024]{1,0:T(8,128)S(1)}, f32[128,1024]{1,0:T(8,128)S(1)}, u32[]{:S(2)}, u32[]{:S(2)}) %collective-permute-start.17) | collective-permute-done | bytes 524320 | tf_op jit(solution)/shard_map/ppermute | solution.py:62
  135.8 12.5 %collective-permute-done.22 = f32[128,1024]{1,0:T(8,128)} collective-permute-done((f32[128,1024]{1,0:T(8,128)S(1)}, f32[128,1024]{1,0:T(8,128)}, u32[]{:S(2)}, u32[]{:S(2)}) %collective-permute-start.22) | collective-permute-done | bytes 524320 | tf_op jit(solution)/shard_map/ppermute | solution.py:62
  148.2 1.2 add_add_fusion
  149.4 0.9 fusion
  (36 shorter events, 0.4 us)
Async XLA Ops:
  0.0 9.9 %collective-permute-start = (bf16[16,2048]{1,0:T(8,128)(2,1)}, bf16[16,2048]{1,0:T(8,128)(2,1)S(1)}, u32[]{:S(2)}, u32[]{:S(2)}) collective-permute-start(bf16[16,2048]{1,0:T(8,128)(2,1)} %param.5), channel_id=1, source_target_pairs={{0,64},{64,0},{1,65},{65,1},{2,66},{66,2},{3,67},{67,3},{4,68},{68... | collective-permute-start | bytes 196616 | tf_op jit(solution)/shard_map/ppermute | solution.py:70
  10.7 15.1 %collective-permute-start.1 = (bf16[16,4096]{1,0:T(8,128)(2,1)S(1)}, bf16[16,4096]{1,0:T(8,128)(2,1)S(1)}, u32[]{:S(2)}, u32[]{:S(2)}) collective-permute-start(bf16[16,4096]{1,0:T(8,128)(2,1)S(1)} %pad_maximum_fusion.1), channel_id=1, source_target_pairs={{0,0},{1,1},{2,2},{3,3},{4,4},{5,5},{6,6},{7,7},{64,8},{65,9},{66,... | collective-permute-start | bytes 393224 | tf_op jit(solution)/shard_map/ppermute | solution.py:52
  23.4 12.2 %collective-permute-start.2 = (bf16[16,4096]{1,0:T(8,128)(2,1)S(1)}, bf16[16,4096]{1,0:T(8,128)(2,1)S(1)}, u32[]{:S(2)}, u32[]{:S(2)}) collective-permute-start(bf16[16,4096]{1,0:T(8,128)(2,1)S(1)} %pad_maximum_fusion.1), channel_id=1, source_target_pairs={{4,0},{5,1},{6,2},{7,3},{0,4},{1,5},{2,6},{3,7},{68,8},{69,9},{70,... | collective-permute-start | bytes 393224 | tf_op jit(solution)/shard_map/ppermute | solution.py:52
  35.7 18.0 %collective-permute-start.3 = (bf16[32,4096]{1,0:T(8,128)(2,1)S(1)}, bf16[32,4096]{1,0:T(8,128)(2,1)S(1)}, u32[]{:S(2)}, u32[]{:S(2)}) collective-permute-start(bf16[32,4096]{1,0:T(8,128)(2,1)S(1)} %pad_maximum_fusion), channel_id=1, source_target_pairs={{0,2},{1,3},{2,4},{3,5},{4,6},{5,7},{6,8},{7,9},{8,10},{9,11},{10,... | collective-permute-start | bytes 786440 | tf_op jit(solution)/shard_map/ppermute | solution.py:35
  41.7 48.0 %collective-permute-start.6 = (bf16[2048,1024]{1,0:T(8,128)(2,1)}, bf16[2048,1024]{1,0:T(8,128)(2,1)}, u32[]{:S(2)}, u32[]{:S(2)}) collective-permute-start(bf16[2048,1024]{1,0:T(8,128)(2,1)} %compare_select_fusion), channel_id=1, source_target_pairs={{0,64},{64,0},{1,65},{65,1},{2,66},{66,2},{3,67},{67,3},{4,68},{68... | collective-permute-start | bytes 12582920 | tf_op jit(solution)/shard_map/ppermute | solution.py:78
  43.6 12.6 %collective-permute-start.10 = (bf16[32,4096]{1,0:T(8,128)(2,1)S(1)}, bf16[32,4096]{1,0:T(8,128)(2,1)S(1)}, u32[]{:S(2)}, u32[]{:S(2)}) collective-permute-start(bf16[32,4096]{1,0:T(8,128)(2,1)S(1)} %get-tuple-element.7), channel_id=1, source_target_pairs={{0,16},{16,32},{32,48},{48,0},{64,112},{80,64},{96,80},{112,96},{1... | collective-permute-start | bytes 786440 | tf_op jit(solution)/shard_map/ppermute | solution.py:35
  47.7 10.6 %collective-permute-start.5 = (bf16[32,4096]{1,0:T(8,128)(2,1)S(1)}, bf16[32,4096]{1,0:T(8,128)(2,1)S(1)}, u32[]{:S(2)}, u32[]{:S(2)}) collective-permute-start(bf16[32,4096]{1,0:T(8,128)(2,1)S(1)} %get-tuple-element.7), channel_id=1, source_target_pairs={{0,15},{1,0},{2,1},{3,2},{4,3},{5,4},{6,5},{7,6},{8,7},{9,8},{10,9... | collective-permute-start | bytes 786440 | tf_op jit(solution)/shard_map/ppermute | solution.py:26
  49.7 11.4 %collective-permute-start.4 = (bf16[32,4096]{1,0:T(8,128)(2,1)S(1)}, bf16[32,4096]{1,0:T(8,128)(2,1)S(1)}, u32[]{:S(2)}, u32[]{:S(2)}) collective-permute-start(bf16[32,4096]{1,0:T(8,128)(2,1)S(1)} %get-tuple-element.7), channel_id=1, source_target_pairs={{0,1},{1,2},{2,3},{3,4},{4,5},{5,6},{6,7},{7,8},{8,9},{9,10},{10,1... | collective-permute-start | bytes 786440 | tf_op jit(solution)/shard_map/ppermute | solution.py:26
  53.7 11.4 %collective-permute-start.8 = (bf16[32,4096]{1,0:T(8,128)(2,1)S(1)}, bf16[32,4096]{1,0:T(8,128)(2,1)S(1)}, u32[]{:S(2)}, u32[]{:S(2)}) collective-permute-start(bf16[32,4096]{1,0:T(8,128)(2,1)S(1)} %collective-permute-done.3), channel_id=1, source_target_pairs={{0,16},{16,32},{32,48},{48,0},{64,112},{80,64},{96,80},{112,96},{1... | collective-permute-start | bytes 786440 | tf_op jit(solution)/shard_map/ppermute | solution.py:35
  56.2 11.4 %collective-permute-start.15 = (bf16[32,4096]{1,0:T(8,128)(2,1)S(1)}, bf16[32,4096]{1,0:T(8,128)(2,1)S(1)}, u32[]{:S(2)}, u32[]{:S(2)}) collective-permute-start(bf16[32,4096]{1,0:T(8,128)(2,1)S(1)} %collective-permute-done.10), channel_id=1, source_target_pairs={{0,16},{16,32},{32,48},{48,0},{64,112},{80,64},{96,80},{112,96},{1... | collective-permute-start | bytes 786440 | tf_op jit(solution)/shard_map/ppermute | solution.py:35
  58.4 11.4 %collective-permute-start.11 = (bf16[32,4096]{1,0:T(8,128)(2,1)S(1)}, bf16[32,4096]{1,0:T(8,128)(2,1)S(1)}, u32[]{:S(2)}, u32[]{:S(2)}) collective-permute-start(bf16[32,4096]{1,0:T(8,128)(2,1)S(1)} %collective-permute-done.5), channel_id=1, source_target_pairs={{0,16},{16,32},{32,48},{48,0},{64,112},{80,64},{96,80},{112,96},{1... | collective-permute-start | bytes 786440 | tf_op jit(solution)/shard_map/ppermute | solution.py:35
  61.1 11.4 %collective-permute-start.9 = (bf16[32,4096]{1,0:T(8,128)(2,1)S(1)}, bf16[32,4096]{1,0:T(8,128)(2,1)S(1)}, u32[]{:S(2)}, u32[]{:S(2)}) collective-permute-start(bf16[32,4096]{1,0:T(8,128)(2,1)S(1)} %collective-permute-done.4), channel_id=1, source_target_pairs={{0,16},{16,32},{32,48},{48,0},{64,112},{80,64},{96,80},{112,96},{1... | collective-permute-start | bytes 786440 | tf_op jit(solution)/shard_map/ppermute | solution.py:35
  65.1 11.4 %collective-permute-start.13 = (bf16[32,4096]{1,0:T(8,128)(2,1)S(1)}, bf16[32,4096]{1,0:T(8,128)(2,1)S(1)}, u32[]{:S(2)}, u32[]{:S(2)}) collective-permute-start(bf16[32,4096]{1,0:T(8,128)(2,1)S(1)} %collective-permute-done.8), channel_id=1, source_target_pairs={{0,16},{16,32},{32,48},{48,0},{64,112},{80,64},{96,80},{112,96},{1... | collective-permute-start | bytes 786440 | tf_op jit(solution)/shard_map/ppermute | solution.py:35
  67.6 21.9 %collective-permute-start.20 = (bf16[32,4096]{1,0:T(8,128)(2,1)S(1)}, bf16[32,4096]{1,0:T(8,128)(2,1)S(1)}, u32[]{:S(2)}, u32[]{:S(2)}) collective-permute-start(bf16[32,4096]{1,0:T(8,128)(2,1)S(1)} %collective-permute-done.15), channel_id=1, source_target_pairs={{0,16},{16,32},{32,48},{48,0},{64,112},{80,64},{96,80},{112,96},{1... | collective-permute-start | bytes 786440 | tf_op jit(solution)/shard_map/ppermute | solution.py:35
  69.8 9.2 %collective-permute-start.16 = (bf16[32,4096]{1,0:T(8,128)(2,1)S(1)}, bf16[32,4096]{1,0:T(8,128)(2,1)S(1)}, u32[]{:S(2)}, u32[]{:S(2)}) collective-permute-start(bf16[32,4096]{1,0:T(8,128)(2,1)S(1)} %collective-permute-done.11), channel_id=1, source_target_pairs={{0,16},{16,32},{32,48},{48,0},{64,112},{80,64},{96,80},{112,96},{1... | collective-permute-start | bytes 786440 | tf_op jit(solution)/shard_map/ppermute | solution.py:35
  72.5 9.2 %collective-permute-start.14 = (bf16[32,4096]{1,0:T(8,128)(2,1)S(1)}, bf16[32,4096]{1,0:T(8,128)(2,1)S(1)}, u32[]{:S(2)}, u32[]{:S(2)}) collective-permute-start(bf16[32,4096]{1,0:T(8,128)(2,1)S(1)} %collective-permute-done.9), channel_id=1, source_target_pairs={{0,16},{16,32},{32,48},{48,0},{64,112},{80,64},{96,80},{112,96},{1... | collective-permute-start | bytes 786440 | tf_op jit(solution)/shard_map/ppermute | solution.py:35
  76.5 8.3 %collective-permute-start.18 = (bf16[32,4096]{1,0:T(8,128)(2,1)S(1)}, bf16[32,4096]{1,0:T(8,128)(2,1)S(1)}, u32[]{:S(2)}, u32[]{:S(2)}) collective-permute-start(bf16[32,4096]{1,0:T(8,128)(2,1)S(1)} %collective-permute-done.13), channel_id=1, source_target_pairs={{0,16},{16,32},{32,48},{48,0},{64,112},{80,64},{96,80},{112,96},{1... | collective-permute-start | bytes 786440 | tf_op jit(solution)/shard_map/ppermute | solution.py:35
  79.0 10.6 %collective-permute-start.21 = (bf16[32,4096]{1,0:T(8,128)(2,1)S(1)}, bf16[32,4096]{1,0:T(8,128)(2,1)S(1)}, u32[]{:S(2)}, u32[]{:S(2)}) collective-permute-start(bf16[32,4096]{1,0:T(8,128)(2,1)S(1)} %collective-permute-done.16), channel_id=1, source_target_pairs={{0,16},{16,32},{32,48},{48,0},{64,112},{80,64},{96,80},{112,96},{1... | collective-permute-start | bytes 786440 | tf_op jit(solution)/shard_map/ppermute | solution.py:35
  81.7 7.8 %collective-permute-start.19 = (bf16[32,4096]{1,0:T(8,128)(2,1)S(1)}, bf16[32,4096]{1,0:T(8,128)(2,1)S(1)}, u32[]{:S(2)}, u32[]{:S(2)}) collective-permute-start(bf16[32,4096]{1,0:T(8,128)(2,1)S(1)} %collective-permute-done.14), channel_id=1, source_target_pairs={{0,16},{16,32},{32,48},{48,0},{64,112},{80,64},{96,80},{112,96},{1... | collective-permute-start | bytes 786440 | tf_op jit(solution)/shard_map/ppermute | solution.py:35
  113.9 15.0 %collective-permute-start.12 = (f32[128,1024]{1,0:T(8,128)}, f32[128,1024]{1,0:T(8,128)S(1)}, u32[]{:S(2)}, u32[]{:S(2)}) collective-permute-start(f32[128,1024]{1,0:T(8,128)} %convolution_add_fusion.2), channel_id=1, source_target_pairs={{0,384},{16,16},{32,160},{48,304},{64,192},{80,336},{96,480},{112,... | collective-permute-start | bytes 1572872 | tf_op jit(solution)/shard_map/ppermute | solution.py:62
  119.7 9.2 %collective-permute-start.7 = (f32[128,1024]{1,0:T(8,128)S(1)}, f32[128,1024]{1,0:T(8,128)S(1)}, u32[]{:S(2)}, u32[]{:S(2)}) collective-permute-start(f32[128,1024]{1,0:T(8,128)S(1)} %convolution_add_fusion.3), channel_id=1, source_target_pairs={{0,0},{16,144},{32,288},{48,432},{64,64},{80,208},{96,352},{112,49... | collective-permute-start | bytes 1572872 | tf_op jit(solution)/shard_map/ppermute | solution.py:62
  120.4 15.3 %collective-permute-start.17 = (f32[128,1024]{1,0:T(8,128)S(1)}, f32[128,1024]{1,0:T(8,128)S(1)}, u32[]{:S(2)}, u32[]{:S(2)}) collective-permute-start(f32[128,1024]{1,0:T(8,128)S(1)} %convolution_add_fusion.1), channel_id=1, source_target_pairs={{0,256},{16,400},{32,32},{48,176},{64,320},{80,464},{96,96},{112,2... | collective-permute-start | bytes 1572872 | tf_op jit(solution)/shard_map/ppermute | solution.py:62
  124.9 23.4 %collective-permute-start.22 = (f32[128,1024]{1,0:T(8,128)S(1)}, f32[128,1024]{1,0:T(8,128)}, u32[]{:S(2)}, u32[]{:S(2)}) collective-permute-start(f32[128,1024]{1,0:T(8,128)S(1)} %convolution_add_fusion), channel_id=1, source_target_pairs={{0,128},{16,272},{32,416},{48,48},{64,448},{80,80},{96,224},{112,3... | collective-permute-start | bytes 1572872 | tf_op jit(solution)/shard_map/ppermute | solution.py:62

commit v2 on v1

v2 whole, which is shorter than its diff:
```python
import jax
import jax.numpy as jnp
from jax import lax
from jax.experimental import pallas as pl
from jax.experimental.pallas import tpu as pltpu
from jax.sharding import Mesh, PartitionSpec as P

Y, CORE, X, Z = 4, 2, 4, 16
HALF = Z // CORE
LANES = 128
CHUNKS = 4


def outer_labels_of(contract_irrep, outer_irrep, block_map, depth, cols):
    first = lax.axis_index("y") * (CORE * depth)
    pair = lax.axis_index("x") * Z + lax.axis_index("z")
    row_labels = lax.dynamic_slice_in_dim(contract_irrep, first, CORE * depth, 0)
    col_labels = lax.dynamic_slice_in_dim(outer_irrep, pair * cols, cols, 0)
    levels = jnp.arange(block_map.shape[0], dtype=jnp.int32)
    partner = jnp.sum(block_map * levels[None, :], axis=1)
    row_partner = jnp.sum(
        jnp.where(row_labels[:, None] == levels[None, :], partner[None, :], 0), axis=1
    )
    return row_partner.reshape(-1, LANES), col_labels.reshape(1, -1)


def over_z(value, step):
    return lax.ppermute(value, "z", [(i, (i + step) % Z) for i in range(Z)])


def apart(value, axis, size, step):
    pairs = []
    for core in range(CORE):
        for i in range(size):
            to = (i + (step if core == 0 else -step)) % size
            pairs.append((core * size + i, core * size + to))
    return lax.ppermute(value, ("core", axis), pairs)


def spread(value, offset):
    pairs = []
    for y in range(Y):
        for k in range(CORE):
            for x in range(X):
                for z in range(Z):
                    source = HALF * k + (z + offset) % HALF
                    sender = z // HALF
                    pairs.append(
                        (
                            ((y * CORE + sender) * X + (x + y) % X) * Z + source,
                            ((y * CORE + k) * X + x) * Z + z,
                        )
                    )
    return lax.ppermute(value, ("y", "core", "x", "z"), pairs)


def hand_in(value, t):
    pairs = []
    for y in range(Y):
        for core in range(CORE):
            for x in range(X):
                to = (x + y - t) % Y if core == 0 else (x + y + t) % Y
                pairs.append(((y * CORE + core) * X + x, (to * CORE + core) * X + x))
    return lax.ppermute(value, ("y", "core", "x"), pairs)


def hold_kernel(place_ref, row_ref, col_ref, own_ref, other_ref, held_ref, sem):
    core, (depth, cols) = place_ref[0], own_ref.shape
    chunk = depth // CHUNKS
    copies = []
    for index, ref in ((core, own_ref), (1 - core, other_ref)):
        for part in range(CHUNKS):
            first = pl.multiple_of(index * depth + part * chunk, chunk)
            copy = pltpu.make_async_copy(
                ref.at[pl.ds(part * chunk, chunk)],
                held_ref.at[pl.ds(first, chunk)],
                sem.at[len(copies)],
            )
            copy.start()
            copies.append((copy, first))
    col = col_ref[...].astype(jnp.float32).astype(jnp.bfloat16)
    zero = jnp.zeros((), held_ref.dtype)
    for copy, first in copies:
        copy.wait()
        for group in range(chunk // LANES):
            labels = row_ref[pl.ds(first // LANES + group, 1), :].astype(jnp.float32)
            labels = jnp.broadcast_to(labels, (LANES, LANES)).T.astype(jnp.bfloat16)
            rows = pl.ds(pl.multiple_of(first + group * LANES, LANES), LANES)
            for lane in range(0, cols, LANES):
                at = slice(lane, lane + LANES)
                keep = labels == col[:, at]
                held_ref[rows, at] = jnp.where(keep, held_ref[rows, at], zero)


def hold(place, rows, columns, own, other):
    depth, cols = own.shape
    vmem = pl.BlockSpec(memory_space=pltpu.VMEM)
    return pl.pallas_call(
        hold_kernel,
        out_shape=pltpu.VMEM((CORE * depth, cols), own.dtype),
        in_specs=[pl.BlockSpec(memory_space=pltpu.SMEM), vmem, vmem]
        + [pl.BlockSpec(memory_space=pltpu.HBM)] * 2,
        out_specs=vmem,
        scratch_shapes=[pltpu.SemaphoreType.DMA((CORE * CHUNKS,))],
        compiler_params=pltpu.CompilerParams(vmem_limit_bytes=12 * 2**20),
        cost_estimate=pl.CostEstimate(
            flops=0, bytes_accessed=4 * CORE * depth * cols, transcendentals=0
        ),
    )(place, rows, columns, own, other)


def product_kernel(place_ref, near_ref, far_ref, held_ref, out_ref):
    base, cols = place_ref[1], held_ref.shape[1]
    rows = out_ref.shape[0] // HALF
    block = jnp.concatenate([near_ref[...], far_ref[...]])
    width = min(256, cols)
    for first in range(0, cols, width):
        part = slice(first, first + width)
        value = jnp.dot(block, held_ref[:, part], preferred_element_type=jnp.float32)
        for index, offset in enumerate((0, 4, -1, 3, 1, 5, -2, 2)):
            source = lax.rem(base + offset + HALF, HALF)
            out_ref[pl.ds(pl.multiple_of(source * rows, rows), rows), part] = value[
                index * rows : (index + 1) * rows
            ]


def product(place, near, far, held):
    rows, cols = 2 * near.shape[0], held.shape[1]
    vmem = pl.BlockSpec(memory_space=pltpu.VMEM)
    return pl.pallas_call(
        product_kernel,
        out_shape=jax.ShapeDtypeStruct((rows, cols), jnp.float32),
        in_specs=[pl.BlockSpec(memory_space=pltpu.SMEM)] + [vmem] * 3,
        out_specs=vmem,
        compiler_params=pltpu.CompilerParams(vmem_limit_bytes=12 * 2**20),
        cost_estimate=pl.CostEstimate(
            flops=2 * rows * held.size, bytes_accessed=2 * held.size, transcendentals=0
        ),
    )(place, near, far, pltpu.with_memory_space_constraint(held, pltpu.VMEM))


def body(amplitudes, integrals, contract_irrep, outer_irrep, block_map):
    core, z = lax.axis_index("core"), lax.axis_index("z")
    swap = [(0, 1), (1, 0)]

    other = lax.ppermute(amplitudes, "core", swap)
    other, integrals, contract_irrep, outer_irrep, block_map = lax.optimization_barrier(
        (other, integrals, contract_irrep, outer_irrep, block_map)
    )
    both = jnp.concatenate(
        [jnp.where(core == 0, amplitudes, other), jnp.where(core == 0, other, amplitudes)], axis=1
    )

    first = spread(both, 0)
    second = spread(both, 4)
    other = lax.ppermute(integrals, "core", swap)
    place = jnp.stack([core, z % HALF]).astype(jnp.int32)
    labels = outer_labels_of(contract_irrep, outer_irrep, block_map, *integrals.shape)
    second, labels = lax.optimization_barrier((second, labels))

    here = jnp.concatenate([first, second])
    turned = jnp.concatenate(
        [jnp.where(core == 0, first, second), jnp.where(core == 0, second, first)]
    )
    below = over_z(here, 1)
    above = over_z(here, -1)
    away = apart(turned, "z", Z, 2)

    held = hold(place, *labels, integrals, other)
    near = jnp.concatenate([here, below])
    away, held = lax.optimization_barrier((away, held))
    far = jnp.concatenate([above, away])
    received = []
    for t in range(X):
        near_next, far_next = near, far
        if t < X - 1:
            near_next, far_next = apart(near, "x", X, 1), apart(far, "x", X, 1)
        if t > 1:
            near, received[t - 2] = lax.optimization_barrier((near, received[t - 2]))
        partial = product(place, near, far, held)
        received.append(hand_in(partial, t))
        if t < X - 1:
            near_next, partial = lax.optimization_barrier((near_next, partial))
        near, far = near_next, far_next
    return (received[0] + received[1]) + (received[2] + received[3])


def solution(mesh):
    grid = Mesh(mesh.devices.reshape(Y, CORE, X, Z), ("y", "core", "x", "z"))
    slab, pair = ("y", "core"), ("x", "z")
    in_specs = (P(pair, slab), P(slab, pair), P(), P(), P())
    return jax.shard_map(
        body, mesh=grid, in_specs=in_specs, out_specs=P(slab, pair), check_vma=False
    )
```

time: 153 us -> 123 us (0.80)
  the two profiles are of different devices: /device:TPU:1 before, /device:TPU:10 now
where the time goes in v2:
time: 123 us; the launch traced here: 122 us
  starting transfers between devices  71.2 us (58%)
  waiting for transfers between devices  32.8 us (27%)
  Pallas kernels  11.2 us (9%)
  local copies, waits for them, and re-layouts  3.67 us (3%)
  other arithmetic  2.86 us (2%)
    ppermute x7, starting transfers between devices, apart(): return lax.ppermute(value, ('core', axis), pairs)  25.1 us
    ppermute x4, waiting for transfers between devices, hand_in(): return lax.ppermute(value, ('y', 'core', 'x'), pairs)  19 us
    ppermute x2, starting transfers between devices, over_z(): return lax.ppermute(value, 'z', [(i, (i + step) % Z) for i in range(Z)])  16 us
    ppermute x2, starting transfers between devices, spread(): return lax.ppermute(value, ('y', 'core', 'x', 'z'), pairs)  13.7 us
    ppermute x4, starting transfers between devices, hand_in(): return lax.ppermute(value, ('y', 'core', 'x'), pairs)  12.4 us
    ppermute x2, waiting for transfers between devices, over_z(): return lax.ppermute(value, 'z', [(i, (i + step) % Z) for i in range(Z)])  8.25 us
    pallas_call x4, Pallas kernels, product(): pl.pallas_call(product_kernel, out_shape=jax.ShapeDtypeStruct((rows, cols...  7.43 us
    pallas_call x1, Pallas kernels, hold(): pl.pallas_call(hold_kernel, out_shape=pltpu.VMEM((CORE * depth, cols), ow...  3.72 us
  transfers between devices with their start and end apart: 17, of which 7 were waited for; matrix products, arithmetic and copies ran while one was open for 3% of the time, Pallas kernels for 9%

profile of v2, /device:TPU:10, one launch (start us, length us, event | category | flops | bytes accessed | tf_op | source)
XLA Modules:
  0.0 122.1 jit_solution(4005688234158896651)
XLA Ops:
  0.0 1.9 %collective-permute-start = (bf16[16,2048]{1,0:T(8,128)(2,1)}, bf16[16,2048]{1,0:T(8,128)(2,1)S(1)}, u32[]{:S(2)}, u32[]{:S(2)}) collective-permute-start(bf16[16,2048]{1,0:T(8,128)(2,1)} %param.5), channel_id=1, source_target_pairs={{0,64},{64,0},{1,65},{65,1},{2,66},{66,2},{3,67},{67,3},{4,68},{68... | collective-permute-start | bytes 196616 | tf_op jit(solution)/shard_map/ppermute | solution.py:146
  1.9 1.4 %collective-permute-done = bf16[16,2048]{1,0:T(8,128)(2,1)S(1)} collective-permute-done((bf16[16,2048]{1,0:T(8,128)(2,1)}, bf16[16,2048]{1,0:T(8,128)(2,1)S(1)}, u32[]{:S(2)}, u32[]{:S(2)}) %collective-permute-start) | collective-permute-done | bytes 65568 | tf_op jit(solution)/shard_map/ppermute | solution.py:146
  3.4 2.1 %collective-permute-start.7 = (bf16[2048,1024]{1,0:T(8,128)(2,1)}, bf16[2048,1024]{1,0:T(8,128)(2,1)}, u32[]{:S(2)}, u32[]{:S(2)}) collective-permute-start(bf16[2048,1024]{1,0:T(8,128)(2,1)} %own_ref), channel_id=1, source_target_pairs={{0,64},{64,0},{1,65},{65,1},{2,66},{66,2},{3,67},{67,3},{4,68},{68... | collective-permute-start | bytes 12582920 | tf_op jit(solution)/shard_map/ppermute | solution.py:156
  5.4 0.1 pad_add_fusion.place_ref
  5.5 0.9 broadcast_select_fusion.3
  6.4 9.1 %collective-permute-start.2 = (bf16[16,4096]{1,0:T(8,128)(2,1)S(1)}, bf16[16,4096]{1,0:T(8,128)(2,1)S(1)}, u32[]{:S(2)}, u32[]{:S(2)}) collective-permute-start(bf16[16,4096]{1,0:T(8,128)(2,1)S(1)} %pad_maximum_fusion.1), channel_id=1, source_target_pairs={{4,0},{5,1},{6,2},{7,3},{0,4},{1,5},{2,6},{3,7},{68,8},{69,9},{70,... | collective-permute-start | bytes 393224 | tf_op jit(solution)/shard_map/ppermute | solution.py:54
  15.5 4.7 %collective-permute-start.1 = (bf16[16,4096]{1,0:T(8,128)(2,1)S(1)}, bf16[16,4096]{1,0:T(8,128)(2,1)S(1)}, u32[]{:S(2)}, u32[]{:S(2)}) collective-permute-start(bf16[16,4096]{1,0:T(8,128)(2,1)S(1)} %pad_maximum_fusion.1), channel_id=1, source_target_pairs={{0,0},{1,1},{2,2},{3,3},{4,4},{5,5},{6,6},{7,7},{64,8},{65,9},{66,... | collective-permute-start | bytes 393224 | tf_op jit(solution)/shard_map/ppermute | solution.py:54
  20.1 0.8 multiply_reduce_fusion
  20.9 0.7 dynamic_slice.7
  21.6 0.7 dynamic_slice.6
  22.3 0.1 select_reduce_fusion
  22.5 0.0 collective-permute-done.2
  22.5 1.3 %collective-permute-done.1 = bf16[16,4096]{1,0:T(8,128)(2,1)S(1)} collective-permute-done((bf16[16,4096]{1,0:T(8,128)(2,1)S(1)}, bf16[16,4096]{1,0:T(8,128)(2,1)S(1)}, u32[]{:S(2)}, u32[]{:S(2)}) %collective-permute-start.1) | collective-permute-done | bytes 131104 | tf_op jit(solution)/shard_map/ppermute | solution.py:54
  23.8 14.1 %collective-permute-start.5 = (bf16[32,4096]{1,0:T(8,128)(2,1)S(1)}, bf16[32,4096]{1,0:T(8,128)(2,1)S(1)}, u32[]{:S(2)}, u32[]{:S(2)}) collective-permute-start(bf16[32,4096]{1,0:T(8,128)(2,1)S(1)} %get-tuple-element.42), channel_id=1, source_target_pairs={{0,15},{1,0},{2,1},{3,2},{4,3},{5,4},{6,5},{7,6},{8,7},{9,8},{10,9... | collective-permute-start | bytes 786440 | tf_op jit(solution)/shard_map/ppermute | solution.py:28
  37.9 1.9 %collective-permute-start.3 = (bf16[32,4096]{1,0:T(8,128)(2,1)S(1)}, bf16[32,4096]{1,0:T(8,128)(2,1)S(1)}, u32[]{:S(2)}, u32[]{:S(2)}) collective-permute-start(bf16[32,4096]{1,0:T(8,128)(2,1)S(1)} %get-tuple-element.42), channel_id=1, source_target_pairs={{0,1},{1,2},{2,3},{3,4},{4,5},{5,6},{6,7},{7,8},{8,9},{9,10},{10,1... | collective-permute-start | bytes 786440 | tf_op jit(solution)/shard_map/ppermute | solution.py:28
  39.9 1.9 %collective-permute-start.6 = (bf16[32,4096]{1,0:T(8,128)(2,1)S(1)}, bf16[32,4096]{1,0:T(8,128)(2,1)S(1)}, u32[]{:S(2)}, u32[]{:S(2)}) collective-permute-start(bf16[32,4096]{1,0:T(8,128)(2,1)S(1)} %pad_maximum_fusion), channel_id=1, source_target_pairs={{0,2},{1,3},{2,4},{3,5},{4,6},{5,7},{6,8},{7,9},{8,10},{9,11},{10,... | collective-permute-start | bytes 786440 | tf_op jit(solution)/shard_map/ppermute | solution.py:37
  41.8 8.3 %collective-permute-done.3 = bf16[32,4096]{1,0:T(8,128)(2,1)S(1)} collective-permute-done((bf16[32,4096]{1,0:T(8,128)(2,1)S(1)}, bf16[32,4096]{1,0:T(8,128)(2,1)S(1)}, u32[]{:S(2)}, u32[]{:S(2)}) %collective-permute-start.3) | collective-permute-done | bytes 262176 | tf_op jit(solution)/shard_map/ppermute | solution.py:28
  50.1 3.4 %collective-permute-start.4 = (bf16[64,4096]{1,0:T(8,128)(2,1)S(1)}, bf16[64,4096]{1,0:T(8,128)(2,1)S(1)}, u32[]{:S(2)}, u32[]{:S(2)}) collective-permute-start(bf16[64,4096]{1,0:T(8,128)(2,1)S(1)} %constant_dynamic-update-slice_fusion.2.near_ref), channel_id=1, source_target_pairs={{0,16},{16,32},{32,48},{48,0},{64,112},{80,64},{96,80},{112,96},{1... | collective-permute-start | bytes 1572872 | tf_op jit(solution)/shard_map/ppermute | solution.py:37
  53.5 0.0 collective-permute-done.5
  53.5 0.0 collective-permute-done.7.other_ref
  53.5 0.0 copy-start
  53.6 2.2 %copy-done = bf16[2048,1024]{1,0:T(8,128)(2,1)S(1)} copy-done((bf16[2048,1024]{1,0:T(8,128)(2,1)S(1)}, bf16[2048,1024]{1,0:T(8,128)(2,1)}, u32[]{:S(2)}) %copy-start) | copy-done | bytes 4194328
  55.7 3.7 %shard_map.55.held_ref = bf16[4096,1024]{1,0:T(8,128)(2,1)S(1)} custom-call(s32[2]{0:T(128)S(1)} %pad_add_fusion.place_ref, s32[32,128]{1,0:T(8,128)S(1)} %bitcast.4, s32[1,1024]{1,0:T(1,128)S(1)} %bitcast.5, bf16[2048,1024]{1,0:T(8,128)(2,1)S(1)} %copy-done, bf16[2048,1024]{1,0:T(8,128)(2,1)} %collective-permute-done.7.other_ref), custom_call_target="tpu_custom_call" | custom-call | bytes 16777216 | tf_op jit(solution)/shard_map/pallas_call | solution.py:98
  59.5 0.0 collective-permute-done.6
  59.5 4.8 %collective-permute-start.9 = (bf16[64,4096]{1,0:T(8,128)(2,1)S(1)}, bf16[64,4096]{1,0:T(8,128)(2,1)S(1)}, u32[]{:S(2)}, u32[]{:S(2)}) collective-permute-start(bf16[64,4096]{1,0:T(8,128)(2,1)S(1)} %constant_dynamic-update-slice_fusion.5.far_ref), channel_id=1, source_target_pairs={{0,16},{16,32},{32,48},{48,0},{64,112},{80,64},{96,80},{112,96},{1... | collective-permute-start | bytes 1572872 | tf_op jit(solution)/shard_map/ppermute | solution.py:37
  64.3 1.9 %shard_map.56 = f32[128,1024]{1,0:T(8,128)S(1)} custom-call(s32[2]{0:T(128)S(1)} %pad_add_fusion.place_ref, bf16[64,4096]{1,0:T(8,128)(2,1)S(1)} %constant_dynamic-update-slice_fusion.2.near_ref, bf16[64,4096]{1,0:T(8,128)(2,1)S(1)} %constant_dynamic-update-slice_fusion.5.far_ref, bf16[4096,1024]{1,0:T(8,128)(2,1)S(1)} %shard_map.55.held_ref), custom_call_target="tpu_custom_call" | custom-call | flops 1073741824 | bytes 8388608 | tf_op jit(solution)/shard_map/pallas_call | solution.py:130
  66.2 0.0 collective-permute-done.4.near_ref
  66.2 1.9 %collective-permute-start.8 = (bf16[64,4096]{1,0:T(8,128)(2,1)S(1)}, bf16[64,4096]{1,0:T(8,128)(2,1)S(1)}, u32[]{:S(2)}, u32[]{:S(2)}) collective-permute-start(bf16[64,4096]{1,0:T(8,128)(2,1)S(1)} %collective-permute-done.4.near_ref), channel_id=1, source_target_pairs={{0,16},{16,32},{32,48},{48,0},{64,112},{80,64},{96,80},{112,96},{1... | collective-permute-start | bytes 1572872 | tf_op jit(solution)/shard_map/ppermute | solution.py:37
  68.1 2.9 %collective-permute-done.9.far_ref = bf16[64,4096]{1,0:T(8,128)(2,1)S(1)} collective-permute-done((bf16[64,4096]{1,0:T(8,128)(2,1)S(1)}, bf16[64,4096]{1,0:T(8,128)(2,1)S(1)}, u32[]{:S(2)}, u32[]{:S(2)}) %collective-permute-start.9) | collective-permute-done | bytes 524320 | tf_op jit(solution)/shard_map/ppermute | solution.py:37
  71.0 4.4 %collective-permute-start.12 = (bf16[64,4096]{1,0:T(8,128)(2,1)S(1)}, bf16[64,4096]{1,0:T(8,128)(2,1)S(1)}, u32[]{:S(2)}, u32[]{:S(2)}) collective-permute-start(bf16[64,4096]{1,0:T(8,128)(2,1)S(1)} %collective-permute-done.9.far_ref), channel_id=1, source_target_pairs={{0,16},{16,32},{32,48},{48,0},{64,112},{80,64},{96,80},{112,96},{1... | collective-permute-start | bytes 1572872 | tf_op jit(solution)/shard_map/ppermute | solution.py:37
  75.4 4.0 %collective-permute-start.10 = (f32[128,1024]{1,0:T(8,128)S(1)}, f32[128,1024]{1,0:T(8,128)S(1)}, u32[]{:S(2)}, u32[]{:S(2)}) collective-permute-start(f32[128,1024]{1,0:T(8,128)S(1)} %shard_map.56), channel_id=1, source_target_pairs={{0,0},{16,144},{32,288},{48,432},{64,64},{80,208},{96,352},{112,49... | collective-permute-start | bytes 1572872 | tf_op jit(solution)/shard_map/ppermute | solution.py:64
  79.3 1.9 %shard_map.57 = f32[128,1024]{1,0:T(8,128)S(1)} custom-call(s32[2]{0:T(128)S(1)} %pad_add_fusion.place_ref, bf16[64,4096]{1,0:T(8,128)(2,1)S(1)} %collective-permute-done.4.near_ref, bf16[64,4096]{1,0:T(8,128)(2,1)S(1)} %collective-permute-done.9.far_ref, bf16[4096,1024]{1,0:T(8,128)(2,1)S(1)} %shard_map.55.held_ref), custom_call_target="tpu_custom_call" | custom-call | flops 1073741824 | bytes 8388608 | tf_op jit(solution)/shard_map/pallas_call | solution.py:130
  81.2 0.0 collective-permute-done.8.near_ref
  81.2 3.1 %collective-permute-start.11 = (bf16[64,4096]{1,0:T(8,128)(2,1)S(1)}, bf16[64,4096]{1,0:T(8,128)(2,1)S(1)}, u32[]{:S(2)}, u32[]{:S(2)}) collective-permute-start(bf16[64,4096]{1,0:T(8,128)(2,1)S(1)} %collective-permute-done.8.near_ref), channel_id=1, source_target_pairs={{0,16},{16,32},{32,48},{48,0},{64,112},{80,64},{96,80},{112,96},{1... | collective-permute-start | bytes 1572872 | tf_op jit(solution)/shard_map/ppermute | solution.py:37
  84.3 0.7 collective-permute-start.13
  85.0 0.0 collective-permute-done.12.far_ref
  85.0 5.6 %collective-permute-start.15 = (bf16[64,4096]{1,0:T(8,128)(2,1)S(1)}, bf16[64,4096]{1,0:T(8,128)(2,1)S(1)}, u32[]{:S(2)}, u32[]{:S(2)}) collective-permute-start(bf16[64,4096]{1,0:T(8,128)(2,1)S(1)} %collective-permute-done.12.far_ref), channel_id=1, source_target_pairs={{0,16},{16,32},{32,48},{48,0},{64,112},{80,64},{96,80},{112,96},{1... | collective-permute-start | bytes 1572872 | tf_op jit(solution)/shard_map/ppermute | solution.py:37
  90.6 6.0 %collective-permute-done.10 = f32[128,1024]{1,0:T(8,128)S(1)} collective-permute-done((f32[128,1024]{1,0:T(8,128)S(1)}, f32[128,1024]{1,0:T(8,128)S(1)}, u32[]{:S(2)}, u32[]{:S(2)}) %collective-permute-start.10) | collective-permute-done | bytes 524320 | tf_op jit(solution)/shard_map/ppermute | solution.py:64
  96.6 1.9 %shard_map.58 = f32[128,1024]{1,0:T(8,128)S(1)} custom-call(s32[2]{0:T(128)S(1)} %pad_add_fusion.place_ref, bf16[64,4096]{1,0:T(8,128)(2,1)S(1)} %collective-permute-done.8.near_ref, bf16[64,4096]{1,0:T(8,128)(2,1)S(1)} %collective-permute-done.12.far_ref, bf16[4096,1024]{1,0:T(8,128)(2,1)S(1)} %shard_map.55.held_ref), custom_call_target="tpu_custom_call" | custom-call | flops 1073741824 | bytes 8388608 | tf_op jit(solution)/shard_map/pallas_call | solution.py:130
  98.4 1.9 %collective-permute-start.14 = (f32[128,1024]{1,0:T(8,128)S(1)}, f32[128,1024]{1,0:T(8,128)S(1)}, u32[]{:S(2)}, u32[]{:S(2)}) collective-permute-start(f32[128,1024]{1,0:T(8,128)S(1)} %shard_map.58), channel_id=1, source_target_pairs={{0,256},{16,400},{32,32},{48,176},{64,320},{80,464},{96,96},{112,2... | collective-permute-start | bytes 1572872 | tf_op jit(solution)/shard_map/ppermute | solution.py:64
  100.3 0.0 collective-permute-done.11.near_ref
  100.4 0.0 collective-permute-done.13
  100.4 0.0 collective-permute-done.15.far_ref
  100.4 1.9 %shard_map.59 = f32[128,1024]{1,0:T(8,128)S(1)} custom-call(s32[2]{0:T(128)S(1)} %pad_add_fusion.place_ref, bf16[64,4096]{1,0:T(8,128)(2,1)S(1)} %collective-permute-done.11.near_ref, bf16[64,4096]{1,0:T(8,128)(2,1)S(1)} %collective-permute-done.15.far_ref, bf16[4096,1024]{1,0:T(8,128)(2,1)S(1)} %shard_map.55.held_ref), custom_call_target="tpu_custom_call" | custom-call | flops 1073741824 | bytes 8388608 | tf_op jit(solution)/shard_map/pallas_call | solution.py:130
  102.3 5.8 %collective-permute-start.16 = (f32[128,1024]{1,0:T(8,128)S(1)}, f32[128,1024]{1,0:T(8,128)S(1)}, u32[]{:S(2)}, u32[]{:S(2)}) collective-permute-start(f32[128,1024]{1,0:T(8,128)S(1)} %shard_map.59), channel_id=1, source_target_pairs={{0,128},{16,272},{32,416},{48,48},{64,448},{80,80},{96,224},{112,3... | collective-permute-start | bytes 1572872 | tf_op jit(solution)/shard_map/ppermute | solution.py:64
  108.1 6.2 %collective-permute-done.14 = f32[128,1024]{1,0:T(8,128)S(1)} collective-permute-done((f32[128,1024]{1,0:T(8,128)S(1)}, f32[128,1024]{1,0:T(8,128)S(1)}, u32[]{:S(2)}, u32[]{:S(2)}) %collective-permute-start.14) | collective-permute-done | bytes 524320 | tf_op jit(solution)/shard_map/ppermute | solution.py:64
  114.4 6.8 %collective-permute-done.16 = f32[128,1024]{1,0:T(8,128)S(1)} collective-permute-done((f32[128,1024]{1,0:T(8,128)S(1)}, f32[128,1024]{1,0:T(8,128)S(1)}, u32[]{:S(2)}, u32[]{:S(2)}) %collective-permute-start.16) | collective-permute-done | bytes 524320 | tf_op jit(solution)/shard_map/ppermute | solution.py:64
  121.1 0.9 add_add_fusion
  (7 shorter events, 0.2 us)
Async XLA Ops:
  0.0 3.3 %collective-permute-start = (bf16[16,2048]{1,0:T(8,128)(2,1)}, bf16[16,2048]{1,0:T(8,128)(2,1)S(1)}, u32[]{:S(2)}, u32[]{:S(2)}) collective-permute-start(bf16[16,2048]{1,0:T(8,128)(2,1)} %param.5), channel_id=1, source_target_pairs={{0,64},{64,0},{1,65},{65,1},{2,66},{66,2},{3,67},{67,3},{4,68},{68... | collective-permute-start | bytes 196616 | tf_op jit(solution)/shard_map/ppermute | solution.py:146
  3.4 50.2 %collective-permute-start.7 = (bf16[2048,1024]{1,0:T(8,128)(2,1)}, bf16[2048,1024]{1,0:T(8,128)(2,1)}, u32[]{:S(2)}, u32[]{:S(2)}) collective-permute-start(bf16[2048,1024]{1,0:T(8,128)(2,1)} %own_ref), channel_id=1, source_target_pairs={{0,64},{64,0},{1,65},{65,1},{2,66},{66,2},{3,67},{67,3},{4,68},{68... | collective-permute-start | bytes 12582920 | tf_op jit(solution)/shard_map/ppermute | solution.py:156
  6.4 16.1 %collective-permute-start.2 = (bf16[16,4096]{1,0:T(8,128)(2,1)S(1)}, bf16[16,4096]{1,0:T(8,128)(2,1)S(1)}, u32[]{:S(2)}, u32[]{:S(2)}) collective-permute-start(bf16[16,4096]{1,0:T(8,128)(2,1)S(1)} %pad_maximum_fusion.1), channel_id=1, source_target_pairs={{4,0},{5,1},{6,2},{7,3},{0,4},{1,5},{2,6},{3,7},{68,8},{69,9},{70,... | collective-permute-start | bytes 393224 | tf_op jit(solution)/shard_map/ppermute | solution.py:54
  15.5 8.3 %collective-permute-start.1 = (bf16[16,4096]{1,0:T(8,128)(2,1)S(1)}, bf16[16,4096]{1,0:T(8,128)(2,1)S(1)}, u32[]{:S(2)}, u32[]{:S(2)}) collective-permute-start(bf16[16,4096]{1,0:T(8,128)(2,1)S(1)} %pad_maximum_fusion.1), channel_id=1, source_target_pairs={{0,0},{1,1},{2,2},{3,3},{4,4},{5,5},{6,6},{7,7},{64,8},{65,9},{66,... | collective-permute-start | bytes 393224 | tf_op jit(solution)/shard_map/ppermute | solution.py:54
  23.8 29.7 %collective-permute-start.5 = (bf16[32,4096]{1,0:T(8,128)(2,1)S(1)}, bf16[32,4096]{1,0:T(8,128)(2,1)S(1)}, u32[]{:S(2)}, u32[]{:S(2)}) collective-permute-start(bf16[32,4096]{1,0:T(8,128)(2,1)S(1)} %get-tuple-element.42), channel_id=1, source_target_pairs={{0,15},{1,0},{2,1},{3,2},{4,3},{5,4},{6,5},{7,6},{8,7},{9,8},{10,9... | collective-permute-start | bytes 786440 | tf_op jit(solution)/shard_map/ppermute | solution.py:28
  37.9 12.1 %collective-permute-start.3 = (bf16[32,4096]{1,0:T(8,128)(2,1)S(1)}, bf16[32,4096]{1,0:T(8,128)(2,1)S(1)}, u32[]{:S(2)}, u32[]{:S(2)}) collective-permute-start(bf16[32,4096]{1,0:T(8,128)(2,1)S(1)} %get-tuple-element.42), channel_id=1, source_target_pairs={{0,1},{1,2},{2,3},{3,4},{4,5},{5,6},{6,7},{7,8},{8,9},{9,10},{10,1... | collective-permute-start | bytes 786440 | tf_op jit(solution)/shard_map/ppermute | solution.py:28
  39.9 19.6 %collective-permute-start.6 = (bf16[32,4096]{1,0:T(8,128)(2,1)S(1)}, bf16[32,4096]{1,0:T(8,128)(2,1)S(1)}, u32[]{:S(2)}, u32[]{:S(2)}) collective-permute-start(bf16[32,4096]{1,0:T(8,128)(2,1)S(1)} %pad_maximum_fusion), channel_id=1, source_target_pairs={{0,2},{1,3},{2,4},{3,5},{4,6},{5,7},{6,8},{7,9},{8,10},{9,11},{10,... | collective-permute-start | bytes 786440 | tf_op jit(solution)/shard_map/ppermute | solution.py:37
  50.1 16.1 %collective-permute-start.4 = (bf16[64,4096]{1,0:T(8,128)(2,1)S(1)}, bf16[64,4096]{1,0:T(8,128)(2,1)S(1)}, u32[]{:S(2)}, u32[]{:S(2)}) collective-permute-start(bf16[64,4096]{1,0:T(8,128)(2,1)S(1)} %constant_dynamic-update-slice_fusion.2.near_ref), channel_id=1, source_target_pairs={{0,16},{16,32},{32,48},{48,0},{64,112},{80,64},{96,80},{112,96},{1... | collective-permute-start | bytes 1572872 | tf_op jit(solution)/shard_map/ppermute | solution.py:37
  53.5 2.2 %copy-start = (bf16[2048,1024]{1,0:T(8,128)(2,1)S(1)}, bf16[2048,1024]{1,0:T(8,128)(2,1)}, u32[]{:S(2)}) copy-start(bf16[2048,1024]{1,0:T(8,128)(2,1)} %own_ref) | copy-start | bytes 12582916
  59.5 11.5 %collective-permute-start.9 = (bf16[64,4096]{1,0:T(8,128)(2,1)S(1)}, bf16[64,4096]{1,0:T(8,128)(2,1)S(1)}, u32[]{:S(2)}, u32[]{:S(2)}) collective-permute-start(bf16[64,4096]{1,0:T(8,128)(2,1)S(1)} %constant_dynamic-update-slice_fusion.5.far_ref), channel_id=1, source_target_pairs={{0,16},{16,32},{32,48},{48,0},{64,112},{80,64},{96,80},{112,96},{1... | collective-permute-start | bytes 1572872 | tf_op jit(solution)/shard_map/ppermute | solution.py:37
  66.2 15.0 %collective-permute-start.8 = (bf16[64,4096]{1,0:T(8,128)(2,1)S(1)}, bf16[64,4096]{1,0:T(8,128)(2,1)S(1)}, u32[]{:S(2)}, u32[]{:S(2)}) collective-permute-start(bf16[64,4096]{1,0:T(8,128)(2,1)S(1)} %collective-permute-done.4.near_ref), channel_id=1, source_target_pairs={{0,16},{16,32},{32,48},{48,0},{64,112},{80,64},{96,80},{112,96},{1... | collective-permute-start | bytes 1572872 | tf_op jit(solution)/shard_map/ppermute | solution.py:37
  71.0 14.0 %collective-permute-start.12 = (bf16[64,4096]{1,0:T(8,128)(2,1)S(1)}, bf16[64,4096]{1,0:T(8,128)(2,1)S(1)}, u32[]{:S(2)}, u32[]{:S(2)}) collective-permute-start(bf16[64,4096]{1,0:T(8,128)(2,1)S(1)} %collective-permute-done.9.far_ref), channel_id=1, source_target_pairs={{0,16},{16,32},{32,48},{48,0},{64,112},{80,64},{96,80},{112,96},{1... | collective-permute-start | bytes 1572872 | tf_op jit(solution)/shard_map/ppermute | solution.py:37
  75.4 21.2 %collective-permute-start.10 = (f32[128,1024]{1,0:T(8,128)S(1)}, f32[128,1024]{1,0:T(8,128)S(1)}, u32[]{:S(2)}, u32[]{:S(2)}) collective-permute-start(f32[128,1024]{1,0:T(8,128)S(1)} %shard_map.56), channel_id=1, source_target_pairs={{0,0},{16,144},{32,288},{48,432},{64,64},{80,208},{96,352},{112,49... | collective-permute-start | bytes 1572872 | tf_op jit(solution)/shard_map/ppermute | solution.py:64
  81.2 19.1 %collective-permute-start.11 = (bf16[64,4096]{1,0:T(8,128)(2,1)S(1)}, bf16[64,4096]{1,0:T(8,128)(2,1)S(1)}, u32[]{:S(2)}, u32[]{:S(2)}) collective-permute-start(bf16[64,4096]{1,0:T(8,128)(2,1)S(1)} %collective-permute-done.8.near_ref), channel_id=1, source_target_pairs={{0,16},{16,32},{32,48},{48,0},{64,112},{80,64},{96,80},{112,96},{1... | collective-permute-start | bytes 1572872 | tf_op jit(solution)/shard_map/ppermute | solution.py:37
  84.3 16.1 %collective-permute-start.13 = (f32[128,1024]{1,0:T(8,128)S(1)}, f32[128,1024]{1,0:T(8,128)S(1)}, u32[]{:S(2)}, u32[]{:S(2)}) collective-permute-start(f32[128,1024]{1,0:T(8,128)S(1)} %shard_map.57), channel_id=1, source_target_pairs={{0,384},{16,16},{32,160},{48,304},{64,192},{80,336},{96,480},{112,... | collective-permute-start | bytes 1572872 | tf_op jit(solution)/shard_map/ppermute | solution.py:64
  85.0 15.4 %collective-permute-start.15 = (bf16[64,4096]{1,0:T(8,128)(2,1)S(1)}, bf16[64,4096]{1,0:T(8,128)(2,1)S(1)}, u32[]{:S(2)}, u32[]{:S(2)}) collective-permute-start(bf16[64,4096]{1,0:T(8,128)(2,1)S(1)} %collective-permute-done.12.far_ref), channel_id=1, source_target_pairs={{0,16},{16,32},{32,48},{48,0},{64,112},{80,64},{96,80},{112,96},{1... | collective-permute-start | bytes 1572872 | tf_op jit(solution)/shard_map/ppermute | solution.py:37
  98.4 15.9 %collective-permute-start.14 = (f32[128,1024]{1,0:T(8,128)S(1)}, f32[128,1024]{1,0:T(8,128)S(1)}, u32[]{:S(2)}, u32[]{:S(2)}) collective-permute-start(f32[128,1024]{1,0:T(8,128)S(1)} %shard_map.58), channel_id=1, source_target_pairs={{0,256},{16,400},{32,32},{48,176},{64,320},{80,464},{96,96},{112,2... | collective-permute-start | bytes 1572872 | tf_op jit(solution)/shard_map/ppermute | solution.py:64
  102.3 18.9 %collective-permute-start.16 = (f32[128,1024]{1,0:T(8,128)S(1)}, f32[128,1024]{1,0:T(8,128)S(1)}, u32[]{:S(2)}, u32[]{:S(2)}) collective-permute-start(f32[128,1024]{1,0:T(8,128)S(1)} %shard_map.59), channel_id=1, source_target_pairs={{0,128},{16,272},{32,416},{48,48},{64,448},{80,80},{96,224},{112,3... | collective-permute-start | bytes 1572872 | tf_op jit(solution)/shard_map/ppermute | solution.py:64

commit v3 on v2

--- a/solution.py
+++ b/solution.py
@@ -7,25 +7,22 @@
 
 Y, CORE, X, Z = 4, 2, 4, 16
 HALF = Z // CORE
-LANES = 128
+TURN = ((0, 1, 3, 2), (2, 3, 1, 0))
+UNIT = 64
 CHUNKS = 4
 
 
 def outer_labels_of(contract_irrep, outer_irrep, block_map, depth, cols):
     first = lax.axis_index("y") * (CORE * depth)
     pair = lax.axis_index("x") * Z + lax.axis_index("z")
-    row_labels = lax.dynamic_slice_in_dim(contract_irrep, first, CORE * depth, 0)
+    row_labels = lax.dynamic_slice_in_dim(contract_irrep, first, CORE * depth, 0)[::UNIT]
     col_labels = lax.dynamic_slice_in_dim(outer_irrep, pair * cols, cols, 0)
     levels = jnp.arange(block_map.shape[0], dtype=jnp.int32)
     partner = jnp.sum(block_map * levels[None, :], axis=1)
     row_partner = jnp.sum(
         jnp.where(row_labels[:, None] == levels[None, :], partner[None, :], 0), axis=1
     )
-    return row_partner.reshape(-1, LANES), col_labels.reshape(1, -1)
-
-
-def over_z(value, step):
-    return lax.ppermute(value, "z", [(i, (i + step) % Z) for i in range(Z)])
+    return row_partner, col_labels.reshape(1, -1)
 
 
 def apart(value, axis, size, step):
@@ -35,6 +32,10 @@
             to = (i + (step if core == 0 else -step)) % size
             pairs.append((core * size + i, core * size + to))
     return lax.ppermute(value, ("core", axis), pairs)
+
+
+def row_block(y, core, x):
+    return (y + TURN[core][x]) % Y
 
 
 def spread(value, offset):
@@ -47,19 +48,19 @@
                     sender = z // HALF
                     pairs.append(
                         (
-                            ((y * CORE + sender) * X + (x + y) % X) * Z + source,
+                            ((y * CORE + sender) * X + row_block(y, k, x)) * Z + source,
                             ((y * CORE + k) * X + x) * Z + z,
                         )
                     )
     return lax.ppermute(value, ("y", "core", "x", "z"), pairs)
 
 
-def hand_in(value, t):
+def hand_in(value, step):
     pairs = []
     for y in range(Y):
         for core in range(CORE):
             for x in range(X):
-                to = (x + y - t) % Y if core == 0 else (x + y + t) % Y
+                to = row_block(y, core, (x - step if core == 0 else x + step) % X)
                 pairs.append(((y * CORE + core) * X + x, (to * CORE + core) * X + x))
     return lax.ppermute(value, ("y", "core", "x"), pairs)
 
@@ -78,27 +79,27 @@
             )
             copy.start()
             copies.append((copy, first))
-    col = col_ref[...].astype(jnp.float32).astype(jnp.bfloat16)
+    tile = 16
+    col = jnp.broadcast_to(col_ref[...].astype(jnp.float32), (tile, cols)).astype(jnp.bfloat16)
     zero = jnp.zeros((), held_ref.dtype)
     for copy, first in copies:
         copy.wait()
-        for group in range(chunk // LANES):
-            labels = row_ref[pl.ds(first // LANES + group, 1), :].astype(jnp.float32)
-            labels = jnp.broadcast_to(labels, (LANES, LANES)).T.astype(jnp.bfloat16)
-            rows = pl.ds(pl.multiple_of(first + group * LANES, LANES), LANES)
-            for lane in range(0, cols, LANES):
-                at = slice(lane, lane + LANES)
-                keep = labels == col[:, at]
-                held_ref[rows, at] = jnp.where(keep, held_ref[rows, at], zero)
+        for unit in range(chunk // UNIT):
+            label = row_ref[first // UNIT + unit].astype(jnp.float32)
+            keep = col == jnp.full((tile, cols), label, jnp.float32).astype(jnp.bfloat16)
+            for part in range(UNIT // tile):
+                rows = pl.ds(pl.multiple_of(first + unit * UNIT + part * tile, tile), tile)
+                held_ref[rows, :] = jnp.where(keep, held_ref[rows, :], zero)
 
 
 def hold(place, rows, columns, own, other):
     depth, cols = own.shape
-    vmem = pl.BlockSpec(memory_space=pltpu.VMEM)
+    vmem, smem = (pl.BlockSpec(memory_space=m) for m in (pltpu.VMEM, pltpu.SMEM))
+    own, other = (pltpu.with_memory_space_constraint(v, pltpu.HBM) for v in (own, other))
     return pl.pallas_call(
         hold_kernel,
         out_shape=pltpu.VMEM((CORE * depth, cols), own.dtype),
-        in_specs=[pl.BlockSpec(memory_space=pltpu.SMEM), vmem, vmem]
+        in_specs=[smem, smem, vmem]
         + [pl.BlockSpec(memory_space=pltpu.HBM)] * 2,
         out_specs=vmem,
         scratch_shapes=[pltpu.SemaphoreType.DMA((CORE * CHUNKS,))],
@@ -110,16 +111,18 @@
 
 
 def product_kernel(place_ref, near_ref, far_ref, held_ref, out_ref):
-    base, cols = place_ref[1], held_ref.shape[1]
+    core, base, cols = place_ref[0], place_ref[1], held_ref.shape[1]
     rows = out_ref.shape[0] // HALF
+    step = 2 * core - 1
+    sources = [base + k * step + half for k in (-1, 2, 0, 1) for half in (0, 4)]
     block = jnp.concatenate([near_ref[...], far_ref[...]])
     width = min(256, cols)
     for first in range(0, cols, width):
         part = slice(first, first + width)
         value = jnp.dot(block, held_ref[:, part], preferred_element_type=jnp.float32)
-        for index, offset in enumerate((0, 4, -1, 3, 1, 5, -2, 2)):
-            source = lax.rem(base + offset + HALF, HALF)
-            out_ref[pl.ds(pl.multiple_of(source * rows, rows), rows), part] = value[
+        for index, source in enumerate(sources):
+            at = lax.rem(source + HALF, HALF) * rows
+            out_ref[pl.ds(pl.multiple_of(at, rows), rows), part] = value[
                 index * rows : (index + 1) * rows
             ]
 
@@ -159,29 +162,25 @@
     second, labels = lax.optimization_barrier((second, labels))
 
     here = jnp.concatenate([first, second])
-    turned = jnp.concatenate(
-        [jnp.where(core == 0, first, second), jnp.where(core == 0, second, first)]
-    )
-    below = over_z(here, 1)
-    above = over_z(here, -1)
-    away = apart(turned, "z", Z, 2)
+    away = apart(here, "z", Z, 2)
+    back = apart(here, "z", Z, 1)
+    ahead = apart(here, "z", Z, -1)
+    near = jnp.concatenate([ahead, away])
+    far = jnp.concatenate([here, back])
 
+    near_back, near_ahead = apart(near, "x", X, 1), apart(near, "x", X, -1)
+    far_back, far_ahead = apart(far, "x", X, 1), apart(far, "x", X, -1)
+    near_away = apart(near_back, "x", X, 1)
+    far, integrals = lax.optimization_barrier((far, integrals))
     held = hold(place, *labels, integrals, other)
-    near = jnp.concatenate([here, below])
-    away, held = lax.optimization_barrier((away, held))
-    far = jnp.concatenate([above, away])
-    received = []
-    for t in range(X):
-        near_next, far_next = near, far
-        if t < X - 1:
-            near_next, far_next = apart(near, "x", X, 1), apart(far, "x", X, 1)
-        if t > 1:
-            near, received[t - 2] = lax.optimization_barrier((near, received[t - 2]))
-        partial = product(place, near, far, held)
-        received.append(hand_in(partial, t))
-        if t < X - 1:
-            near_next, partial = lax.optimization_barrier((near_next, partial))
-        near, far = near_next, far_next
+    own = product(place, near, far, held)
+    received = [hand_in(own, 0)]
+    far_back, own = lax.optimization_barrier((far_back, own))
+    far_away = apart(far_back, "x", X, 1)
+    received.append(hand_in(product(place, near_back, far_back, held), 1))
+    received.append(hand_in(product(place, near_ahead, far_ahead, held), -1))
+    far_away, received[0] = lax.optimization_barrier((far_away, received[0]))
+    received.append(hand_in(product(place, near_away, far_away, held), 2))
     return (received[0] + received[1]) + (received[2] + received[3])
 
 

time: 123 us -> 111 us (0.902)
  the two profiles are of different devices: /device:TPU:10 before, /device:TPU:1 now
where the time goes in v3:
time: 111 us; the launch traced here: 110 us
  starting transfers between devices  62.2 us (56%)
  waiting for transfers between devices  31.2 us (28%)
  Pallas kernels  11.8 us (11%)
  other arithmetic  2.77 us (2%)
  local copies, waits for them, and re-layouts  1.66 us (1%)
    ppermute x9, starting transfers between devices, apart(): return lax.ppermute(value, ('core', axis), pairs)  26.4 us
    ppermute x4, waiting for transfers between devices, hand_in(): return lax.ppermute(value, ('y', 'core', 'x'), pairs)  13.2 us
    ppermute x2, starting transfers between devices, spread(): return lax.ppermute(value, ('y', 'core', 'x', 'z'), pairs)  12.9 us
    ppermute x4, starting transfers between devices, hand_in(): return lax.ppermute(value, ('y', 'core', 'x'), pairs)  11.8 us
    ppermute x2, waiting for transfers between devices, spread(): return lax.ppermute(value, ('y', 'core', 'x', 'z'), pairs)  9.38 us
    ppermute x1, starting transfers between devices, body(): other = lax.ppermute(amplitudes, 'core', swap)  8.77 us
    pallas_call x4, Pallas kernels, product(): pl.pallas_call(product_kernel, out_shape=jax.ShapeDtypeStruct((rows, cols...  7.53 us
    ppermute x9, waiting for transfers between devices, apart(): return lax.ppermute(value, ('core', axis), pairs)  7.45 us
  transfers between devices with their start and end apart: 17, of which 7 were waited for; matrix products, arithmetic and copies ran while one was open for 3% of the time, Pallas kernels for 11%

profile of v3, /device:TPU:1, one launch (start us, length us, event | category | flops | bytes accessed | tf_op | source)
XLA Modules:
  0.0 109.9 jit_solution(10546044589956390870)
XLA Ops:
  0.0 8.8 %collective-permute-start = (bf16[16,2048]{1,0:T(8,128)(2,1)}, bf16[16,2048]{1,0:T(8,128)(2,1)S(1)}, u32[]{:S(2)}, u32[]{:S(2)}) collective-permute-start(bf16[16,2048]{1,0:T(8,128)(2,1)} %param.5), channel_id=1, source_target_pairs={{0,64},{64,0},{1,65},{65,1},{2,66},{66,2},{3,67},{67,3},{4,68},{68... | collective-permute-start | bytes 196616 | tf_op jit(solution)/shard_map/ppermute | solution.py:149
  8.8 1.1 collective-permute-done
  9.9 2.3 %collective-permute-start.7 = (bf16[2048,1024]{1,0:T(8,128)(2,1)}, bf16[2048,1024]{1,0:T(8,128)(2,1)}, u32[]{:S(2)}, u32[]{:S(2)}) collective-permute-start(bf16[2048,1024]{1,0:T(8,128)(2,1)} %own_ref), channel_id=1, source_target_pairs={{0,64},{64,0},{1,65},{65,1},{2,66},{66,2},{3,67},{67,3},{4,68},{68... | collective-permute-start | bytes 12582920 | tf_op jit(solution)/shard_map/ppermute | solution.py:159
  12.1 0.9 broadcast_select_fusion.1
  13.0 7.1 %collective-permute-start.2 = (bf16[16,4096]{1,0:T(8,128)(2,1)S(1)}, bf16[16,4096]{1,0:T(8,128)(2,1)S(1)}, u32[]{:S(2)}, u32[]{:S(2)}) collective-permute-start(bf16[16,4096]{1,0:T(8,128)(2,1)S(1)} %pad_maximum_fusion), channel_id=1, source_target_pairs={{4,0},{5,1},{6,2},{7,3},{0,4},{1,5},{2,6},{3,7},{68,8},{69,9},{70,... | collective-permute-start | bytes 393224 | tf_op jit(solution)/shard_map/ppermute | solution.py:55
  20.2 5.8 %collective-permute-start.1 = (bf16[16,4096]{1,0:T(8,128)(2,1)S(1)}, bf16[16,4096]{1,0:T(8,128)(2,1)S(1)}, u32[]{:S(2)}, u32[]{:S(2)}) collective-permute-start(bf16[16,4096]{1,0:T(8,128)(2,1)S(1)} %pad_maximum_fusion), channel_id=1, source_target_pairs={{0,0},{1,1},{2,2},{3,3},{4,4},{5,5},{6,6},{7,7},{64,8},{65,9},{66,... | collective-permute-start | bytes 393224 | tf_op jit(solution)/shard_map/ppermute | solution.py:55
  26.0 0.8 multiply_reduce_fusion
  26.8 0.7 dynamic_slice.6
  27.5 0.1 slice.3
  27.6 0.7 dynamic_slice.7
  28.3 0.1 select_reduce_fusion.row_ref
  28.4 0.0 collective-permute-done.2
  28.4 9.4 %collective-permute-done.1 = bf16[16,4096]{1,0:T(8,128)(2,1)S(1)} collective-permute-done((bf16[16,4096]{1,0:T(8,128)(2,1)S(1)}, bf16[16,4096]{1,0:T(8,128)(2,1)S(1)}, u32[]{:S(2)}, u32[]{:S(2)}) %collective-permute-start.1) | collective-permute-done | bytes 131104 | tf_op jit(solution)/shard_map/ppermute | solution.py:55
  37.8 1.9 %collective-permute-start.3 = (bf16[32,4096]{1,0:T(8,128)(2,1)S(1)}, bf16[32,4096]{1,0:T(8,128)(2,1)S(1)}, u32[]{:S(2)}, u32[]{:S(2)}) collective-permute-start(bf16[32,4096]{1,0:T(8,128)(2,1)S(1)} %get-tuple-element.32), channel_id=1, source_target_pairs={{0,1},{1,2},{2,3},{3,4},{4,5},{5,6},{6,7},{7,8},{8,9},{9,10},{10,1... | collective-permute-start | bytes 786440 | tf_op jit(solution)/shard_map/ppermute | solution.py:34
  39.8 4.4 %collective-permute-start.5 = (bf16[32,4096]{1,0:T(8,128)(2,1)S(1)}, bf16[32,4096]{1,0:T(8,128)(2,1)S(1)}, u32[]{:S(2)}, u32[]{:S(2)}) collective-permute-start(bf16[32,4096]{1,0:T(8,128)(2,1)S(1)} %get-tuple-element.32), channel_id=1, source_target_pairs={{0,15},{1,0},{2,1},{3,2},{4,3},{5,4},{6,5},{7,6},{8,7},{9,8},{10,9... | collective-permute-start | bytes 786440 | tf_op jit(solution)/shard_map/ppermute | solution.py:34
  44.1 1.9 %collective-permute-start.6 = (bf16[32,4096]{1,0:T(8,128)(2,1)S(1)}, bf16[32,4096]{1,0:T(8,128)(2,1)S(1)}, u32[]{:S(2)}, u32[]{:S(2)}) collective-permute-start(bf16[32,4096]{1,0:T(8,128)(2,1)S(1)} %get-tuple-element.32), channel_id=1, source_target_pairs={{0,2},{1,3},{2,4},{3,5},{4,6},{5,7},{6,8},{7,9},{8,10},{9,11},{10,... | collective-permute-start | bytes 786440 | tf_op jit(solution)/shard_map/ppermute | solution.py:34
  46.1 0.0 collective-permute-done.3
  46.1 4.1 %collective-permute-start.4 = (bf16[64,4096]{1,0:T(8,128)(2,1)S(1)}, bf16[64,4096]{1,0:T(8,128)(2,1)S(1)}, u32[]{:S(2)}, u32[]{:S(2)}) collective-permute-start(bf16[64,4096]{1,0:T(8,128)(2,1)S(1)} %constant_dynamic-update-slice_fusion.2.far_ref), channel_id=1, source_target_pairs={{0,16},{16,32},{32,48},{48,0},{64,112},{80,64},{96,80},{112,96},{1... | collective-permute-start | bytes 1572872 | tf_op jit(solution)/shard_map/ppermute | solution.py:34
  50.2 2.3 %collective-permute-done.5 = bf16[32,4096]{1,0:T(8,128)(2,1)S(1)} collective-permute-done((bf16[32,4096]{1,0:T(8,128)(2,1)S(1)}, bf16[32,4096]{1,0:T(8,128)(2,1)S(1)}, u32[]{:S(2)}, u32[]{:S(2)}) %collective-permute-start.5) | collective-permute-done | bytes 262176 | tf_op jit(solution)/shard_map/ppermute | solution.py:34
  52.5 3.8 %collective-permute-done.6 = bf16[32,4096]{1,0:T(8,128)(2,1)S(1)} collective-permute-done((bf16[32,4096]{1,0:T(8,128)(2,1)S(1)}, bf16[32,4096]{1,0:T(8,128)(2,1)S(1)}, u32[]{:S(2)}, u32[]{:S(2)}) %collective-permute-start.6) | collective-permute-done | bytes 262176 | tf_op jit(solution)/shard_map/ppermute | solution.py:34
  56.4 3.8 %collective-permute-start.10 = (bf16[64,4096]{1,0:T(8,128)(2,1)S(1)}, bf16[64,4096]{1,0:T(8,128)(2,1)S(1)}, u32[]{:S(2)}, u32[]{:S(2)}) collective-permute-start(bf16[64,4096]{1,0:T(8,128)(2,1)S(1)} %constant_dynamic-update-slice_fusion.5.near_ref), channel_id=1, source_target_pairs={{0,16},{16,32},{32,48},{48,0},{64,112},{80,64},{96,80},{112,96},{1... | collective-permute-start | bytes 1572872 | tf_op jit(solution)/shard_map/ppermute | solution.py:34
  60.2 0.1 pad_add_fusion.place_ref
  60.3 1.9 %collective-permute-start.13 = (bf16[64,4096]{1,0:T(8,128)(2,1)S(1)}, bf16[64,4096]{1,0:T(8,128)(2,1)S(1)}, u32[]{:S(2)}, u32[]{:S(2)}) collective-permute-start(bf16[64,4096]{1,0:T(8,128)(2,1)S(1)} %constant_dynamic-update-slice_fusion.2.far_ref), channel_id=1, source_target_pairs={{0,48},{16,0},{32,16},{48,32},{64,80},{80,96},{96,112},{112,64},{1... | collective-permute-start | bytes 1572872 | tf_op jit(solution)/shard_map/ppermute | solution.py:34
  62.2 1.9 %collective-permute-start.12 = (bf16[64,4096]{1,0:T(8,128)(2,1)S(1)}, bf16[64,4096]{1,0:T(8,128)(2,1)S(1)}, u32[]{:S(2)}, u32[]{:S(2)}) collective-permute-start(bf16[64,4096]{1,0:T(8,128)(2,1)S(1)} %constant_dynamic-update-slice_fusion.5.near_ref), channel_id=1, source_target_pairs={{0,48},{16,0},{32,16},{48,32},{64,80},{80,96},{96,112},{112,64},{1... | collective-permute-start | bytes 1572872 | tf_op jit(solution)/shard_map/ppermute | solution.py:34
  64.1 0.0 collective-permute-done.7.other_ref
  64.2 4.3 %shard_map.55.held_ref = bf16[4096,1024]{1,0:T(8,128)(2,1)S(1)} custom-call(s32[2]{0:T(128)S(1)} %pad_add_fusion.place_ref, s32[64]{0:T(128)S(1)} %select_reduce_fusion.row_ref, s32[1,1024]{1,0:T(1,128)S(1)} %bitcast.3, bf16[2048,1024]{1,0:T(8,128)(2,1)} %own_ref, bf16[2048,1024]{1,0:T(8,128)(2,1)} %collective-permute-done.7.other_ref), custom_call_target="tpu_custom_call" | custom-call | bytes 16777216 | tf_op jit(solution)/shard_map/pallas_call | solution.py:99
  68.4 1.9 %shard_map.56 = f32[128,1024]{1,0:T(8,128)S(1)} custom-call(s32[2]{0:T(128)S(1)} %pad_add_fusion.place_ref, bf16[64,4096]{1,0:T(8,128)(2,1)S(1)} %constant_dynamic-update-slice_fusion.5.near_ref, bf16[64,4096]{1,0:T(8,128)(2,1)S(1)} %constant_dynamic-update-slice_fusion.2.far_ref, bf16[4096,1024]{1,0:T(8,128)(2,1)S(1)} %shard_map.55.held_ref), custom_call_target="tpu_custom_call" | custom-call | flops 1073741824 | bytes 8388608 | tf_op jit(solution)/shard_map/pallas_call | solution.py:133
  70.4 0.0 collective-permute-done.4.far_ref
  70.4 4.6 %collective-permute-start.8 = (bf16[64,4096]{1,0:T(8,128)(2,1)S(1)}, bf16[64,4096]{1,0:T(8,128)(2,1)S(1)}, u32[]{:S(2)}, u32[]{:S(2)}) collective-permute-start(bf16[64,4096]{1,0:T(8,128)(2,1)S(1)} %collective-permute-done.4.far_ref), channel_id=1, source_target_pairs={{0,16},{16,32},{32,48},{48,0},{64,112},{80,64},{96,80},{112,96},{1... | collective-permute-start | bytes 1572872 | tf_op jit(solution)/shard_map/ppermute | solution.py:34
  74.9 6.1 %collective-permute-start.9 = (f32[128,1024]{1,0:T(8,128)S(1)}, f32[128,1024]{1,0:T(8,128)S(1)}, u32[]{:S(2)}, u32[]{:S(2)}) collective-permute-start(f32[128,1024]{1,0:T(8,128)S(1)} %shard_map.56), channel_id=1, source_target_pairs={{0,0},{16,144},{32,416},{48,304},{64,320},{80,464},{96,224},{112,1... | collective-permute-start | bytes 1572872 | tf_op jit(solution)/shard_map/ppermute | solution.py:65
  81.1 0.0 collective-permute-done.10.near_ref
  81.1 1.9 %collective-permute-start.15 = (bf16[64,4096]{1,0:T(8,128)(2,1)S(1)}, bf16[64,4096]{1,0:T(8,128)(2,1)S(1)}, u32[]{:S(2)}, u32[]{:S(2)}) collective-permute-start(bf16[64,4096]{1,0:T(8,128)(2,1)S(1)} %collective-permute-done.10.near_ref), channel_id=1, source_target_pairs={{0,16},{16,32},{32,48},{48,0},{64,112},{80,64},{96,80},{112,96},{1... | collective-permute-start | bytes 1572872 | tf_op jit(solution)/shard_map/ppermute | solution.py:34
  83.0 1.9 %shard_map.57 = f32[128,1024]{1,0:T(8,128)S(1)} custom-call(s32[2]{0:T(128)S(1)} %pad_add_fusion.place_ref, bf16[64,4096]{1,0:T(8,128)(2,1)S(1)} %collective-permute-done.10.near_ref, bf16[64,4096]{1,0:T(8,128)(2,1)S(1)} %collective-permute-done.4.far_ref, bf16[4096,1024]{1,0:T(8,128)(2,1)S(1)} %shard_map.55.held_ref), custom_call_target="tpu_custom_call" | custom-call | flops 1073741824 | bytes 8388608 | tf_op jit(solution)/shard_map/pallas_call | solution.py:133
  84.9 0.0 collective-permute-done.13.far_ref
  84.9 2.5 %collective-permute-start.11 = (f32[128,1024]{1,0:T(8,128)S(1)}, f32[128,1024]{1,0:T(8,128)S(1)}, u32[]{:S(2)}, u32[]{:S(2)}) collective-permute-start(f32[128,1024]{1,0:T(8,128)S(1)} %shard_map.57), channel_id=1, source_target_pairs={{0,256},{16,16},{32,160},{48,432},{64,448},{80,208},{96,96},{112,3... | collective-permute-start | bytes 1572872 | tf_op jit(solution)/shard_map/ppermute | solution.py:65
  87.4 0.0 collective-permute-done.12.near_ref
  87.4 1.9 %shard_map.58 = f32[128,1024]{1,0:T(8,128)S(1)} custom-call(s32[2]{0:T(128)S(1)} %pad_add_fusion.place_ref, bf16[64,4096]{1,0:T(8,128)(2,1)S(1)} %collective-permute-done.12.near_ref, bf16[64,4096]{1,0:T(8,128)(2,1)S(1)} %collective-permute-done.13.far_ref, bf16[4096,1024]{1,0:T(8,128)(2,1)S(1)} %shard_map.55.held_ref), custom_call_target="tpu_custom_call" | custom-call | flops 1073741824 | bytes 8388608 | tf_op jit(solution)/shard_map/pallas_call | solution.py:133
  89.3 0.7 collective-permute-start.14
  90.0 0.0 collective-permute-done.8.far_ref
  90.0 0.0 collective-permute-done.9
  90.0 1.3 %collective-permute-done.15.near_ref = bf16[64,4096]{1,0:T(8,128)(2,1)S(1)} collective-permute-done((bf16[64,4096]{1,0:T(8,128)(2,1)S(1)}, bf16[64,4096]{1,0:T(8,128)(2,1)S(1)}, u32[]{:S(2)}, u32[]{:S(2)}) %collective-permute-start.15) | collective-permute-done | bytes 524320 | tf_op jit(solution)/shard_map/ppermute | solution.py:34
  91.3 1.9 %shard_map.59 = f32[128,1024]{1,0:T(8,128)S(1)} custom-call(s32[2]{0:T(128)S(1)} %pad_add_fusion.place_ref, bf16[64,4096]{1,0:T(8,128)(2,1)S(1)} %collective-permute-done.15.near_ref, bf16[64,4096]{1,0:T(8,128)(2,1)S(1)} %collective-permute-done.8.far_ref, bf16[4096,1024]{1,0:T(8,128)(2,1)S(1)} %shard_map.55.held_ref), custom_call_target="tpu_custom_call" | custom-call | flops 1073741824 | bytes 8388608 | tf_op jit(solution)/shard_map/pallas_call | solution.py:133
  93.2 2.5 %collective-permute-start.16 = (f32[128,1024]{1,0:T(8,128)S(1)}, f32[128,1024]{1,0:T(8,128)S(1)}, u32[]{:S(2)}, u32[]{:S(2)}) collective-permute-start(f32[128,1024]{1,0:T(8,128)S(1)} %shard_map.59), channel_id=1, source_target_pairs={{0,384},{16,272},{32,32},{48,176},{64,192},{80,80},{96,352},{112,4... | collective-permute-start | bytes 1572872 | tf_op jit(solution)/shard_map/ppermute | solution.py:65
  95.7 4.2 %collective-permute-done.11 = f32[128,1024]{1,0:T(8,128)S(1)} collective-permute-done((f32[128,1024]{1,0:T(8,128)S(1)}, f32[128,1024]{1,0:T(8,128)S(1)}, u32[]{:S(2)}, u32[]{:S(2)}) %collective-permute-start.11) | collective-permute-done | bytes 524320 | tf_op jit(solution)/shard_map/ppermute | solution.py:65
  99.9 0.0 collective-permute-done.14
  99.9 9.0 %collective-permute-done.16 = f32[128,1024]{1,0:T(8,128)S(1)} collective-permute-done((f32[128,1024]{1,0:T(8,128)S(1)}, f32[128,1024]{1,0:T(8,128)S(1)}, u32[]{:S(2)}, u32[]{:S(2)}) %collective-permute-start.16) | collective-permute-done | bytes 524320 | tf_op jit(solution)/shard_map/ppermute | solution.py:65
  109.0 0.9 add_add_fusion
  (6 shorter events, 0.1 us)
Async XLA Ops:
  0.0 9.9 %collective-permute-start = (bf16[16,2048]{1,0:T(8,128)(2,1)}, bf16[16,2048]{1,0:T(8,128)(2,1)S(1)}, u32[]{:S(2)}, u32[]{:S(2)}) collective-permute-start(bf16[16,2048]{1,0:T(8,128)(2,1)} %param.5), channel_id=1, source_target_pairs={{0,64},{64,0},{1,65},{65,1},{2,66},{66,2},{3,67},{67,3},{4,68},{68... | collective-permute-start | bytes 196616 | tf_op jit(solution)/shard_map/ppermute | solution.py:149
  9.9 54.3 %collective-permute-start.7 = (bf16[2048,1024]{1,0:T(8,128)(2,1)}, bf16[2048,1024]{1,0:T(8,128)(2,1)}, u32[]{:S(2)}, u32[]{:S(2)}) collective-permute-start(bf16[2048,1024]{1,0:T(8,128)(2,1)} %own_ref), channel_id=1, source_target_pairs={{0,64},{64,0},{1,65},{65,1},{2,66},{66,2},{3,67},{67,3},{4,68},{68... | collective-permute-start | bytes 12582920 | tf_op jit(solution)/shard_map/ppermute | solution.py:159
  13.0 15.4 %collective-permute-start.2 = (bf16[16,4096]{1,0:T(8,128)(2,1)S(1)}, bf16[16,4096]{1,0:T(8,128)(2,1)S(1)}, u32[]{:S(2)}, u32[]{:S(2)}) collective-permute-start(bf16[16,4096]{1,0:T(8,128)(2,1)S(1)} %pad_maximum_fusion), channel_id=1, source_target_pairs={{4,0},{5,1},{6,2},{7,3},{0,4},{1,5},{2,6},{3,7},{68,8},{69,9},{70,... | collective-permute-start | bytes 393224 | tf_op jit(solution)/shard_map/ppermute | solution.py:55
  20.2 17.6 %collective-permute-start.1 = (bf16[16,4096]{1,0:T(8,128)(2,1)S(1)}, bf16[16,4096]{1,0:T(8,128)(2,1)S(1)}, u32[]{:S(2)}, u32[]{:S(2)}) collective-permute-start(bf16[16,4096]{1,0:T(8,128)(2,1)S(1)} %pad_maximum_fusion), channel_id=1, source_target_pairs={{0,0},{1,1},{2,2},{3,3},{4,4},{5,5},{6,6},{7,7},{64,8},{65,9},{66,... | collective-permute-start | bytes 393224 | tf_op jit(solution)/shard_map/ppermute | solution.py:55
  37.8 8.2 %collective-permute-start.3 = (bf16[32,4096]{1,0:T(8,128)(2,1)S(1)}, bf16[32,4096]{1,0:T(8,128)(2,1)S(1)}, u32[]{:S(2)}, u32[]{:S(2)}) collective-permute-start(bf16[32,4096]{1,0:T(8,128)(2,1)S(1)} %get-tuple-element.32), channel_id=1, source_target_pairs={{0,1},{1,2},{2,3},{3,4},{4,5},{5,6},{6,7},{7,8},{8,9},{9,10},{10,1... | collective-permute-start | bytes 786440 | tf_op jit(solution)/shard_map/ppermute | solution.py:34
  39.8 12.7 %collective-permute-start.5 = (bf16[32,4096]{1,0:T(8,128)(2,1)S(1)}, bf16[32,4096]{1,0:T(8,128)(2,1)S(1)}, u32[]{:S(2)}, u32[]{:S(2)}) collective-permute-start(bf16[32,4096]{1,0:T(8,128)(2,1)S(1)} %get-tuple-element.32), channel_id=1, source_target_pairs={{0,15},{1,0},{2,1},{3,2},{4,3},{5,4},{6,5},{7,6},{8,7},{9,8},{10,9... | collective-permute-start | bytes 786440 | tf_op jit(solution)/shard_map/ppermute | solution.py:34
  44.1 12.2 %collective-permute-start.6 = (bf16[32,4096]{1,0:T(8,128)(2,1)S(1)}, bf16[32,4096]{1,0:T(8,128)(2,1)S(1)}, u32[]{:S(2)}, u32[]{:S(2)}) collective-permute-start(bf16[32,4096]{1,0:T(8,128)(2,1)S(1)} %get-tuple-element.32), channel_id=1, source_target_pairs={{0,2},{1,3},{2,4},{3,5},{4,6},{5,7},{6,8},{7,9},{8,10},{9,11},{10,... | collective-permute-start | bytes 786440 | tf_op jit(solution)/shard_map/ppermute | solution.py:34
  46.1 24.2 %collective-permute-start.4 = (bf16[64,4096]{1,0:T(8,128)(2,1)S(1)}, bf16[64,4096]{1,0:T(8,128)(2,1)S(1)}, u32[]{:S(2)}, u32[]{:S(2)}) collective-permute-start(bf16[64,4096]{1,0:T(8,128)(2,1)S(1)} %constant_dynamic-update-slice_fusion.2.far_ref), channel_id=1, source_target_pairs={{0,16},{16,32},{32,48},{48,0},{64,112},{80,64},{96,80},{112,96},{1... | collective-permute-start | bytes 1572872 | tf_op jit(solution)/shard_map/ppermute | solution.py:34
  56.4 24.7 %collective-permute-start.10 = (bf16[64,4096]{1,0:T(8,128)(2,1)S(1)}, bf16[64,4096]{1,0:T(8,128)(2,1)S(1)}, u32[]{:S(2)}, u32[]{:S(2)}) collective-permute-start(bf16[64,4096]{1,0:T(8,128)(2,1)S(1)} %constant_dynamic-update-slice_fusion.5.near_ref), channel_id=1, source_target_pairs={{0,16},{16,32},{32,48},{48,0},{64,112},{80,64},{96,80},{112,96},{1... | collective-permute-start | bytes 1572872 | tf_op jit(solution)/shard_map/ppermute | solution.py:34
  60.3 24.6 %collective-permute-start.13 = (bf16[64,4096]{1,0:T(8,128)(2,1)S(1)}, bf16[64,4096]{1,0:T(8,128)(2,1)S(1)}, u32[]{:S(2)}, u32[]{:S(2)}) collective-permute-start(bf16[64,4096]{1,0:T(8,128)(2,1)S(1)} %constant_dynamic-update-slice_fusion.2.far_ref), channel_id=1, source_target_pairs={{0,48},{16,0},{32,16},{48,32},{64,80},{80,96},{96,112},{112,64},{1... | collective-permute-start | bytes 1572872 | tf_op jit(solution)/shard_map/ppermute | solution.py:34
  62.2 25.2 %collective-permute-start.12 = (bf16[64,4096]{1,0:T(8,128)(2,1)S(1)}, bf16[64,4096]{1,0:T(8,128)(2,1)S(1)}, u32[]{:S(2)}, u32[]{:S(2)}) collective-permute-start(bf16[64,4096]{1,0:T(8,128)(2,1)S(1)} %constant_dynamic-update-slice_fusion.5.near_ref), channel_id=1, source_target_pairs={{0,48},{16,0},{32,16},{48,32},{64,80},{80,96},{96,112},{112,64},{1... | collective-permute-start | bytes 1572872 | tf_op jit(solution)/shard_map/ppermute | solution.py:34
  70.4 19.6 %collective-permute-start.8 = (bf16[64,4096]{1,0:T(8,128)(2,1)S(1)}, bf16[64,4096]{1,0:T(8,128)(2,1)S(1)}, u32[]{:S(2)}, u32[]{:S(2)}) collective-permute-start(bf16[64,4096]{1,0:T(8,128)(2,1)S(1)} %collective-permute-done.4.far_ref), channel_id=1, source_target_pairs={{0,16},{16,32},{32,48},{48,0},{64,112},{80,64},{96,80},{112,96},{1... | collective-permute-start | bytes 1572872 | tf_op jit(solution)/shard_map/ppermute | solution.py:34
  74.9 15.1 %collective-permute-start.9 = (f32[128,1024]{1,0:T(8,128)S(1)}, f32[128,1024]{1,0:T(8,128)S(1)}, u32[]{:S(2)}, u32[]{:S(2)}) collective-permute-start(f32[128,1024]{1,0:T(8,128)S(1)} %shard_map.56), channel_id=1, source_target_pairs={{0,0},{16,144},{32,416},{48,304},{64,320},{80,464},{96,224},{112,1... | collective-permute-start | bytes 1572872 | tf_op jit(solution)/shard_map/ppermute | solution.py:65
  81.1 10.2 %collective-permute-start.15 = (bf16[64,4096]{1,0:T(8,128)(2,1)S(1)}, bf16[64,4096]{1,0:T(8,128)(2,1)S(1)}, u32[]{:S(2)}, u32[]{:S(2)}) collective-permute-start(bf16[64,4096]{1,0:T(8,128)(2,1)S(1)} %collective-permute-done.10.near_ref), channel_id=1, source_target_pairs={{0,16},{16,32},{32,48},{48,0},{64,112},{80,64},{96,80},{112,96},{1... | collective-permute-start | bytes 1572872 | tf_op jit(solution)/shard_map/ppermute | solution.py:34
  84.9 15.0 %collective-permute-start.11 = (f32[128,1024]{1,0:T(8,128)S(1)}, f32[128,1024]{1,0:T(8,128)S(1)}, u32[]{:S(2)}, u32[]{:S(2)}) collective-permute-start(f32[128,1024]{1,0:T(8,128)S(1)} %shard_map.57), channel_id=1, source_target_pairs={{0,256},{16,16},{32,160},{48,432},{64,448},{80,208},{96,96},{112,3... | collective-permute-start | bytes 1572872 | tf_op jit(solution)/shard_map/ppermute | solution.py:65
  89.3 10.7 %collective-permute-start.14 = (f32[128,1024]{1,0:T(8,128)S(1)}, f32[128,1024]{1,0:T(8,128)S(1)}, u32[]{:S(2)}, u32[]{:S(2)}) collective-permute-start(f32[128,1024]{1,0:T(8,128)S(1)} %shard_map.58), channel_id=1, source_target_pairs={{0,128},{16,400},{32,288},{48,48},{64,64},{80,336},{96,480},{112,2... | collective-permute-start | bytes 1572872 | tf_op jit(solution)/shard_map/ppermute | solution.py:65
  93.2 15.8 %collective-permute-start.16 = (f32[128,1024]{1,0:T(8,128)S(1)}, f32[128,1024]{1,0:T(8,128)S(1)}, u32[]{:S(2)}, u32[]{:S(2)}) collective-permute-start(f32[128,1024]{1,0:T(8,128)S(1)} %shard_map.59), channel_id=1, source_target_pairs={{0,384},{16,272},{32,32},{48,176},{64,192},{80,80},{96,352},{112,4... | collective-permute-start | bytes 1572872 | tf_op jit(solution)/shard_map/ppermute | solution.py:65

commit v4 on v3

--- a/solution.py
+++ b/solution.py
@@ -111,17 +111,29 @@
 
 
 def product_kernel(place_ref, near_ref, far_ref, held_ref, out_ref):
-    core, base, cols = place_ref[0], place_ref[1], held_ref.shape[1]
-    rows = out_ref.shape[0] // HALF
+    core, z, cols = place_ref[0], place_ref[1], held_ref.shape[1]
+    rows, depth = out_ref.shape[0] // HALF, held_ref.shape[0] // CORE
     step = 2 * core - 1
-    sources = [base + k * step + half for k in (-1, 2, 0, 1) for half in (0, 4)]
-    block = jnp.concatenate([near_ref[...], far_ref[...]])
+    origins = [lax.rem(z + k * step + Z, Z) for k in (-1, 2, 0, 1)]
+
+    def columns(half):
+        pieces = []
+        for index, origin in enumerate(origins):
+            ref, first = (near_ref, far_ref)[index // 2], index % 2 * 2 * rows
+            swapped = origin // HALF
+            at = pl.multiple_of((swapped if half == 0 else 1 - swapped) * depth, depth)
+            pieces.append(ref[first : first + 2 * rows, pl.ds(at, depth)])
+        return jnp.concatenate(pieces)
+
+    left, right = columns(0), columns(1)
+    sources = [origin + half for origin in origins for half in (0, 4)]
     width = min(256, cols)
     for first in range(0, cols, width):
         part = slice(first, first + width)
-        value = jnp.dot(block, held_ref[:, part], preferred_element_type=jnp.float32)
+        value = jnp.dot(left, held_ref[:depth, part], preferred_element_type=jnp.float32)
+        value += jnp.dot(right, held_ref[depth:, part], preferred_element_type=jnp.float32)
         for index, source in enumerate(sources):
-            at = lax.rem(source + HALF, HALF) * rows
+            at = lax.rem(source, HALF) * rows
             out_ref[pl.ds(pl.multiple_of(at, rows), rows), part] = value[
                 index * rows : (index + 1) * rows
             ]
@@ -147,35 +159,31 @@
     swap = [(0, 1), (1, 0)]
 
     other = lax.ppermute(amplitudes, "core", swap)
-    other, integrals, contract_irrep, outer_irrep, block_map = lax.optimization_barrier(
-        (other, integrals, contract_irrep, outer_irrep, block_map)
-    )
-    both = jnp.concatenate(
-        [jnp.where(core == 0, amplitudes, other), jnp.where(core == 0, other, amplitudes)], axis=1
-    )
+    other, integrals = lax.optimization_barrier((other, integrals))
+    both = jnp.concatenate([amplitudes, other], axis=1)
+    other = lax.ppermute(integrals, "core", swap)
 
     first = spread(both, 0)
     second = spread(both, 4)
-    other = lax.ppermute(integrals, "core", swap)
-    place = jnp.stack([core, z % HALF]).astype(jnp.int32)
+    place = jnp.stack([core, z]).astype(jnp.int32)
     labels = outer_labels_of(contract_irrep, outer_irrep, block_map, *integrals.shape)
     second, labels = lax.optimization_barrier((second, labels))
 
     here = jnp.concatenate([first, second])
+    back = apart(here, "z", Z, 1)
     away = apart(here, "z", Z, 2)
-    back = apart(here, "z", Z, 1)
+    far = jnp.concatenate([here, back])
     ahead = apart(here, "z", Z, -1)
     near = jnp.concatenate([ahead, away])
-    far = jnp.concatenate([here, back])
 
     near_back, near_ahead = apart(near, "x", X, 1), apart(near, "x", X, -1)
     far_back, far_ahead = apart(far, "x", X, 1), apart(far, "x", X, -1)
     near_away = apart(near_back, "x", X, 1)
-    far, integrals = lax.optimization_barrier((far, integrals))
+    near, integrals = lax.optimization_barrier((near, integrals))
     held = hold(place, *labels, integrals, other)
     own = product(place, near, far, held)
     received = [hand_in(own, 0)]
-    far_back, own = lax.optimization_barrier((far_back, own))
+    far_back, far_ahead, own = lax.optimization_barrier((far_back, far_ahead, own))
     far_away = apart(far_back, "x", X, 1)
     received.append(hand_in(product(place, near_back, far_back, held), 1))
     received.append(hand_in(product(place, near_ahead, far_ahead, held), -1))

time: 111 us -> 109 us (0.982)
  starting transfers between devices: 62.2 us -> 60.1 us
    ppermute x4, starting transfers between devices: 11.8 us -> 9.76 us  [hand_in(): return lax.ppermute(value, ('y', 'core', 'x'), pairs)]
    ppermute x4, waiting for transfers between devices: 13.2 us -> 15.3 us  [hand_in(): return lax.ppermute(value, ('y', 'core', 'x'), pairs)]
    ppermute x9, waiting for transfers between devices: 7.45 us -> 5.53 us  [apart(): return lax.ppermute(value, ('core', axis), pairs)]
where the time goes in v4:
time: 109 us; the launch traced here: 108 us
  starting transfers between devices  60.1 us (55%)
  waiting for transfers between devices  31.3 us (29%)
  Pallas kernels  11.8 us (11%)
  local copies, waits for them, and re-layouts  2.51 us (2%)
  other arithmetic  1.91 us (2%)
    ppermute x9, starting transfers between devices, apart(): return lax.ppermute(value, ('core', axis), pairs)  26.4 us
    ppermute x4, waiting for transfers between devices, hand_in(): return lax.ppermute(value, ('y', 'core', 'x'), pairs)  15.3 us
    ppermute x2, starting transfers between devices, spread(): return lax.ppermute(value, ('y', 'core', 'x', 'z'), pairs)  12.9 us
    ppermute x4, starting transfers between devices, hand_in(): return lax.ppermute(value, ('y', 'core', 'x'), pairs)  9.76 us
    ppermute x2, waiting for transfers between devices, spread(): return lax.ppermute(value, ('y', 'core', 'x', 'z'), pairs)  9.38 us
    ppermute x1, starting transfers between devices, body(): other = lax.ppermute(amplitudes, 'core', swap)  8.77 us
    pallas_call x4, Pallas kernels, product(): pl.pallas_call(product_kernel, out_shape=jax.ShapeDtypeStruct((rows, cols...  7.52 us
    ppermute x9, waiting for transfers between devices, apart(): return lax.ppermute(value, ('core', axis), pairs)  5.53 us
  transfers between devices with their start and end apart: 17, of which 7 were waited for; matrix products, arithmetic and copies ran while one was open for 3% of the time, Pallas kernels for 11%

profile of v4, /device:TPU:1, one launch (start us, length us, event | category | flops | bytes accessed | tf_op | source)
XLA Modules:
  0.0 107.9 jit_solution(1480878340817710981)
XLA Ops:
  0.0 8.8 %collective-permute-start = (bf16[16,2048]{1,0:T(8,128)(2,1)}, bf16[16,2048]{1,0:T(8,128)(2,1)S(1)}, u32[]{:S(2)}, u32[]{:S(2)}) collective-permute-start(bf16[16,2048]{1,0:T(8,128)(2,1)} %param.5), channel_id=1, source_target_pairs={{0,64},{64,0},{1,65},{65,1},{2,66},{66,2},{3,67},{67,3},{4,68},{68... | collective-permute-start | bytes 196616 | tf_op jit(solution)/shard_map/ppermute | solution.py:161
  8.8 1.1 %collective-permute-done = bf16[16,2048]{1,0:T(8,128)(2,1)S(1)} collective-permute-done((bf16[16,2048]{1,0:T(8,128)(2,1)}, bf16[16,2048]{1,0:T(8,128)(2,1)S(1)}, u32[]{:S(2)}, u32[]{:S(2)}) %collective-permute-start) | collective-permute-done | bytes 65568 | tf_op jit(solution)/shard_map/ppermute | solution.py:161
  9.9 2.3 %collective-permute-start.8 = (bf16[2048,1024]{1,0:T(8,128)(2,1)}, bf16[2048,1024]{1,0:T(8,128)(2,1)}, u32[]{:S(2)}, u32[]{:S(2)}) collective-permute-start(bf16[2048,1024]{1,0:T(8,128)(2,1)} %own_ref), channel_id=1, source_target_pairs={{0,64},{64,0},{1,65},{65,1},{2,66},{66,2},{3,67},{67,3},{4,68},{68... | collective-permute-start | bytes 12582920 | tf_op jit(solution)/shard_map/ppermute | solution.py:164
  12.1 0.8 constant_dynamic-update-slice_fusion.1
  13.0 7.1 %collective-permute-start.2 = (bf16[16,4096]{1,0:T(8,128)(2,1)S(1)}, bf16[16,4096]{1,0:T(8,128)(2,1)S(1)}, u32[]{:S(2)}, u32[]{:S(2)}) collective-permute-start(bf16[16,4096]{1,0:T(8,128)(2,1)S(1)} %constant_dynamic-update-slice_fusion), channel_id=1, source_target_pairs={{4,0},{5,1},{6,2},{7,3},{0,4},{1,5},{2,6},{3,7},{68,8},{69,9},{70,... | collective-permute-start | bytes 393224 | tf_op jit(solution)/shard_map/ppermute | solution.py:55
  20.1 5.8 %collective-permute-start.1 = (bf16[16,4096]{1,0:T(8,128)(2,1)S(1)}, bf16[16,4096]{1,0:T(8,128)(2,1)S(1)}, u32[]{:S(2)}, u32[]{:S(2)}) collective-permute-start(bf16[16,4096]{1,0:T(8,128)(2,1)S(1)} %constant_dynamic-update-slice_fusion), channel_id=1, source_target_pairs={{0,0},{1,1},{2,2},{3,3},{4,4},{5,5},{6,6},{7,7},{64,8},{65,9},{66,... | collective-permute-start | bytes 393224 | tf_op jit(solution)/shard_map/ppermute | solution.py:55
  25.9 0.8 multiply_reduce_fusion
  26.7 0.7 dynamic_slice.6
  27.4 0.1 slice.3
  27.6 0.7 dynamic_slice.7
  28.3 0.1 select_reduce_fusion.row_ref
  28.4 0.0 collective-permute-done.2
  28.4 9.4 %collective-permute-done.1 = bf16[16,4096]{1,0:T(8,128)(2,1)S(1)} collective-permute-done((bf16[16,4096]{1,0:T(8,128)(2,1)S(1)}, bf16[16,4096]{1,0:T(8,128)(2,1)S(1)}, u32[]{:S(2)}, u32[]{:S(2)}) %collective-permute-start.1) | collective-permute-done | bytes 131104 | tf_op jit(solution)/shard_map/ppermute | solution.py:55
  37.8 1.9 %collective-permute-start.3 = (bf16[32,4096]{1,0:T(8,128)(2,1)S(1)}, bf16[32,4096]{1,0:T(8,128)(2,1)S(1)}, u32[]{:S(2)}, u32[]{:S(2)}) collective-permute-start(bf16[32,4096]{1,0:T(8,128)(2,1)S(1)} %get-tuple-element.28), channel_id=1, source_target_pairs={{0,1},{1,2},{2,3},{3,4},{4,5},{5,6},{6,7},{7,8},{8,9},{9,10},{10,1... | collective-permute-start | bytes 786440 | tf_op jit(solution)/shard_map/ppermute | solution.py:34
  39.7 4.4 %collective-permute-start.6 = (bf16[32,4096]{1,0:T(8,128)(2,1)S(1)}, bf16[32,4096]{1,0:T(8,128)(2,1)S(1)}, u32[]{:S(2)}, u32[]{:S(2)}) collective-permute-start(bf16[32,4096]{1,0:T(8,128)(2,1)S(1)} %get-tuple-element.28), channel_id=1, source_target_pairs={{0,15},{1,0},{2,1},{3,2},{4,3},{5,4},{6,5},{7,6},{8,7},{9,8},{10,9... | collective-permute-start | bytes 786440 | tf_op jit(solution)/shard_map/ppermute | solution.py:34
  44.1 1.9 %collective-permute-start.7 = (bf16[32,4096]{1,0:T(8,128)(2,1)S(1)}, bf16[32,4096]{1,0:T(8,128)(2,1)S(1)}, u32[]{:S(2)}, u32[]{:S(2)}) collective-permute-start(bf16[32,4096]{1,0:T(8,128)(2,1)S(1)} %get-tuple-element.28), channel_id=1, source_target_pairs={{0,2},{1,3},{2,4},{3,5},{4,6},{5,7},{6,8},{7,9},{8,10},{9,11},{10,... | collective-permute-start | bytes 786440 | tf_op jit(solution)/shard_map/ppermute | solution.py:34
  46.0 0.0 collective-permute-done.3
  46.1 4.1 %collective-permute-start.4 = (bf16[64,4096]{1,0:T(8,128)(2,1)S(1)}, bf16[64,4096]{1,0:T(8,128)(2,1)S(1)}, u32[]{:S(2)}, u32[]{:S(2)}) collective-permute-start(bf16[64,4096]{1,0:T(8,128)(2,1)S(1)} %constant_dynamic-update-slice_fusion.4.far_ref), channel_id=1, source_target_pairs={{0,16},{16,32},{32,48},{48,0},{64,112},{80,64},{96,80},{112,96},{1... | collective-permute-start | bytes 1572872 | tf_op jit(solution)/shard_map/ppermute | solution.py:34
  50.2 1.9 %collective-permute-start.5 = (bf16[64,4096]{1,0:T(8,128)(2,1)S(1)}, bf16[64,4096]{1,0:T(8,128)(2,1)S(1)}, u32[]{:S(2)}, u32[]{:S(2)}) collective-permute-start(bf16[64,4096]{1,0:T(8,128)(2,1)S(1)} %constant_dynamic-update-slice_fusion.4.far_ref), channel_id=1, source_target_pairs={{0,48},{16,0},{32,16},{48,32},{64,80},{80,96},{96,112},{112,64},{1... | collective-permute-start | bytes 1572872 | tf_op jit(solution)/shard_map/ppermute | solution.py:34
  52.1 0.4 collective-permute-done.6
  52.5 3.8 %collective-permute-done.7 = bf16[32,4096]{1,0:T(8,128)(2,1)S(1)} collective-permute-done((bf16[32,4096]{1,0:T(8,128)(2,1)S(1)}, bf16[32,4096]{1,0:T(8,128)(2,1)S(1)}, u32[]{:S(2)}, u32[]{:S(2)}) %collective-permute-start.7) | collective-permute-done | bytes 262176 | tf_op jit(solution)/shard_map/ppermute | solution.py:34
  56.3 3.8 %collective-permute-start.11 = (bf16[64,4096]{1,0:T(8,128)(2,1)S(1)}, bf16[64,4096]{1,0:T(8,128)(2,1)S(1)}, u32[]{:S(2)}, u32[]{:S(2)}) collective-permute-start(bf16[64,4096]{1,0:T(8,128)(2,1)S(1)} %constant_dynamic-update-slice_fusion.7.near_ref), channel_id=1, source_target_pairs={{0,16},{16,32},{32,48},{48,0},{64,112},{80,64},{96,80},{112,96},{1... | collective-permute-start | bytes 1572872 | tf_op jit(solution)/shard_map/ppermute | solution.py:34
  60.2 0.1 pad_add_fusion.place_ref
  60.3 1.9 %collective-permute-start.13 = (bf16[64,4096]{1,0:T(8,128)(2,1)S(1)}, bf16[64,4096]{1,0:T(8,128)(2,1)S(1)}, u32[]{:S(2)}, u32[]{:S(2)}) collective-permute-start(bf16[64,4096]{1,0:T(8,128)(2,1)S(1)} %constant_dynamic-update-slice_fusion.7.near_ref), channel_id=1, source_target_pairs={{0,48},{16,0},{32,16},{48,32},{64,80},{80,96},{96,112},{112,64},{1... | collective-permute-start | bytes 1572872 | tf_op jit(solution)/shard_map/ppermute | solution.py:34
  62.2 0.0 collective-permute-done.8.other_ref
  62.2 4.3 %shard_map.55.held_ref = bf16[4096,1024]{1,0:T(8,128)(2,1)S(1)} custom-call(s32[2]{0:T(128)S(1)} %pad_add_fusion.place_ref, s32[64]{0:T(128)S(1)} %select_reduce_fusion.row_ref, s32[1,1024]{1,0:T(1,128)S(1)} %bitcast.3, bf16[2048,1024]{1,0:T(8,128)(2,1)} %own_ref, bf16[2048,1024]{1,0:T(8,128)(2,1)} %collective-permute-done.8.other_ref), custom_call_target="tpu_custom_call" | custom-call | bytes 16777216 | tf_op jit(solution)/shard_map/pallas_call | solution.py:99
  66.5 1.9 %shard_map.56 = f32[128,1024]{1,0:T(8,128)S(1)} custom-call(s32[2]{0:T(128)S(1)} %pad_add_fusion.place_ref, bf16[64,4096]{1,0:T(8,128)(2,1)S(1)} %constant_dynamic-update-slice_fusion.7.near_ref, bf16[64,4096]{1,0:T(8,128)(2,1)S(1)} %constant_dynamic-update-slice_fusion.4.far_ref, bf16[4096,1024]{1,0:T(8,128)(2,1)S(1)} %shard_map.55.held_ref), custom_call_target="tpu_custom_call" | custom-call | flops 1073741824 | bytes 8388608 | tf_op jit(solution)/shard_map/pallas_call | solution.py:145
  68.4 0.0 collective-permute-done.4.far_ref
  68.4 0.0 collective-permute-done.5.far_ref
  68.4 4.6 %collective-permute-start.9 = (bf16[64,4096]{1,0:T(8,128)(2,1)S(1)}, bf16[64,4096]{1,0:T(8,128)(2,1)S(1)}, u32[]{:S(2)}, u32[]{:S(2)}) collective-permute-start(bf16[64,4096]{1,0:T(8,128)(2,1)S(1)} %collective-permute-done.4.far_ref), channel_id=1, source_target_pairs={{0,16},{16,32},{32,48},{48,0},{64,112},{80,64},{96,80},{112,96},{1... | collective-permute-start | bytes 1572872 | tf_op jit(solution)/shard_map/ppermute | solution.py:34
  73.0 4.7 %collective-permute-start.10 = (f32[128,1024]{1,0:T(8,128)S(1)}, f32[128,1024]{1,0:T(8,128)S(1)}, u32[]{:S(2)}, u32[]{:S(2)}) collective-permute-start(f32[128,1024]{1,0:T(8,128)S(1)} %shard_map.56), channel_id=1, source_target_pairs={{0,0},{16,144},{32,416},{48,304},{64,320},{80,464},{96,224},{112,1... | collective-permute-start | bytes 1572872 | tf_op jit(solution)/shard_map/ppermute | solution.py:65
  77.6 0.0 collective-permute-done.11.near_ref
  77.6 1.9 %collective-permute-start.15 = (bf16[64,4096]{1,0:T(8,128)(2,1)S(1)}, bf16[64,4096]{1,0:T(8,128)(2,1)S(1)}, u32[]{:S(2)}, u32[]{:S(2)}) collective-permute-start(bf16[64,4096]{1,0:T(8,128)(2,1)S(1)} %collective-permute-done.11.near_ref), channel_id=1, source_target_pairs={{0,16},{16,32},{32,48},{48,0},{64,112},{80,64},{96,80},{112,96},{1... | collective-permute-start | bytes 1572872 | tf_op jit(solution)/shard_map/ppermute | solution.py:34
  79.6 1.9 %shard_map.57 = f32[128,1024]{1,0:T(8,128)S(1)} custom-call(s32[2]{0:T(128)S(1)} %pad_add_fusion.place_ref, bf16[64,4096]{1,0:T(8,128)(2,1)S(1)} %collective-permute-done.11.near_ref, bf16[64,4096]{1,0:T(8,128)(2,1)S(1)} %collective-permute-done.4.far_ref, bf16[4096,1024]{1,0:T(8,128)(2,1)S(1)} %shard_map.55.held_ref), custom_call_target="tpu_custom_call" | custom-call | flops 1073741824 | bytes 8388608 | tf_op jit(solution)/shard_map/pallas_call | solution.py:145
  81.5 2.5 %collective-permute-start.12 = (f32[128,1024]{1,0:T(8,128)S(1)}, f32[128,1024]{1,0:T(8,128)S(1)}, u32[]{:S(2)}, u32[]{:S(2)}) collective-permute-start(f32[128,1024]{1,0:T(8,128)S(1)} %shard_map.57), channel_id=1, source_target_pairs={{0,256},{16,16},{32,160},{48,432},{64,448},{80,208},{96,96},{112,3... | collective-permute-start | bytes 1572872 | tf_op jit(solution)/shard_map/ppermute | solution.py:65
  83.9 0.0 collective-permute-done.13.near_ref
  84.0 1.9 %shard_map.58 = f32[128,1024]{1,0:T(8,128)S(1)} custom-call(s32[2]{0:T(128)S(1)} %pad_add_fusion.place_ref, bf16[64,4096]{1,0:T(8,128)(2,1)S(1)} %collective-permute-done.13.near_ref, bf16[64,4096]{1,0:T(8,128)(2,1)S(1)} %collective-permute-done.5.far_ref, bf16[4096,1024]{1,0:T(8,128)(2,1)S(1)} %shard_map.55.held_ref), custom_call_target="tpu_custom_call" | custom-call | flops 1073741824 | bytes 8388608 | tf_op jit(solution)/shard_map/pallas_call | solution.py:145
  85.8 0.7 collective-permute-start.14
  86.5 0.0 collective-permute-done.9.far_ref
  86.5 0.0 collective-permute-done.10
  86.6 1.3 %collective-permute-done.15.near_ref = bf16[64,4096]{1,0:T(8,128)(2,1)S(1)} collective-permute-done((bf16[64,4096]{1,0:T(8,128)(2,1)S(1)}, bf16[64,4096]{1,0:T(8,128)(2,1)S(1)}, u32[]{:S(2)}, u32[]{:S(2)}) %collective-permute-start.15) | collective-permute-done | bytes 524320 | tf_op jit(solution)/shard_map/ppermute | solution.py:34
  87.9 1.9 %shard_map.59 = f32[128,1024]{1,0:T(8,128)S(1)} custom-call(s32[2]{0:T(128)S(1)} %pad_add_fusion.place_ref, bf16[64,4096]{1,0:T(8,128)(2,1)S(1)} %collective-permute-done.15.near_ref, bf16[64,4096]{1,0:T(8,128)(2,1)S(1)} %collective-permute-done.9.far_ref, bf16[4096,1024]{1,0:T(8,128)(2,1)S(1)} %shard_map.55.held_ref), custom_call_target="tpu_custom_call" | custom-call | flops 1073741824 | bytes 8388608 | tf_op jit(solution)/shard_map/pallas_call | solution.py:145
  89.8 1.9 %collective-permute-start.16 = (f32[128,1024]{1,0:T(8,128)S(1)}, f32[128,1024]{1,0:T(8,128)S(1)}, u32[]{:S(2)}, u32[]{:S(2)}) collective-permute-start(f32[128,1024]{1,0:T(8,128)S(1)} %shard_map.59), channel_id=1, source_target_pairs={{0,384},{16,272},{32,32},{48,176},{64,192},{80,80},{96,352},{112,4... | collective-permute-start | bytes 1572872 | tf_op jit(solution)/shard_map/ppermute | solution.py:65
  91.7 3.8 %collective-permute-done.12 = f32[128,1024]{1,0:T(8,128)S(1)} collective-permute-done((f32[128,1024]{1,0:T(8,128)S(1)}, f32[128,1024]{1,0:T(8,128)S(1)}, u32[]{:S(2)}, u32[]{:S(2)}) %collective-permute-start.12) | collective-permute-done | bytes 524320 | tf_op jit(solution)/shard_map/ppermute | solution.py:65
  95.5 0.0 collective-permute-done.14
  95.5 11.4 %collective-permute-done.16 = f32[128,1024]{1,0:T(8,128)S(1)} collective-permute-done((f32[128,1024]{1,0:T(8,128)S(1)}, f32[128,1024]{1,0:T(8,128)S(1)}, u32[]{:S(2)}, u32[]{:S(2)}) %collective-permute-start.16) | collective-permute-done | bytes 524320 | tf_op jit(solution)/shard_map/ppermute | solution.py:65
  107.0 0.9 add_add_fusion
  (6 shorter events, 0.1 us)
Async XLA Ops:
  0.0 9.9 %collective-permute-start = (bf16[16,2048]{1,0:T(8,128)(2,1)}, bf16[16,2048]{1,0:T(8,128)(2,1)S(1)}, u32[]{:S(2)}, u32[]{:S(2)}) collective-permute-start(bf16[16,2048]{1,0:T(8,128)(2,1)} %param.5), channel_id=1, source_target_pairs={{0,64},{64,0},{1,65},{65,1},{2,66},{66,2},{3,67},{67,3},{4,68},{68... | collective-permute-start | bytes 196616 | tf_op jit(solution)/shard_map/ppermute | solution.py:161
  9.9 52.3 %collective-permute-start.8 = (bf16[2048,1024]{1,0:T(8,128)(2,1)}, bf16[2048,1024]{1,0:T(8,128)(2,1)}, u32[]{:S(2)}, u32[]{:S(2)}) collective-permute-start(bf16[2048,1024]{1,0:T(8,128)(2,1)} %own_ref), channel_id=1, source_target_pairs={{0,64},{64,0},{1,65},{65,1},{2,66},{66,2},{3,67},{67,3},{4,68},{68... | collective-permute-start | bytes 12582920 | tf_op jit(solution)/shard_map/ppermute | solution.py:164
  13.0 15.4 %collective-permute-start.2 = (bf16[16,4096]{1,0:T(8,128)(2,1)S(1)}, bf16[16,4096]{1,0:T(8,128)(2,1)S(1)}, u32[]{:S(2)}, u32[]{:S(2)}) collective-permute-start(bf16[16,4096]{1,0:T(8,128)(2,1)S(1)} %constant_dynamic-update-slice_fusion), channel_id=1, source_target_pairs={{4,0},{5,1},{6,2},{7,3},{0,4},{1,5},{2,6},{3,7},{68,8},{69,9},{70,... | collective-permute-start | bytes 393224 | tf_op jit(solution)/shard_map/ppermute | solution.py:55
  20.1 17.6 %collective-permute-start.1 = (bf16[16,4096]{1,0:T(8,128)(2,1)S(1)}, bf16[16,4096]{1,0:T(8,128)(2,1)S(1)}, u32[]{:S(2)}, u32[]{:S(2)}) collective-permute-start(bf16[16,4096]{1,0:T(8,128)(2,1)S(1)} %constant_dynamic-update-slice_fusion), channel_id=1, source_target_pairs={{0,0},{1,1},{2,2},{3,3},{4,4},{5,5},{6,6},{7,7},{64,8},{65,9},{66,... | collective-permute-start | bytes 393224 | tf_op jit(solution)/shard_map/ppermute | solution.py:55
  37.8 8.2 %collective-permute-start.3 = (bf16[32,4096]{1,0:T(8,128)(2,1)S(1)}, bf16[32,4096]{1,0:T(8,128)(2,1)S(1)}, u32[]{:S(2)}, u32[]{:S(2)}) collective-permute-start(bf16[32,4096]{1,0:T(8,128)(2,1)S(1)} %get-tuple-element.28), channel_id=1, source_target_pairs={{0,1},{1,2},{2,3},{3,4},{4,5},{5,6},{6,7},{7,8},{8,9},{9,10},{10,1... | collective-permute-start | bytes 786440 | tf_op jit(solution)/shard_map/ppermute | solution.py:34
  39.7 12.7 %collective-permute-start.6 = (bf16[32,4096]{1,0:T(8,128)(2,1)S(1)}, bf16[32,4096]{1,0:T(8,128)(2,1)S(1)}, u32[]{:S(2)}, u32[]{:S(2)}) collective-permute-start(bf16[32,4096]{1,0:T(8,128)(2,1)S(1)} %get-tuple-element.28), channel_id=1, source_target_pairs={{0,15},{1,0},{2,1},{3,2},{4,3},{5,4},{6,5},{7,6},{8,7},{9,8},{10,9... | collective-permute-start | bytes 786440 | tf_op jit(solution)/shard_map/ppermute | solution.py:34
  44.1 12.2 %collective-permute-start.7 = (bf16[32,4096]{1,0:T(8,128)(2,1)S(1)}, bf16[32,4096]{1,0:T(8,128)(2,1)S(1)}, u32[]{:S(2)}, u32[]{:S(2)}) collective-permute-start(bf16[32,4096]{1,0:T(8,128)(2,1)S(1)} %get-tuple-element.28), channel_id=1, source_target_pairs={{0,2},{1,3},{2,4},{3,5},{4,6},{5,7},{6,8},{7,9},{8,10},{9,11},{10,... | collective-permute-start | bytes 786440 | tf_op jit(solution)/shard_map/ppermute | solution.py:34
  46.1 22.3 %collective-permute-start.4 = (bf16[64,4096]{1,0:T(8,128)(2,1)S(1)}, bf16[64,4096]{1,0:T(8,128)(2,1)S(1)}, u32[]{:S(2)}, u32[]{:S(2)}) collective-permute-start(bf16[64,4096]{1,0:T(8,128)(2,1)S(1)} %constant_dynamic-update-slice_fusion.4.far_ref), channel_id=1, source_target_pairs={{0,16},{16,32},{32,48},{48,0},{64,112},{80,64},{96,80},{112,96},{1... | collective-permute-start | bytes 1572872 | tf_op jit(solution)/shard_map/ppermute | solution.py:34
  50.2 18.2 %collective-permute-start.5 = (bf16[64,4096]{1,0:T(8,128)(2,1)S(1)}, bf16[64,4096]{1,0:T(8,128)(2,1)S(1)}, u32[]{:S(2)}, u32[]{:S(2)}) collective-permute-start(bf16[64,4096]{1,0:T(8,128)(2,1)S(1)} %constant_dynamic-update-slice_fusion.4.far_ref), channel_id=1, source_target_pairs={{0,48},{16,0},{32,16},{48,32},{64,80},{80,96},{96,112},{112,64},{1... | collective-permute-start | bytes 1572872 | tf_op jit(solution)/shard_map/ppermute | solution.py:34
  56.3 21.3 %collective-permute-start.11 = (bf16[64,4096]{1,0:T(8,128)(2,1)S(1)}, bf16[64,4096]{1,0:T(8,128)(2,1)S(1)}, u32[]{:S(2)}, u32[]{:S(2)}) collective-permute-start(bf16[64,4096]{1,0:T(8,128)(2,1)S(1)} %constant_dynamic-update-slice_fusion.7.near_ref), channel_id=1, source_target_pairs={{0,16},{16,32},{32,48},{48,0},{64,112},{80,64},{96,80},{112,96},{1... | collective-permute-start | bytes 1572872 | tf_op jit(solution)/shard_map/ppermute | solution.py:34
  60.3 23.7 %collective-permute-start.13 = (bf16[64,4096]{1,0:T(8,128)(2,1)S(1)}, bf16[64,4096]{1,0:T(8,128)(2,1)S(1)}, u32[]{:S(2)}, u32[]{:S(2)}) collective-permute-start(bf16[64,4096]{1,0:T(8,128)(2,1)S(1)} %constant_dynamic-update-slice_fusion.7.near_ref), channel_id=1, source_target_pairs={{0,48},{16,0},{32,16},{48,32},{64,80},{80,96},{96,112},{112,64},{1... | collective-permute-start | bytes 1572872 | tf_op jit(solution)/shard_map/ppermute | solution.py:34
  68.4 18.2 %collective-permute-start.9 = (bf16[64,4096]{1,0:T(8,128)(2,1)S(1)}, bf16[64,4096]{1,0:T(8,128)(2,1)S(1)}, u32[]{:S(2)}, u32[]{:S(2)}) collective-permute-start(bf16[64,4096]{1,0:T(8,128)(2,1)S(1)} %collective-permute-done.4.far_ref), channel_id=1, source_target_pairs={{0,16},{16,32},{32,48},{48,0},{64,112},{80,64},{96,80},{112,96},{1... | collective-permute-start | bytes 1572872 | tf_op jit(solution)/shard_map/ppermute | solution.py:34
  73.0 13.6 %collective-permute-start.10 = (f32[128,1024]{1,0:T(8,128)S(1)}, f32[128,1024]{1,0:T(8,128)S(1)}, u32[]{:S(2)}, u32[]{:S(2)}) collective-permute-start(f32[128,1024]{1,0:T(8,128)S(1)} %shard_map.56), channel_id=1, source_target_pairs={{0,0},{16,144},{32,416},{48,304},{64,320},{80,464},{96,224},{112,1... | collective-permute-start | bytes 1572872 | tf_op jit(solution)/shard_map/ppermute | solution.py:65
  77.6 10.2 %collective-permute-start.15 = (bf16[64,4096]{1,0:T(8,128)(2,1)S(1)}, bf16[64,4096]{1,0:T(8,128)(2,1)S(1)}, u32[]{:S(2)}, u32[]{:S(2)}) collective-permute-start(bf16[64,4096]{1,0:T(8,128)(2,1)S(1)} %collective-permute-done.11.near_ref), channel_id=1, source_target_pairs={{0,16},{16,32},{32,48},{48,0},{64,112},{80,64},{96,80},{112,96},{1... | collective-permute-start | bytes 1572872 | tf_op jit(solution)/shard_map/ppermute | solution.py:34
  81.5 14.1 %collective-permute-start.12 = (f32[128,1024]{1,0:T(8,128)S(1)}, f32[128,1024]{1,0:T(8,128)S(1)}, u32[]{:S(2)}, u32[]{:S(2)}) collective-permute-start(f32[128,1024]{1,0:T(8,128)S(1)} %shard_map.57), channel_id=1, source_target_pairs={{0,256},{16,16},{32,160},{48,432},{64,448},{80,208},{96,96},{112,3... | collective-permute-start | bytes 1572872 | tf_op jit(solution)/shard_map/ppermute | solution.py:65
  85.8 9.7 %collective-permute-start.14 = (f32[128,1024]{1,0:T(8,128)S(1)}, f32[128,1024]{1,0:T(8,128)S(1)}, u32[]{:S(2)}, u32[]{:S(2)}) collective-permute-start(f32[128,1024]{1,0:T(8,128)S(1)} %shard_map.58), channel_id=1, source_target_pairs={{0,128},{16,400},{32,288},{48,48},{64,64},{80,336},{96,480},{112,2... | collective-permute-start | bytes 1572872 | tf_op jit(solution)/shard_map/ppermute | solution.py:65
  89.8 17.2 %collective-permute-start.16 = (f32[128,1024]{1,0:T(8,128)S(1)}, f32[128,1024]{1,0:T(8,128)S(1)}, u32[]{:S(2)}, u32[]{:S(2)}) collective-permute-start(f32[128,1024]{1,0:T(8,128)S(1)} %shard_map.59), channel_id=1, source_target_pairs={{0,384},{16,272},{32,32},{48,176},{64,192},{80,80},{96,352},{112,4... | collective-permute-start | bytes 1572872 | tf_op jit(solution)/shard_map/ppermute | solution.py:65

commit v5 on v4

--- a/solution.py
+++ b/solution.py
@@ -65,78 +65,100 @@
     return lax.ppermute(value, ("y", "core", "x"), pairs)
 
 
-def hold_kernel(place_ref, row_ref, col_ref, own_ref, other_ref, held_ref, sem):
+def origins_of(place_ref):
+    step = 2 * place_ref[0] - 1
+    return [lax.rem(place_ref[1] + k * step + Z, Z) for k in (2, -1, 0, 1)]
+
+
+def columns(origins, near_ref, far_ref, half, first, width):
+    depth, pieces = near_ref.shape[1] // CORE, []
+    rows = near_ref.shape[0] // 2
+    for index, origin in enumerate(origins):
+        ref, top = (near_ref, far_ref)[index // 2], index % 2 * rows
+        at = pl.multiple_of(lax.rem(origin // HALF + half, CORE) * depth + first, width)
+        pieces.append(ref[top : top + rows, pl.ds(at, width)])
+    return jnp.concatenate(pieces)
+
+
+def place_rows(origins, out_ref, part, value):
+    rows = out_ref.shape[0] // HALF
+    for index in range(HALF):
+        at = lax.rem(origins[index // 2] + index % 2 * 4, HALF) * rows
+        out_ref[pl.ds(pl.multiple_of(at, rows), rows), part] = value[
+            index * rows : (index + 1) * rows
+        ]
+
+
+def first_kernel(
+    place_ref, row_ref, col_ref, own_ref, other_ref, near_ref, far_ref, held_ref, out_ref, sum_ref, sem
+):
     core, (depth, cols) = place_ref[0], own_ref.shape
-    chunk = depth // CHUNKS
+    chunk, tile = depth // CHUNKS, 16
     copies = []
-    for index, ref in ((core, own_ref), (1 - core, other_ref)):
+    for half, ref in ((core, own_ref), (1 - core, other_ref)):
         for part in range(CHUNKS):
-            first = pl.multiple_of(index * depth + part * chunk, chunk)
+            first = pl.multiple_of(half * depth + part * chunk, chunk)
             copy = pltpu.make_async_copy(
                 ref.at[pl.ds(part * chunk, chunk)],
                 held_ref.at[pl.ds(first, chunk)],
                 sem.at[len(copies)],
             )
             copy.start()
-            copies.append((copy, first))
-    tile = 16
+            copies.append((copy, first, half, part))
     col = jnp.broadcast_to(col_ref[...].astype(jnp.float32), (tile, cols)).astype(jnp.bfloat16)
     zero = jnp.zeros((), held_ref.dtype)
-    for copy, first in copies:
+    origins = origins_of(place_ref)
+    for copy, first, half, part in copies:
         copy.wait()
         for unit in range(chunk // UNIT):
             label = row_ref[first // UNIT + unit].astype(jnp.float32)
             keep = col == jnp.full((tile, cols), label, jnp.float32).astype(jnp.bfloat16)
-            for part in range(UNIT // tile):
-                rows = pl.ds(pl.multiple_of(first + unit * UNIT + part * tile, tile), tile)
+            for strip in range(UNIT // tile):
+                rows = pl.ds(pl.multiple_of(first + unit * UNIT + strip * tile, tile), tile)
                 held_ref[rows, :] = jnp.where(keep, held_ref[rows, :], zero)
-
-
-def hold(place, rows, columns, own, other):
+        block = columns(origins, near_ref, far_ref, half, part * chunk, chunk)
+        value = jnp.dot(block, held_ref[pl.ds(first, chunk), :], preferred_element_type=jnp.float32)
+        if copy is copies[0][0]:
+            sum_ref[...] = value
+        else:
+            sum_ref[...] += value
+    place_rows(origins, out_ref, slice(None), sum_ref[...])
+
+
+def first_product(place, rows, columns, own, other, near, far):
     depth, cols = own.shape
+    height = 2 * near.shape[0]
     vmem, smem = (pl.BlockSpec(memory_space=m) for m in (pltpu.VMEM, pltpu.SMEM))
     own, other = (pltpu.with_memory_space_constraint(v, pltpu.HBM) for v in (own, other))
     return pl.pallas_call(
-        hold_kernel,
-        out_shape=pltpu.VMEM((CORE * depth, cols), own.dtype),
-        in_specs=[smem, smem, vmem]
-        + [pl.BlockSpec(memory_space=pltpu.HBM)] * 2,
-        out_specs=vmem,
-        scratch_shapes=[pltpu.SemaphoreType.DMA((CORE * CHUNKS,))],
-        compiler_params=pltpu.CompilerParams(vmem_limit_bytes=12 * 2**20),
+        first_kernel,
+        out_shape=(
+            pltpu.VMEM((CORE * depth, cols), own.dtype),
+            jax.ShapeDtypeStruct((height, cols), jnp.float32),
+        ),
+        in_specs=[smem, smem, vmem] + [pl.BlockSpec(memory_space=pltpu.HBM)] * 2 + [vmem] * 2,
+        out_specs=(vmem, vmem),
+        scratch_shapes=[
+            pltpu.VMEM((height, cols), jnp.float32),
+            pltpu.SemaphoreType.DMA((CORE * CHUNKS,)),
+        ],
+        compiler_params=pltpu.CompilerParams(vmem_limit_bytes=14 * 2**20),
         cost_estimate=pl.CostEstimate(
-            flops=0, bytes_accessed=4 * CORE * depth * cols, transcendentals=0
+            flops=2 * height * CORE * own.size, bytes_accessed=4 * CORE * own.size, transcendentals=0
         ),
-    )(place, rows, columns, own, other)
+    )(place, rows, columns, own, other, near, far)
 
 
 def product_kernel(place_ref, near_ref, far_ref, held_ref, out_ref):
-    core, z, cols = place_ref[0], place_ref[1], held_ref.shape[1]
-    rows, depth = out_ref.shape[0] // HALF, held_ref.shape[0] // CORE
-    step = 2 * core - 1
-    origins = [lax.rem(z + k * step + Z, Z) for k in (-1, 2, 0, 1)]
-
-    def columns(half):
-        pieces = []
-        for index, origin in enumerate(origins):
-            ref, first = (near_ref, far_ref)[index // 2], index % 2 * 2 * rows
-            swapped = origin // HALF
-            at = pl.multiple_of((swapped if half == 0 else 1 - swapped) * depth, depth)
-            pieces.append(ref[first : first + 2 * rows, pl.ds(at, depth)])
-        return jnp.concatenate(pieces)
-
-    left, right = columns(0), columns(1)
-    sources = [origin + half for origin in origins for half in (0, 4)]
+    cols, depth = held_ref.shape[1], held_ref.shape[0] // CORE
+    origins = origins_of(place_ref)
+    left, right = (columns(origins, near_ref, far_ref, half, 0, depth) for half in range(CORE))
     width = min(256, cols)
     for first in range(0, cols, width):
         part = slice(first, first + width)
         value = jnp.dot(left, held_ref[:depth, part], preferred_element_type=jnp.float32)
         value += jnp.dot(right, held_ref[depth:, part], preferred_element_type=jnp.float32)
-        for index, source in enumerate(sources):
-            at = lax.rem(source, HALF) * rows
-            out_ref[pl.ds(pl.multiple_of(at, rows), rows), part] = value[
-                index * rows : (index + 1) * rows
-            ]
+        place_rows(origins, out_ref, part, value)
 
 
 def product(place, near, far, held):
@@ -159,8 +181,9 @@
     swap = [(0, 1), (1, 0)]
 
     other = lax.ppermute(amplitudes, "core", swap)
-    other, integrals = lax.optimization_barrier((other, integrals))
-    both = jnp.concatenate([amplitudes, other], axis=1)
+    both = jnp.pad(amplitudes, ((0, 0), (0, amplitudes.shape[1])))
+    both, other, integrals = lax.optimization_barrier((both, other, integrals))
+    both = lax.dynamic_update_slice_in_dim(both, other, amplitudes.shape[1], 1)
     other = lax.ppermute(integrals, "core", swap)
 
     first = spread(both, 0)
@@ -174,14 +197,13 @@
     away = apart(here, "z", Z, 2)
     far = jnp.concatenate([here, back])
     ahead = apart(here, "z", Z, -1)
-    near = jnp.concatenate([ahead, away])
+    near = jnp.concatenate([away, ahead])
 
     near_back, near_ahead = apart(near, "x", X, 1), apart(near, "x", X, -1)
     far_back, far_ahead = apart(far, "x", X, 1), apart(far, "x", X, -1)
     near_away = apart(near_back, "x", X, 1)
     near, integrals = lax.optimization_barrier((near, integrals))
-    held = hold(place, *labels, integrals, other)
-    own = product(place, near, far, held)
+    held, own = first_product(place, *labels, integrals, other, near, far)
     received = [hand_in(own, 0)]
     far_back, far_ahead, own = lax.optimization_barrier((far_back, far_ahead, own))
     far_away = apart(far_back, "x", X, 1)

time: 109 us -> 104 us (0.954)
  waiting for transfers between devices: 31.3 us -> 23.8 us
  starting transfers between devices: 60.1 us -> 63.9 us
    ppermute x9, waiting for transfers between devices: 5.53 us -> 1.06 us  [apart(): return lax.ppermute(value, ('core', axis), pairs)]
    ppermute x4, starting transfers between devices: 9.76 us -> 12.1 us  [hand_in(): return lax.ppermute(value, ('y', 'core', 'x'), pairs)]
    ppermute x4, waiting for transfers between devices: 15.3 us -> 13.1 us  [hand_in(): return lax.ppermute(value, ('y', 'core', 'x'), pairs)]
    pallas_call x4 -> x3, Pallas kernels: 7.52 us -> 5.62 us  [product(): pl.pallas_call(product_kernel, out_shape=jax.ShapeDtypeStruct((rows, cols...]
    ppermute x9, starting transfers between devices: 26.4 us -> 27.8 us  [apart(): return lax.ppermute(value, ('core', axis), pairs)]
    pallas_call x1, Pallas kernels: 4.27 us -> 5.54 us  [first_product(): pl.pallas_call(first_kernel, out_shape=(pltpu.VMEM((CORE * depth, cols),...]
  transfers between devices with their start and end apart: 17 -> 17, of which waited for: 7 -> 6; matrix products, arithmetic and copies ran while one was open for 3% -> 3% of each run, Pallas kernels for 11% -> 11%
where the time goes in v5:
time: 104 us
  starting transfers between devices  63.9 us (61%)
  waiting for transfers between devices  23.8 us (23%)
  Pallas kernels  11.2 us (11%)
  local copies, waits for them, and re-layouts  2.52 us (2%)
  other arithmetic  1.93 us (2%)
    ppermute x9, starting transfers between devices, apart(): return lax.ppermute(value, ('core', axis), pairs)  27.8 us
    ppermute x4, waiting for transfers between devices, hand_in(): return lax.ppermute(value, ('y', 'core', 'x'), pairs)  13.1 us
    ppermute x2, starting transfers between devices, spread(): return lax.ppermute(value, ('y', 'core', 'x', 'z'), pairs)  12.9 us
    ppermute x4, starting transfers between devices, hand_in(): return lax.ppermute(value, ('y', 'core', 'x'), pairs)  12.1 us
    ppermute x2, waiting for transfers between devices, spread(): return lax.ppermute(value, ('y', 'core', 'x', 'z'), pairs)  9.38 us
    ppermute x1, starting transfers between devices, body(): other = lax.ppermute(amplitudes, 'core', swap)  8.77 us
    pallas_call x3, Pallas kernels, product(): pl.pallas_call(product_kernel, out_shape=jax.ShapeDtypeStruct((rows, cols...  5.62 us
    pallas_call x1, Pallas kernels, first_product(): pl.pallas_call(first_kernel, out_shape=(pltpu.VMEM((CORE * depth, cols),...  5.54 us
  transfers between devices with their start and end apart: 17, of which 6 were waited for; matrix products, arithmetic and copies ran while one was open for 3% of the time, Pallas kernels for 11%

profile of v5, /device:TPU:1, one launch (start us, length us, event | category | flops | bytes accessed | tf_op | source)
XLA Modules:
  0.0 103.6 jit_solution(12248851215084942152)
XLA Ops:
  0.0 8.8 %collective-permute-start = (bf16[16,2048]{1,0:T(8,128)(2,1)}, bf16[16,2048]{1,0:T(8,128)(2,1)S(1)}, u32[]{:S(2)}, u32[]{:S(2)}) collective-permute-start(bf16[16,2048]{1,0:T(8,128)(2,1)} %param.5), channel_id=1, source_target_pairs={{0,64},{64,0},{1,65},{65,1},{2,66},{66,2},{3,67},{67,3},{4,68},{68... | collective-permute-start | bytes 196616 | tf_op jit(solution)/shard_map/ppermute | solution.py:183
  8.8 0.9 pad.4
  9.6 0.2 collective-permute-done
  9.9 2.3 %collective-permute-start.8 = (bf16[2048,1024]{1,0:T(8,128)(2,1)}, bf16[2048,1024]{1,0:T(8,128)(2,1)}, u32[]{:S(2)}, u32[]{:S(2)}) collective-permute-start(bf16[2048,1024]{1,0:T(8,128)(2,1)} %own_ref), channel_id=1, source_target_pairs={{0,64},{64,0},{1,65},{65,1},{2,66},{66,2},{3,67},{67,3},{4,68},{68... | collective-permute-start | bytes 12582920 | tf_op jit(solution)/shard_map/ppermute | solution.py:187
  12.1 7.1 %collective-permute-start.2 = (bf16[16,4096]{1,0:T(8,128)(2,1)S(1)}, bf16[16,4096]{1,0:T(8,128)(2,1)S(1)}, u32[]{:S(2)}, u32[]{:S(2)}) collective-permute-start(bf16[16,4096]{1,0:T(8,128)(2,1)S(1)} %constant_dynamic-update-slice_fusion.7), channel_id=1, source_target_pairs={{4,0},{5,1},{6,2},{7,3},{0,4},{1,5},{2,6},{3,7},{68,8},{69,9},{70,... | collective-permute-start | bytes 393224 | tf_op jit(solution)/shard_map/ppermute | solution.py:55
  19.3 5.8 %collective-permute-start.1 = (bf16[16,4096]{1,0:T(8,128)(2,1)S(1)}, bf16[16,4096]{1,0:T(8,128)(2,1)S(1)}, u32[]{:S(2)}, u32[]{:S(2)}) collective-permute-start(bf16[16,4096]{1,0:T(8,128)(2,1)S(1)} %constant_dynamic-update-slice_fusion.7), channel_id=1, source_target_pairs={{0,0},{1,1},{2,2},{3,3},{4,4},{5,5},{6,6},{7,7},{64,8},{65,9},{66,... | collective-permute-start | bytes 393224 | tf_op jit(solution)/shard_map/ppermute | solution.py:55
  25.1 0.8 multiply_reduce_fusion
  25.9 0.7 dynamic_slice.6
  26.6 0.1 slice.3
  26.8 0.7 dynamic_slice.7
  27.5 0.1 select_reduce_fusion.row_ref
  27.5 0.0 collective-permute-done.2
  27.5 9.4 %collective-permute-done.1 = bf16[16,4096]{1,0:T(8,128)(2,1)S(1)} collective-permute-done((bf16[16,4096]{1,0:T(8,128)(2,1)S(1)}, bf16[16,4096]{1,0:T(8,128)(2,1)S(1)}, u32[]{:S(2)}, u32[]{:S(2)}) %collective-permute-start.1) | collective-permute-done | bytes 131104 | tf_op jit(solution)/shard_map/ppermute | solution.py:55
  37.0 1.9 %collective-permute-start.3 = (bf16[32,4096]{1,0:T(8,128)(2,1)S(1)}, bf16[32,4096]{1,0:T(8,128)(2,1)S(1)}, u32[]{:S(2)}, u32[]{:S(2)}) collective-permute-start(bf16[32,4096]{1,0:T(8,128)(2,1)S(1)} %get-tuple-element.34), channel_id=1, source_target_pairs={{0,1},{1,2},{2,3},{3,4},{4,5},{5,6},{6,7},{7,8},{8,9},{9,10},{10,1... | collective-permute-start | bytes 786440 | tf_op jit(solution)/shard_map/ppermute | solution.py:34
  38.9 1.9 %collective-permute-start.6 = (bf16[32,4096]{1,0:T(8,128)(2,1)S(1)}, bf16[32,4096]{1,0:T(8,128)(2,1)S(1)}, u32[]{:S(2)}, u32[]{:S(2)}) collective-permute-start(bf16[32,4096]{1,0:T(8,128)(2,1)S(1)} %get-tuple-element.34), channel_id=1, source_target_pairs={{0,2},{1,3},{2,4},{3,5},{4,6},{5,7},{6,8},{7,9},{8,10},{9,11},{10,... | collective-permute-start | bytes 786440 | tf_op jit(solution)/shard_map/ppermute | solution.py:34
  40.8 4.2 %collective-permute-start.7 = (bf16[32,4096]{1,0:T(8,128)(2,1)S(1)}, bf16[32,4096]{1,0:T(8,128)(2,1)S(1)}, u32[]{:S(2)}, u32[]{:S(2)}) collective-permute-start(bf16[32,4096]{1,0:T(8,128)(2,1)S(1)} %get-tuple-element.34), channel_id=1, source_target_pairs={{0,15},{1,0},{2,1},{3,2},{4,3},{5,4},{6,5},{7,6},{8,7},{9,8},{10,9... | collective-permute-start | bytes 786440 | tf_op jit(solution)/shard_map/ppermute | solution.py:34
  45.0 0.0 collective-permute-done.3
  45.1 4.2 %collective-permute-start.4 = (bf16[64,4096]{1,0:T(8,128)(2,1)S(1)}, bf16[64,4096]{1,0:T(8,128)(2,1)S(1)}, u32[]{:S(2)}, u32[]{:S(2)}) collective-permute-start(bf16[64,4096]{1,0:T(8,128)(2,1)S(1)} %constant_dynamic-update-slice_fusion.2.far_ref), channel_id=1, source_target_pairs={{0,16},{16,32},{32,48},{48,0},{64,112},{80,64},{96,80},{112,96},{1... | collective-permute-start | bytes 1572872 | tf_op jit(solution)/shard_map/ppermute | solution.py:34
  49.3 1.9 %collective-permute-start.5 = (bf16[64,4096]{1,0:T(8,128)(2,1)S(1)}, bf16[64,4096]{1,0:T(8,128)(2,1)S(1)}, u32[]{:S(2)}, u32[]{:S(2)}) collective-permute-start(bf16[64,4096]{1,0:T(8,128)(2,1)S(1)} %constant_dynamic-update-slice_fusion.2.far_ref), channel_id=1, source_target_pairs={{0,48},{16,0},{32,16},{48,32},{64,80},{80,96},{96,112},{112,64},{1... | collective-permute-start | bytes 1572872 | tf_op jit(solution)/shard_map/ppermute | solution.py:34
  51.2 0.7 collective-permute-done.6
  51.9 0.4 collective-permute-done.7
  52.3 4.8 %collective-permute-start.11 = (bf16[64,4096]{1,0:T(8,128)(2,1)S(1)}, bf16[64,4096]{1,0:T(8,128)(2,1)S(1)}, u32[]{:S(2)}, u32[]{:S(2)}) collective-permute-start(bf16[64,4096]{1,0:T(8,128)(2,1)S(1)} %constant_dynamic-update-slice_fusion.5.near_ref), channel_id=1, source_target_pairs={{0,16},{16,32},{32,48},{48,0},{64,112},{80,64},{96,80},{112,96},{1... | collective-permute-start | bytes 1572872 | tf_op jit(solution)/shard_map/ppermute | solution.py:34
  57.1 0.1 pad_add_fusion.place_ref
  57.2 1.9 %collective-permute-start.13 = (bf16[64,4096]{1,0:T(8,128)(2,1)S(1)}, bf16[64,4096]{1,0:T(8,128)(2,1)S(1)}, u32[]{:S(2)}, u32[]{:S(2)}) collective-permute-start(bf16[64,4096]{1,0:T(8,128)(2,1)S(1)} %constant_dynamic-update-slice_fusion.5.near_ref), channel_id=1, source_target_pairs={{0,48},{16,0},{32,16},{48,32},{64,80},{80,96},{96,112},{112,64},{1... | collective-permute-start | bytes 1572872 | tf_op jit(solution)/shard_map/ppermute | solution.py:34
  59.1 0.0 collective-permute-done.8.other_ref
  59.1 5.5 %shard_map.55 = (bf16[4096,1024]{1,0:T(8,128)(2,1)S(1)}, f32[128,1024]{1,0:T(8,128)S(1)}) custom-call(s32[2]{0:T(128)S(1)} %pad_add_fusion.place_ref, s32[64]{0:T(128)S(1)} %select_reduce_fusion.row_ref, s32[1,1024]{1,0:T(1,128)S(1)} %bitcast.3, bf16[2048,1024]{1,0:T(8,128)(2,1)} %own_ref, bf16[2048,1024]{1,0:T(8,128)(2,1)} %collective-permute-done.8.other_ref, ...), custom_call_target="tpu_custom_call" | custom-call | flops 1073741824 | bytes 16777216 | tf_op jit(solution)/shard_map/pallas_call | solution.py:133
  64.6 0.0 collective-permute-done.4.far_ref
  64.6 0.0 collective-permute-done.5.far_ref
  64.7 4.5 %collective-permute-start.9 = (bf16[64,4096]{1,0:T(8,128)(2,1)S(1)}, bf16[64,4096]{1,0:T(8,128)(2,1)S(1)}, u32[]{:S(2)}, u32[]{:S(2)}) collective-permute-start(bf16[64,4096]{1,0:T(8,128)(2,1)S(1)} %collective-permute-done.4.far_ref), channel_id=1, source_target_pairs={{0,16},{16,32},{32,48},{48,0},{64,112},{80,64},{96,80},{112,96},{1... | collective-permute-start | bytes 1572872 | tf_op jit(solution)/shard_map/ppermute | solution.py:34
  69.2 4.2 %collective-permute-start.10 = (f32[128,1024]{1,0:T(8,128)S(1)}, f32[128,1024]{1,0:T(8,128)S(1)}, u32[]{:S(2)}, u32[]{:S(2)}) collective-permute-start(f32[128,1024]{1,0:T(8,128)S(1)} %get-tuple-element.27), channel_id=1, source_target_pairs={{0,0},{16,144},{32,416},{48,304},{64,320},{80,464},{96,224},{112,1... | collective-permute-start | bytes 1572872 | tf_op jit(solution)/shard_map/ppermute | solution.py:65
  73.4 0.0 collective-permute-done.11.near_ref
  73.5 2.5 %collective-permute-start.15 = (bf16[64,4096]{1,0:T(8,128)(2,1)S(1)}, bf16[64,4096]{1,0:T(8,128)(2,1)S(1)}, u32[]{:S(2)}, u32[]{:S(2)}) collective-permute-start(bf16[64,4096]{1,0:T(8,128)(2,1)S(1)} %collective-permute-done.11.near_ref), channel_id=1, source_target_pairs={{0,16},{16,32},{32,48},{48,0},{64,112},{80,64},{96,80},{112,96},{1... | collective-permute-start | bytes 1572872 | tf_op jit(solution)/shard_map/ppermute | solution.py:34
  75.9 1.9 %shard_map.56 = f32[128,1024]{1,0:T(8,128)S(1)} custom-call(s32[2]{0:T(128)S(1)} %pad_add_fusion.place_ref, bf16[64,4096]{1,0:T(8,128)(2,1)S(1)} %collective-permute-done.11.near_ref, bf16[64,4096]{1,0:T(8,128)(2,1)S(1)} %collective-permute-done.4.far_ref, bf16[4096,1024]{1,0:T(8,128)(2,1)S(1)} %get-tuple-element.30.held_ref), custom_call_target="tpu_custom_call" | custom-call | flops 1073741824 | bytes 8388608 | tf_op jit(solution)/shard_map/pallas_call | solution.py:167
  77.8 5.3 %collective-permute-start.12 = (f32[128,1024]{1,0:T(8,128)S(1)}, f32[128,1024]{1,0:T(8,128)S(1)}, u32[]{:S(2)}, u32[]{:S(2)}) collective-permute-start(f32[128,1024]{1,0:T(8,128)S(1)} %shard_map.56), channel_id=1, source_target_pairs={{0,256},{16,16},{32,160},{48,432},{64,448},{80,208},{96,96},{112,3... | collective-permute-start | bytes 1572872 | tf_op jit(solution)/shard_map/ppermute | solution.py:65
  83.1 0.0 collective-permute-done.13.near_ref
  83.1 1.9 %shard_map.57 = f32[128,1024]{1,0:T(8,128)S(1)} custom-call(s32[2]{0:T(128)S(1)} %pad_add_fusion.place_ref, bf16[64,4096]{1,0:T(8,128)(2,1)S(1)} %collective-permute-done.13.near_ref, bf16[64,4096]{1,0:T(8,128)(2,1)S(1)} %collective-permute-done.5.far_ref, bf16[4096,1024]{1,0:T(8,128)(2,1)S(1)} %get-tuple-element.30.held_ref), custom_call_target="tpu_custom_call" | custom-call | flops 1073741824 | bytes 8388608 | tf_op jit(solution)/shard_map/pallas_call | solution.py:167
  85.0 0.7 collective-permute-start.14
  85.7 0.0 collective-permute-done.9.far_ref
  85.7 0.0 collective-permute-done.10
  85.7 0.0 collective-permute-done.15.near_ref
  85.7 1.9 %shard_map.58 = f32[128,1024]{1,0:T(8,128)S(1)} custom-call(s32[2]{0:T(128)S(1)} %pad_add_fusion.place_ref, bf16[64,4096]{1,0:T(8,128)(2,1)S(1)} %collective-permute-done.15.near_ref, bf16[64,4096]{1,0:T(8,128)(2,1)S(1)} %collective-permute-done.9.far_ref, bf16[4096,1024]{1,0:T(8,128)(2,1)S(1)} %get-tuple-element.30.held_ref), custom_call_target="tpu_custom_call" | custom-call | flops 1073741824 | bytes 8388608 | tf_op jit(solution)/shard_map/pallas_call | solution.py:167
  87.6 1.9 %collective-permute-start.16 = (f32[128,1024]{1,0:T(8,128)S(1)}, f32[128,1024]{1,0:T(8,128)S(1)}, u32[]{:S(2)}, u32[]{:S(2)}) collective-permute-start(f32[128,1024]{1,0:T(8,128)S(1)} %shard_map.58), channel_id=1, source_target_pairs={{0,384},{16,272},{32,32},{48,176},{64,192},{80,80},{96,352},{112,4... | collective-permute-start | bytes 1572872 | tf_op jit(solution)/shard_map/ppermute | solution.py:65
  89.5 5.1 %collective-permute-done.12 = f32[128,1024]{1,0:T(8,128)S(1)} collective-permute-done((f32[128,1024]{1,0:T(8,128)S(1)}, f32[128,1024]{1,0:T(8,128)S(1)}, u32[]{:S(2)}, u32[]{:S(2)}) %collective-permute-start.12) | collective-permute-done | bytes 524320 | tf_op jit(solution)/shard_map/ppermute | solution.py:65
  94.6 0.0 collective-permute-done.14
  94.6 8.1 %collective-permute-done.16 = f32[128,1024]{1,0:T(8,128)S(1)} collective-permute-done((f32[128,1024]{1,0:T(8,128)S(1)}, f32[128,1024]{1,0:T(8,128)S(1)}, u32[]{:S(2)}, u32[]{:S(2)}) %collective-permute-start.16) | collective-permute-done | bytes 524320 | tf_op jit(solution)/shard_map/ppermute | solution.py:65
  102.6 1.0 add_add_fusion
  (6 shorter events, 0.1 us)
Async XLA Ops:
  0.0 9.9 %collective-permute-start = (bf16[16,2048]{1,0:T(8,128)(2,1)}, bf16[16,2048]{1,0:T(8,128)(2,1)S(1)}, u32[]{:S(2)}, u32[]{:S(2)}) collective-permute-start(bf16[16,2048]{1,0:T(8,128)(2,1)} %param.5), channel_id=1, source_target_pairs={{0,64},{64,0},{1,65},{65,1},{2,66},{66,2},{3,67},{67,3},{4,68},{68... | collective-permute-start | bytes 196616 | tf_op jit(solution)/shard_map/ppermute | solution.py:183
  9.9 49.2 %collective-permute-start.8 = (bf16[2048,1024]{1,0:T(8,128)(2,1)}, bf16[2048,1024]{1,0:T(8,128)(2,1)}, u32[]{:S(2)}, u32[]{:S(2)}) collective-permute-start(bf16[2048,1024]{1,0:T(8,128)(2,1)} %own_ref), channel_id=1, source_target_pairs={{0,64},{64,0},{1,65},{65,1},{2,66},{66,2},{3,67},{67,3},{4,68},{68... | collective-permute-start | bytes 12582920 | tf_op jit(solution)/shard_map/ppermute | solution.py:187
  12.1 15.4 %collective-permute-start.2 = (bf16[16,4096]{1,0:T(8,128)(2,1)S(1)}, bf16[16,4096]{1,0:T(8,128)(2,1)S(1)}, u32[]{:S(2)}, u32[]{:S(2)}) collective-permute-start(bf16[16,4096]{1,0:T(8,128)(2,1)S(1)} %constant_dynamic-update-slice_fusion.7), channel_id=1, source_target_pairs={{4,0},{5,1},{6,2},{7,3},{0,4},{1,5},{2,6},{3,7},{68,8},{69,9},{70,... | collective-permute-start | bytes 393224 | tf_op jit(solution)/shard_map/ppermute | solution.py:55
  19.3 17.6 %collective-permute-start.1 = (bf16[16,4096]{1,0:T(8,128)(2,1)S(1)}, bf16[16,4096]{1,0:T(8,128)(2,1)S(1)}, u32[]{:S(2)}, u32[]{:S(2)}) collective-permute-start(bf16[16,4096]{1,0:T(8,128)(2,1)S(1)} %constant_dynamic-update-slice_fusion.7), channel_id=1, source_target_pairs={{0,0},{1,1},{2,2},{3,3},{4,4},{5,5},{6,6},{7,7},{64,8},{65,9},{66,... | collective-permute-start | bytes 393224 | tf_op jit(solution)/shard_map/ppermute | solution.py:55
  37.0 8.1 %collective-permute-start.3 = (bf16[32,4096]{1,0:T(8,128)(2,1)S(1)}, bf16[32,4096]{1,0:T(8,128)(2,1)S(1)}, u32[]{:S(2)}, u32[]{:S(2)}) collective-permute-start(bf16[32,4096]{1,0:T(8,128)(2,1)S(1)} %get-tuple-element.34), channel_id=1, source_target_pairs={{0,1},{1,2},{2,3},{3,4},{4,5},{5,6},{6,7},{7,8},{8,9},{9,10},{10,1... | collective-permute-start | bytes 786440 | tf_op jit(solution)/shard_map/ppermute | solution.py:34
  38.9 13.0 %collective-permute-start.6 = (bf16[32,4096]{1,0:T(8,128)(2,1)S(1)}, bf16[32,4096]{1,0:T(8,128)(2,1)S(1)}, u32[]{:S(2)}, u32[]{:S(2)}) collective-permute-start(bf16[32,4096]{1,0:T(8,128)(2,1)S(1)} %get-tuple-element.34), channel_id=1, source_target_pairs={{0,2},{1,3},{2,4},{3,5},{4,6},{5,7},{6,8},{7,9},{8,10},{9,11},{10,... | collective-permute-start | bytes 786440 | tf_op jit(solution)/shard_map/ppermute | solution.py:34
  40.8 11.4 %collective-permute-start.7 = (bf16[32,4096]{1,0:T(8,128)(2,1)S(1)}, bf16[32,4096]{1,0:T(8,128)(2,1)S(1)}, u32[]{:S(2)}, u32[]{:S(2)}) collective-permute-start(bf16[32,4096]{1,0:T(8,128)(2,1)S(1)} %get-tuple-element.34), channel_id=1, source_target_pairs={{0,15},{1,0},{2,1},{3,2},{4,3},{5,4},{6,5},{7,6},{8,7},{9,8},{10,9... | collective-permute-start | bytes 786440 | tf_op jit(solution)/shard_map/ppermute | solution.py:34
  45.1 19.6 %collective-permute-start.4 = (bf16[64,4096]{1,0:T(8,128)(2,1)S(1)}, bf16[64,4096]{1,0:T(8,128)(2,1)S(1)}, u32[]{:S(2)}, u32[]{:S(2)}) collective-permute-start(bf16[64,4096]{1,0:T(8,128)(2,1)S(1)} %constant_dynamic-update-slice_fusion.2.far_ref), channel_id=1, source_target_pairs={{0,16},{16,32},{32,48},{48,0},{64,112},{80,64},{96,80},{112,96},{1... | collective-permute-start | bytes 1572872 | tf_op jit(solution)/shard_map/ppermute | solution.py:34
  49.3 15.4 %collective-permute-start.5 = (bf16[64,4096]{1,0:T(8,128)(2,1)S(1)}, bf16[64,4096]{1,0:T(8,128)(2,1)S(1)}, u32[]{:S(2)}, u32[]{:S(2)}) collective-permute-start(bf16[64,4096]{1,0:T(8,128)(2,1)S(1)} %constant_dynamic-update-slice_fusion.2.far_ref), channel_id=1, source_target_pairs={{0,48},{16,0},{32,16},{48,32},{64,80},{80,96},{96,112},{112,64},{1... | collective-permute-start | bytes 1572872 | tf_op jit(solution)/shard_map/ppermute | solution.py:34
  52.3 21.2 %collective-permute-start.11 = (bf16[64,4096]{1,0:T(8,128)(2,1)S(1)}, bf16[64,4096]{1,0:T(8,128)(2,1)S(1)}, u32[]{:S(2)}, u32[]{:S(2)}) collective-permute-start(bf16[64,4096]{1,0:T(8,128)(2,1)S(1)} %constant_dynamic-update-slice_fusion.5.near_ref), channel_id=1, source_target_pairs={{0,16},{16,32},{32,48},{48,0},{64,112},{80,64},{96,80},{112,96},{1... | collective-permute-start | bytes 1572872 | tf_op jit(solution)/shard_map/ppermute | solution.py:34
  57.2 25.9 %collective-permute-start.13 = (bf16[64,4096]{1,0:T(8,128)(2,1)S(1)}, bf16[64,4096]{1,0:T(8,128)(2,1)S(1)}, u32[]{:S(2)}, u32[]{:S(2)}) collective-permute-start(bf16[64,4096]{1,0:T(8,128)(2,1)S(1)} %constant_dynamic-update-slice_fusion.5.near_ref), channel_id=1, source_target_pairs={{0,48},{16,0},{32,16},{48,32},{64,80},{80,96},{96,112},{112,64},{1... | collective-permute-start | bytes 1572872 | tf_op jit(solution)/shard_map/ppermute | solution.py:34
  64.7 21.0 %collective-permute-start.9 = (bf16[64,4096]{1,0:T(8,128)(2,1)S(1)}, bf16[64,4096]{1,0:T(8,128)(2,1)S(1)}, u32[]{:S(2)}, u32[]{:S(2)}) collective-permute-start(bf16[64,4096]{1,0:T(8,128)(2,1)S(1)} %collective-permute-done.4.far_ref), channel_id=1, source_target_pairs={{0,16},{16,32},{32,48},{48,0},{64,112},{80,64},{96,80},{112,96},{1... | collective-permute-start | bytes 1572872 | tf_op jit(solution)/shard_map/ppermute | solution.py:34
  69.2 16.5 %collective-permute-start.10 = (f32[128,1024]{1,0:T(8,128)S(1)}, f32[128,1024]{1,0:T(8,128)S(1)}, u32[]{:S(2)}, u32[]{:S(2)}) collective-permute-start(f32[128,1024]{1,0:T(8,128)S(1)} %get-tuple-element.27), channel_id=1, source_target_pairs={{0,0},{16,144},{32,416},{48,304},{64,320},{80,464},{96,224},{112,1... | collective-permute-start | bytes 1572872 | tf_op jit(solution)/shard_map/ppermute | solution.py:65
  73.5 12.2 %collective-permute-start.15 = (bf16[64,4096]{1,0:T(8,128)(2,1)S(1)}, bf16[64,4096]{1,0:T(8,128)(2,1)S(1)}, u32[]{:S(2)}, u32[]{:S(2)}) collective-permute-start(bf16[64,4096]{1,0:T(8,128)(2,1)S(1)} %collective-permute-done.11.near_ref), channel_id=1, source_target_pairs={{0,16},{16,32},{32,48},{48,0},{64,112},{80,64},{96,80},{112,96},{1... | collective-permute-start | bytes 1572872 | tf_op jit(solution)/shard_map/ppermute | solution.py:34
  77.8 16.8 %collective-permute-start.12 = (f32[128,1024]{1,0:T(8,128)S(1)}, f32[128,1024]{1,0:T(8,128)S(1)}, u32[]{:S(2)}, u32[]{:S(2)}) collective-permute-start(f32[128,1024]{1,0:T(8,128)S(1)} %shard_map.56), channel_id=1, source_target_pairs={{0,256},{16,16},{32,160},{48,432},{64,448},{80,208},{96,96},{112,3... | collective-permute-start | bytes 1572872 | tf_op jit(solution)/shard_map/ppermute | solution.py:65
  85.0 9.6 %collective-permute-start.14 = (f32[128,1024]{1,0:T(8,128)S(1)}, f32[128,1024]{1,0:T(8,128)S(1)}, u32[]{:S(2)}, u32[]{:S(2)}) collective-permute-start(f32[128,1024]{1,0:T(8,128)S(1)} %shard_map.57), channel_id=1, source_target_pairs={{0,128},{16,400},{32,288},{48,48},{64,64},{80,336},{96,480},{112,2... | collective-permute-start | bytes 1572872 | tf_op jit(solution)/shard_map/ppermute | solution.py:65
  87.6 15.1 %collective-permute-start.16 = (f32[128,1024]{1,0:T(8,128)S(1)}, f32[128,1024]{1,0:T(8,128)S(1)}, u32[]{:S(2)}, u32[]{:S(2)}) collective-permute-start(f32[128,1024]{1,0:T(8,128)S(1)} %shard_map.58), channel_id=1, source_target_pairs={{0,384},{16,272},{32,32},{48,176},{64,192},{80,80},{96,352},{112,4... | collective-permute-start | bytes 1572872 | tf_op jit(solution)/shard_map/ppermute | solution.py:65

commit v6 on v5

--- a/solution.py
+++ b/solution.py
@@ -9,19 +9,31 @@
 HALF = Z // CORE
 TURN = ((0, 1, 3, 2), (2, 3, 1, 0))
 UNIT = 64
+COVER = 10**11
 CHUNKS = 4
 
 
+def partner_kernel(y_ref, label_ref, map_ref, partner_ref, by_label_ref):
+    levels, units = map_ref.shape[0], partner_ref.shape[0]
+    for label in range(levels):
+        by_label_ref[label] = sum(map_ref[label, level] * level for level in range(1, levels))
+    first = y_ref[0] * (units * UNIT)
+    for unit in range(units):
+        partner_ref[unit] = by_label_ref[label_ref[first + unit * UNIT]]
+
+
 def outer_labels_of(contract_irrep, outer_irrep, block_map, depth, cols):
-    first = lax.axis_index("y") * (CORE * depth)
     pair = lax.axis_index("x") * Z + lax.axis_index("z")
-    row_labels = lax.dynamic_slice_in_dim(contract_irrep, first, CORE * depth, 0)[::UNIT]
     col_labels = lax.dynamic_slice_in_dim(outer_irrep, pair * cols, cols, 0)
-    levels = jnp.arange(block_map.shape[0], dtype=jnp.int32)
-    partner = jnp.sum(block_map * levels[None, :], axis=1)
-    row_partner = jnp.sum(
-        jnp.where(row_labels[:, None] == levels[None, :], partner[None, :], 0), axis=1
-    )
+    smem = pl.BlockSpec(memory_space=pltpu.SMEM)
+    row_partner = pl.pallas_call(
+        partner_kernel,
+        out_shape=jax.ShapeDtypeStruct((CORE * depth // UNIT,), jnp.int32),
+        in_specs=[smem] * 3,
+        out_specs=smem,
+        scratch_shapes=[pltpu.SMEM((block_map.shape[0],), jnp.int32)],
+        cost_estimate=pl.CostEstimate(flops=COVER, bytes_accessed=0, transcendentals=0),
+    )(lax.axis_index("y").astype(jnp.int32).reshape(1), contract_irrep, block_map)
     return row_partner, col_labels.reshape(1, -1)
 
 
@@ -129,7 +141,9 @@
     depth, cols = own.shape
     height = 2 * near.shape[0]
     vmem, smem = (pl.BlockSpec(memory_space=m) for m in (pltpu.VMEM, pltpu.SMEM))
-    own, other = (pltpu.with_memory_space_constraint(v, pltpu.HBM) for v in (own, other))
+    own, other, rows = (
+        pltpu.with_memory_space_constraint(v, pltpu.HBM) for v in (own, other, rows)
+    )
     return pl.pallas_call(
         first_kernel,
         out_shape=(

time: 104 us -> 101 us (0.971)
  the two profiles are of different devices: /device:TPU:1 before, /device:TPU:4 now
where the time goes in v6:
time: 101 us
  starting transfers between devices  64.5 us (64%)
  waiting for transfers between devices  19.4 us (19%)
  Pallas kernels  13.6 us (13%)
  local copies, waits for them, and re-layouts  1.64 us (2%)
  other arithmetic  1.04 us (1%)
    ppermute x9, starting transfers between devices, apart(): return lax.ppermute(value, ('core', axis), pairs)  31.6 us
    ppermute x4, waiting for transfers between devices, hand_in(): return lax.ppermute(value, ('y', 'core', 'x'), pairs)  14.2 us
    ppermute x2, starting transfers between devices, spread(): return lax.ppermute(value, ('y', 'core', 'x', 'z'), pairs)  12.5 us
    ppermute x4, starting transfers between devices, hand_in(): return lax.ppermute(value, ('y', 'core', 'x'), pairs)  10.7 us
    ppermute x1, starting transfers between devices, body(): other = lax.ppermute(integrals, 'core', swap)  7.84 us
    pallas_call x1, Pallas kernels, first_product(): pl.pallas_call(first_kernel, out_shape=(pltpu.VMEM((CORE * depth, cols),...  5.64 us
    pallas_call x3, Pallas kernels, product(): pl.pallas_call(product_kernel, out_shape=jax.ShapeDtypeStruct((rows, cols...  5.52 us
    ppermute x9, waiting for transfers between devices, apart(): return lax.ppermute(value, ('core', axis), pairs)  4.63 us
  transfers between devices with their start and end apart: 17, of which 3 were waited for; matrix products, arithmetic and copies ran while one was open for 2% of the time, Pallas kernels for 14%

profile of v6, /device:TPU:4, one launch (start us, length us, event | category | flops | bytes accessed | tf_op | source)
XLA Modules:
  0.0 100.5 jit_solution(16149991783832257235)
XLA Ops:
  0.0 1.9 %collective-permute-start = (bf16[16,2048]{1,0:T(8,128)(2,1)}, bf16[16,2048]{1,0:T(8,128)(2,1)S(1)}, u32[]{:S(2)}, u32[]{:S(2)}) collective-permute-start(bf16[16,2048]{1,0:T(8,128)(2,1)} %param.5), channel_id=1, source_target_pairs={{0,64},{64,0},{1,65},{65,1},{2,66},{66,2},{3,67},{67,3},{4,68},{68... | collective-permute-start | bytes 196616 | tf_op jit(solution)/shard_map/ppermute | solution.py:197
  1.9 0.9 pad.4
  2.8 0.6 collective-permute-done
  3.4 9.7 %collective-permute-start.2 = (bf16[16,4096]{1,0:T(8,128)(2,1)S(1)}, bf16[16,4096]{1,0:T(8,128)(2,1)S(1)}, u32[]{:S(2)}, u32[]{:S(2)}) collective-permute-start(bf16[16,4096]{1,0:T(8,128)(2,1)S(1)} %constant_dynamic-update-slice_fusion.7), channel_id=1, source_target_pairs={{4,0},{5,1},{6,2},{7,3},{0,4},{1,5},{2,6},{3,7},{68,8},{69,9},{70,... | collective-permute-start | bytes 393224 | tf_op jit(solution)/shard_map/ppermute | solution.py:67
  13.1 2.7 %collective-permute-start.1 = (bf16[16,4096]{1,0:T(8,128)(2,1)S(1)}, bf16[16,4096]{1,0:T(8,128)(2,1)S(1)}, u32[]{:S(2)}, u32[]{:S(2)}) collective-permute-start(bf16[16,4096]{1,0:T(8,128)(2,1)S(1)} %constant_dynamic-update-slice_fusion.7), channel_id=1, source_target_pairs={{0,0},{1,1},{2,2},{3,3},{4,4},{5,5},{6,6},{7,7},{64,8},{65,9},{66,... | collective-permute-start | bytes 393224 | tf_op jit(solution)/shard_map/ppermute | solution.py:67
  15.8 7.8 %collective-permute-start.8 = (bf16[2048,1024]{1,0:T(8,128)(2,1)}, bf16[2048,1024]{1,0:T(8,128)(2,1)}, u32[]{:S(2)}, u32[]{:S(2)}) collective-permute-start(bf16[2048,1024]{1,0:T(8,128)(2,1)} %own_ref), channel_id=1, source_target_pairs={{0,64},{64,0},{1,65},{65,1},{2,66},{66,2},{3,67},{67,3},{4,68},{68... | collective-permute-start | bytes 12582920 | tf_op jit(solution)/shard_map/ppermute | solution.py:201
  23.7 2.5 %shard_map.55.row_ref = s32[64]{0:T(128)} custom-call(s32[1]{0:T(128)} %bitcast.y_ref, s32[16384]{0:T(1024)} %label_ref.1, s32[8,8]{1,0:T(8,128)} %map_ref.1), custom_call_target="tpu_custom_call" | custom-call | flops 99999997952 | tf_op jit(solution)/shard_map/pallas_call | solution.py:29
  26.2 0.7 dynamic_slice.3
  26.8 0.0 collective-permute-done.2
  26.8 0.0 collective-permute-done.1
  26.9 3.2 %collective-permute-start.3 = (bf16[32,4096]{1,0:T(8,128)(2,1)S(1)}, bf16[32,4096]{1,0:T(8,128)(2,1)S(1)}, u32[]{:S(2)}, u32[]{:S(2)}) collective-permute-start(bf16[32,4096]{1,0:T(8,128)(2,1)S(1)} %get-tuple-element.34), channel_id=1, source_target_pairs={{0,1},{1,2},{2,3},{3,4},{4,5},{5,6},{6,7},{7,8},{8,9},{9,10},{10,1... | collective-permute-start | bytes 786440 | tf_op jit(solution)/shard_map/ppermute | solution.py:46
  30.1 5.2 %collective-permute-start.6 = (bf16[32,4096]{1,0:T(8,128)(2,1)S(1)}, bf16[32,4096]{1,0:T(8,128)(2,1)S(1)}, u32[]{:S(2)}, u32[]{:S(2)}) collective-permute-start(bf16[32,4096]{1,0:T(8,128)(2,1)S(1)} %get-tuple-element.34), channel_id=1, source_target_pairs={{0,2},{1,3},{2,4},{3,5},{4,6},{5,7},{6,8},{7,9},{8,10},{9,11},{10,... | collective-permute-start | bytes 786440 | tf_op jit(solution)/shard_map/ppermute | solution.py:46
  35.3 3.2 %collective-permute-start.7 = (bf16[32,4096]{1,0:T(8,128)(2,1)S(1)}, bf16[32,4096]{1,0:T(8,128)(2,1)S(1)}, u32[]{:S(2)}, u32[]{:S(2)}) collective-permute-start(bf16[32,4096]{1,0:T(8,128)(2,1)S(1)} %get-tuple-element.34), channel_id=1, source_target_pairs={{0,15},{1,0},{2,1},{3,2},{4,3},{5,4},{6,5},{7,6},{8,7},{9,8},{10,9... | collective-permute-start | bytes 786440 | tf_op jit(solution)/shard_map/ppermute | solution.py:46
  38.5 0.0 collective-permute-done.3
  38.5 2.2 %collective-permute-start.4 = (bf16[64,4096]{1,0:T(8,128)(2,1)S(1)}, bf16[64,4096]{1,0:T(8,128)(2,1)S(1)}, u32[]{:S(2)}, u32[]{:S(2)}) collective-permute-start(bf16[64,4096]{1,0:T(8,128)(2,1)S(1)} %constant_dynamic-update-slice_fusion.2.far_ref), channel_id=1, source_target_pairs={{0,16},{16,32},{32,48},{48,0},{64,112},{80,64},{96,80},{112,96},{1... | collective-permute-start | bytes 1572872 | tf_op jit(solution)/shard_map/ppermute | solution.py:46
  40.7 3.7 %collective-permute-start.5 = (bf16[64,4096]{1,0:T(8,128)(2,1)S(1)}, bf16[64,4096]{1,0:T(8,128)(2,1)S(1)}, u32[]{:S(2)}, u32[]{:S(2)}) collective-permute-start(bf16[64,4096]{1,0:T(8,128)(2,1)S(1)} %constant_dynamic-update-slice_fusion.2.far_ref), channel_id=1, source_target_pairs={{0,48},{16,0},{32,16},{48,32},{64,80},{80,96},{96,112},{112,64},{1... | collective-permute-start | bytes 1572872 | tf_op jit(solution)/shard_map/ppermute | solution.py:46
  44.4 4.6 %collective-permute-done.6 = bf16[32,4096]{1,0:T(8,128)(2,1)S(1)} collective-permute-done((bf16[32,4096]{1,0:T(8,128)(2,1)S(1)}, bf16[32,4096]{1,0:T(8,128)(2,1)S(1)}, u32[]{:S(2)}, u32[]{:S(2)}) %collective-permute-start.6) | collective-permute-done | bytes 262176 | tf_op jit(solution)/shard_map/ppermute | solution.py:46
  49.0 0.0 collective-permute-done.7
  49.1 3.4 %collective-permute-start.11 = (bf16[64,4096]{1,0:T(8,128)(2,1)S(1)}, bf16[64,4096]{1,0:T(8,128)(2,1)S(1)}, u32[]{:S(2)}, u32[]{:S(2)}) collective-permute-start(bf16[64,4096]{1,0:T(8,128)(2,1)S(1)} %constant_dynamic-update-slice_fusion.5.near_ref), channel_id=1, source_target_pairs={{0,16},{16,32},{32,48},{48,0},{64,112},{80,64},{96,80},{112,96},{1... | collective-permute-start | bytes 1572872 | tf_op jit(solution)/shard_map/ppermute | solution.py:46
  52.4 0.1 pad_add_fusion.place_ref
  52.5 2.5 %collective-permute-start.13 = (bf16[64,4096]{1,0:T(8,128)(2,1)S(1)}, bf16[64,4096]{1,0:T(8,128)(2,1)S(1)}, u32[]{:S(2)}, u32[]{:S(2)}) collective-permute-start(bf16[64,4096]{1,0:T(8,128)(2,1)S(1)} %constant_dynamic-update-slice_fusion.5.near_ref), channel_id=1, source_target_pairs={{0,48},{16,0},{32,16},{48,32},{64,80},{80,96},{96,112},{112,64},{1... | collective-permute-start | bytes 1572872 | tf_op jit(solution)/shard_map/ppermute | solution.py:46
  55.0 0.0 collective-permute-done.8.other_ref
  55.0 5.6 %shard_map.56 = (bf16[4096,1024]{1,0:T(8,128)(2,1)S(1)}, f32[128,1024]{1,0:T(8,128)S(1)}) custom-call(s32[2]{0:T(128)S(1)} %pad_add_fusion.place_ref, s32[64]{0:T(128)} %shard_map.55.row_ref, s32[1,1024]{1,0:T(1,128)S(1)} %bitcast.4, bf16[2048,1024]{1,0:T(8,128)(2,1)} %own_ref, bf16[2048,1024]{1,0:T(8,128)(2,1)} %collective-permute-done.8.other_ref, ...), custom_call_target="tpu_custom_call" | custom-call | flops 1073741824 | bytes 16777216 | tf_op jit(solution)/shard_map/pallas_call | solution.py:147
  60.6 0.0 collective-permute-done.4.far_ref
  60.7 0.0 collective-permute-done.5.far_ref
  60.7 3.4 %collective-permute-start.9 = (bf16[64,4096]{1,0:T(8,128)(2,1)S(1)}, bf16[64,4096]{1,0:T(8,128)(2,1)S(1)}, u32[]{:S(2)}, u32[]{:S(2)}) collective-permute-start(bf16[64,4096]{1,0:T(8,128)(2,1)S(1)} %collective-permute-done.4.far_ref), channel_id=1, source_target_pairs={{0,16},{16,32},{32,48},{48,0},{64,112},{80,64},{96,80},{112,96},{1... | collective-permute-start | bytes 1572872 | tf_op jit(solution)/shard_map/ppermute | solution.py:46
  64.0 5.1 %collective-permute-start.10 = (f32[128,1024]{1,0:T(8,128)S(1)}, f32[128,1024]{1,0:T(8,128)S(1)}, u32[]{:S(2)}, u32[]{:S(2)}) collective-permute-start(f32[128,1024]{1,0:T(8,128)S(1)} %get-tuple-element.27), channel_id=1, source_target_pairs={{0,0},{16,144},{32,416},{48,304},{64,320},{80,464},{96,224},{112,1... | collective-permute-start | bytes 1572872 | tf_op jit(solution)/shard_map/ppermute | solution.py:77
  69.2 0.0 collective-permute-done.11.near_ref
  69.2 5.0 %collective-permute-start.15 = (bf16[64,4096]{1,0:T(8,128)(2,1)S(1)}, bf16[64,4096]{1,0:T(8,128)(2,1)S(1)}, u32[]{:S(2)}, u32[]{:S(2)}) collective-permute-start(bf16[64,4096]{1,0:T(8,128)(2,1)S(1)} %collective-permute-done.11.near_ref), channel_id=1, source_target_pairs={{0,16},{16,32},{32,48},{48,0},{64,112},{80,64},{96,80},{112,96},{1... | collective-permute-start | bytes 1572872 | tf_op jit(solution)/shard_map/ppermute | solution.py:46
  74.2 1.8 %shard_map.57 = f32[128,1024]{1,0:T(8,128)S(1)} custom-call(s32[2]{0:T(128)S(1)} %pad_add_fusion.place_ref, bf16[64,4096]{1,0:T(8,128)(2,1)S(1)} %collective-permute-done.11.near_ref, bf16[64,4096]{1,0:T(8,128)(2,1)S(1)} %collective-permute-done.4.far_ref, bf16[4096,1024]{1,0:T(8,128)(2,1)S(1)} %get-tuple-element.30.held_ref), custom_call_target="tpu_custom_call" | custom-call | flops 1073741824 | bytes 8388608 | tf_op jit(solution)/shard_map/pallas_call | solution.py:181
  76.0 1.9 %collective-permute-start.12 = (f32[128,1024]{1,0:T(8,128)S(1)}, f32[128,1024]{1,0:T(8,128)S(1)}, u32[]{:S(2)}, u32[]{:S(2)}) collective-permute-start(f32[128,1024]{1,0:T(8,128)S(1)} %shard_map.57), channel_id=1, source_target_pairs={{0,256},{16,16},{32,160},{48,432},{64,448},{80,208},{96,96},{112,3... | collective-permute-start | bytes 1572872 | tf_op jit(solution)/shard_map/ppermute | solution.py:77
  78.0 0.0 collective-permute-done.13.near_ref
  78.0 1.8 %shard_map.58 = f32[128,1024]{1,0:T(8,128)S(1)} custom-call(s32[2]{0:T(128)S(1)} %pad_add_fusion.place_ref, bf16[64,4096]{1,0:T(8,128)(2,1)S(1)} %collective-permute-done.13.near_ref, bf16[64,4096]{1,0:T(8,128)(2,1)S(1)} %collective-permute-done.5.far_ref, bf16[4096,1024]{1,0:T(8,128)(2,1)S(1)} %get-tuple-element.30.held_ref), custom_call_target="tpu_custom_call" | custom-call | flops 1073741824 | bytes 8388608 | tf_op jit(solution)/shard_map/pallas_call | solution.py:181
  79.8 3.0 %collective-permute-start.14 = (f32[128,1024]{1,0:T(8,128)S(1)}, f32[128,1024]{1,0:T(8,128)S(1)}, u32[]{:S(2)}, u32[]{:S(2)}) collective-permute-start(f32[128,1024]{1,0:T(8,128)S(1)} %shard_map.58), channel_id=1, source_target_pairs={{0,128},{16,400},{32,288},{48,48},{64,64},{80,336},{96,480},{112,2... | collective-permute-start | bytes 1572872 | tf_op jit(solution)/shard_map/ppermute | solution.py:77
  82.8 0.0 collective-permute-done.9.far_ref
  82.8 0.0 collective-permute-done.10
  82.8 0.0 collective-permute-done.15.near_ref
  82.8 1.9 %shard_map.59 = f32[128,1024]{1,0:T(8,128)S(1)} custom-call(s32[2]{0:T(128)S(1)} %pad_add_fusion.place_ref, bf16[64,4096]{1,0:T(8,128)(2,1)S(1)} %collective-permute-done.15.near_ref, bf16[64,4096]{1,0:T(8,128)(2,1)S(1)} %collective-permute-done.9.far_ref, bf16[4096,1024]{1,0:T(8,128)(2,1)S(1)} %get-tuple-element.30.held_ref), custom_call_target="tpu_custom_call" | custom-call | flops 1073741824 | bytes 8388608 | tf_op jit(solution)/shard_map/pallas_call | solution.py:181
  84.7 0.7 collective-permute-start.16
  85.4 14.2 %collective-permute-done.12 = f32[128,1024]{1,0:T(8,128)S(1)} collective-permute-done((f32[128,1024]{1,0:T(8,128)S(1)}, f32[128,1024]{1,0:T(8,128)S(1)}, u32[]{:S(2)}, u32[]{:S(2)}) %collective-permute-start.12) | collective-permute-done | bytes 524320 | tf_op jit(solution)/shard_map/ppermute | solution.py:77
  99.6 0.0 collective-permute-done.14
  99.6 0.0 collective-permute-done.16
  99.6 1.0 add_add_fusion
  (6 shorter events, 0.1 us)
Async XLA Ops:
  0.0 3.3 %collective-permute-start = (bf16[16,2048]{1,0:T(8,128)(2,1)}, bf16[16,2048]{1,0:T(8,128)(2,1)S(1)}, u32[]{:S(2)}, u32[]{:S(2)}) collective-permute-start(bf16[16,2048]{1,0:T(8,128)(2,1)} %param.5), channel_id=1, source_target_pairs={{0,64},{64,0},{1,65},{65,1},{2,66},{66,2},{3,67},{67,3},{4,68},{68... | collective-permute-start | bytes 196616 | tf_op jit(solution)/shard_map/ppermute | solution.py:197
  3.4 23.5 %collective-permute-start.2 = (bf16[16,4096]{1,0:T(8,128)(2,1)S(1)}, bf16[16,4096]{1,0:T(8,128)(2,1)S(1)}, u32[]{:S(2)}, u32[]{:S(2)}) collective-permute-start(bf16[16,4096]{1,0:T(8,128)(2,1)S(1)} %constant_dynamic-update-slice_fusion.7), channel_id=1, source_target_pairs={{4,0},{5,1},{6,2},{7,3},{0,4},{1,5},{2,6},{3,7},{68,8},{69,9},{70,... | collective-permute-start | bytes 393224 | tf_op jit(solution)/shard_map/ppermute | solution.py:67
  13.1 13.8 %collective-permute-start.1 = (bf16[16,4096]{1,0:T(8,128)(2,1)S(1)}, bf16[16,4096]{1,0:T(8,128)(2,1)S(1)}, u32[]{:S(2)}, u32[]{:S(2)}) collective-permute-start(bf16[16,4096]{1,0:T(8,128)(2,1)S(1)} %constant_dynamic-update-slice_fusion.7), channel_id=1, source_target_pairs={{0,0},{1,1},{2,2},{3,3},{4,4},{5,5},{6,6},{7,7},{64,8},{65,9},{66,... | collective-permute-start | bytes 393224 | tf_op jit(solution)/shard_map/ppermute | solution.py:67
  15.8 39.2 %collective-permute-start.8 = (bf16[2048,1024]{1,0:T(8,128)(2,1)}, bf16[2048,1024]{1,0:T(8,128)(2,1)}, u32[]{:S(2)}, u32[]{:S(2)}) collective-permute-start(bf16[2048,1024]{1,0:T(8,128)(2,1)} %own_ref), channel_id=1, source_target_pairs={{0,64},{64,0},{1,65},{65,1},{2,66},{66,2},{3,67},{67,3},{4,68},{68... | collective-permute-start | bytes 12582920 | tf_op jit(solution)/shard_map/ppermute | solution.py:201
  26.9 11.6 %collective-permute-start.3 = (bf16[32,4096]{1,0:T(8,128)(2,1)S(1)}, bf16[32,4096]{1,0:T(8,128)(2,1)S(1)}, u32[]{:S(2)}, u32[]{:S(2)}) collective-permute-start(bf16[32,4096]{1,0:T(8,128)(2,1)S(1)} %get-tuple-element.34), channel_id=1, source_target_pairs={{0,1},{1,2},{2,3},{3,4},{4,5},{5,6},{6,7},{7,8},{8,9},{9,10},{10,1... | collective-permute-start | bytes 786440 | tf_op jit(solution)/shard_map/ppermute | solution.py:46
  30.1 18.9 %collective-permute-start.6 = (bf16[32,4096]{1,0:T(8,128)(2,1)S(1)}, bf16[32,4096]{1,0:T(8,128)(2,1)S(1)}, u32[]{:S(2)}, u32[]{:S(2)}) collective-permute-start(bf16[32,4096]{1,0:T(8,128)(2,1)S(1)} %get-tuple-element.34), channel_id=1, source_target_pairs={{0,2},{1,3},{2,4},{3,5},{4,6},{5,7},{6,8},{7,9},{8,10},{9,11},{10,... | collective-permute-start | bytes 786440 | tf_op jit(solution)/shard_map/ppermute | solution.py:46
  35.3 13.8 %collective-permute-start.7 = (bf16[32,4096]{1,0:T(8,128)(2,1)S(1)}, bf16[32,4096]{1,0:T(8,128)(2,1)S(1)}, u32[]{:S(2)}, u32[]{:S(2)}) collective-permute-start(bf16[32,4096]{1,0:T(8,128)(2,1)S(1)} %get-tuple-element.34), channel_id=1, source_target_pairs={{0,15},{1,0},{2,1},{3,2},{4,3},{5,4},{6,5},{7,6},{8,7},{9,8},{10,9... | collective-permute-start | bytes 786440 | tf_op jit(solution)/shard_map/ppermute | solution.py:46
  38.5 22.1 %collective-permute-start.4 = (bf16[64,4096]{1,0:T(8,128)(2,1)S(1)}, bf16[64,4096]{1,0:T(8,128)(2,1)S(1)}, u32[]{:S(2)}, u32[]{:S(2)}) collective-permute-start(bf16[64,4096]{1,0:T(8,128)(2,1)S(1)} %constant_dynamic-update-slice_fusion.2.far_ref), channel_id=1, source_target_pairs={{0,16},{16,32},{32,48},{48,0},{64,112},{80,64},{96,80},{112,96},{1... | collective-permute-start | bytes 1572872 | tf_op jit(solution)/shard_map/ppermute | solution.py:46
  40.7 20.0 %collective-permute-start.5 = (bf16[64,4096]{1,0:T(8,128)(2,1)S(1)}, bf16[64,4096]{1,0:T(8,128)(2,1)S(1)}, u32[]{:S(2)}, u32[]{:S(2)}) collective-permute-start(bf16[64,4096]{1,0:T(8,128)(2,1)S(1)} %constant_dynamic-update-slice_fusion.2.far_ref), channel_id=1, source_target_pairs={{0,48},{16,0},{32,16},{48,32},{64,80},{80,96},{96,112},{112,64},{1... | collective-permute-start | bytes 1572872 | tf_op jit(solution)/shard_map/ppermute | solution.py:46
  49.1 20.1 %collective-permute-start.11 = (bf16[64,4096]{1,0:T(8,128)(2,1)S(1)}, bf16[64,4096]{1,0:T(8,128)(2,1)S(1)}, u32[]{:S(2)}, u32[]{:S(2)}) collective-permute-start(bf16[64,4096]{1,0:T(8,128)(2,1)S(1)} %constant_dynamic-update-slice_fusion.5.near_ref), channel_id=1, source_target_pairs={{0,16},{16,32},{32,48},{48,0},{64,112},{80,64},{96,80},{112,96},{1... | collective-permute-start | bytes 1572872 | tf_op jit(solution)/shard_map/ppermute | solution.py:46
  52.5 25.4 %collective-permute-start.13 = (bf16[64,4096]{1,0:T(8,128)(2,1)S(1)}, bf16[64,4096]{1,0:T(8,128)(2,1)S(1)}, u32[]{:S(2)}, u32[]{:S(2)}) collective-permute-start(bf16[64,4096]{1,0:T(8,128)(2,1)S(1)} %constant_dynamic-update-slice_fusion.5.near_ref), channel_id=1, source_target_pairs={{0,48},{16,0},{32,16},{48,32},{64,80},{80,96},{96,112},{112,64},{1... | collective-permute-start | bytes 1572872 | tf_op jit(solution)/shard_map/ppermute | solution.py:46
  60.7 22.1 %collective-permute-start.9 = (bf16[64,4096]{1,0:T(8,128)(2,1)S(1)}, bf16[64,4096]{1,0:T(8,128)(2,1)S(1)}, u32[]{:S(2)}, u32[]{:S(2)}) collective-permute-start(bf16[64,4096]{1,0:T(8,128)(2,1)S(1)} %collective-permute-done.4.far_ref), channel_id=1, source_target_pairs={{0,16},{16,32},{32,48},{48,0},{64,112},{80,64},{96,80},{112,96},{1... | collective-permute-start | bytes 1572872 | tf_op jit(solution)/shard_map/ppermute | solution.py:46
  64.0 18.8 %collective-permute-start.10 = (f32[128,1024]{1,0:T(8,128)S(1)}, f32[128,1024]{1,0:T(8,128)S(1)}, u32[]{:S(2)}, u32[]{:S(2)}) collective-permute-start(f32[128,1024]{1,0:T(8,128)S(1)} %get-tuple-element.27), channel_id=1, source_target_pairs={{0,0},{16,144},{32,416},{48,304},{64,320},{80,464},{96,224},{112,1... | collective-permute-start | bytes 1572872 | tf_op jit(solution)/shard_map/ppermute | solution.py:77
  69.2 13.7 %collective-permute-start.15 = (bf16[64,4096]{1,0:T(8,128)(2,1)S(1)}, bf16[64,4096]{1,0:T(8,128)(2,1)S(1)}, u32[]{:S(2)}, u32[]{:S(2)}) collective-permute-start(bf16[64,4096]{1,0:T(8,128)(2,1)S(1)} %collective-permute-done.11.near_ref), channel_id=1, source_target_pairs={{0,16},{16,32},{32,48},{48,0},{64,112},{80,64},{96,80},{112,96},{1... | collective-permute-start | bytes 1572872 | tf_op jit(solution)/shard_map/ppermute | solution.py:46
  76.0 23.5 %collective-permute-start.12 = (f32[128,1024]{1,0:T(8,128)S(1)}, f32[128,1024]{1,0:T(8,128)S(1)}, u32[]{:S(2)}, u32[]{:S(2)}) collective-permute-start(f32[128,1024]{1,0:T(8,128)S(1)} %shard_map.57), channel_id=1, source_target_pairs={{0,256},{16,16},{32,160},{48,432},{64,448},{80,208},{96,96},{112,3... | collective-permute-start | bytes 1572872 | tf_op jit(solution)/shard_map/ppermute | solution.py:77
  79.8 19.7 %collective-permute-start.14 = (f32[128,1024]{1,0:T(8,128)S(1)}, f32[128,1024]{1,0:T(8,128)S(1)}, u32[]{:S(2)}, u32[]{:S(2)}) collective-permute-start(f32[128,1024]{1,0:T(8,128)S(1)} %shard_map.58), channel_id=1, source_target_pairs={{0,128},{16,400},{32,288},{48,48},{64,64},{80,336},{96,480},{112,2... | collective-permute-start | bytes 1572872 | tf_op jit(solution)/shard_map/ppermute | solution.py:77
  84.7 14.9 %collective-permute-start.16 = (f32[128,1024]{1,0:T(8,128)S(1)}, f32[128,1024]{1,0:T(8,128)S(1)}, u32[]{:S(2)}, u32[]{:S(2)}) collective-permute-start(f32[128,1024]{1,0:T(8,128)S(1)} %shard_map.59), channel_id=1, source_target_pairs={{0,384},{16,272},{32,32},{48,176},{64,192},{80,80},{96,352},{112,4... | collective-permute-start | bytes 1572872 | tf_op jit(solution)/shard_map/ppermute | solution.py:77

commit v7 on v6

--- a/solution.py
+++ b/solution.py
@@ -10,7 +10,7 @@
 TURN = ((0, 1, 3, 2), (2, 3, 1, 0))
 UNIT = 64
 COVER = 10**11
-CHUNKS = 4
+CHUNKS = 2
 
 
 def partner_kernel(y_ref, label_ref, map_ref, partner_ref, by_label_ref):
@@ -225,7 +225,8 @@
     received.append(hand_in(product(place, near_ahead, far_ahead, held), -1))
     far_away, received[0] = lax.optimization_barrier((far_away, received[0]))
     received.append(hand_in(product(place, near_away, far_away, held), 2))
-    return (received[0] + received[1]) + (received[2] + received[3])
+    early, last = lax.optimization_barrier(((received[0] + received[1]) + received[2], received[3]))
+    return early + last
 
 
 def solution(mesh):

time: 101 us -> 101 us (level)
  no operation moved by 1% of the time
where the time goes in v7:
time: 101 us
  starting transfers between devices  64.6 us (64%)
  waiting for transfers between devices  19.3 us (19%)
  Pallas kernels  13.8 us (14%)
  local copies, waits for them, and re-layouts  1.64 us (2%)
  other arithmetic  1.03 us (1%)
    ppermute x9, starting transfers between devices, apart(): return lax.ppermute(value, ('core', axis), pairs)  31.6 us
    ppermute x4, waiting for transfers between devices, hand_in(): return lax.ppermute(value, ('y', 'core', 'x'), pairs)  14.1 us
    ppermute x2, starting transfers between devices, spread(): return lax.ppermute(value, ('y', 'core', 'x', 'z'), pairs)  12.5 us
    ppermute x4, starting transfers between devices, hand_in(): return lax.ppermute(value, ('y', 'core', 'x'), pairs)  10.7 us
    ppermute x1, starting transfers between devices, body(): other = lax.ppermute(integrals, 'core', swap)  7.84 us
    pallas_call x1, Pallas kernels, first_product(): pl.pallas_call(first_kernel, out_shape=(pltpu.VMEM((CORE * depth, cols),...  5.75 us
    pallas_call x3, Pallas kernels, product(): pl.pallas_call(product_kernel, out_shape=jax.ShapeDtypeStruct((rows, cols...  5.54 us
    ppermute x9, waiting for transfers between devices, apart(): return lax.ppermute(value, ('core', axis), pairs)  4.63 us
  transfers between devices with their start and end apart: 17, of which 3 were waited for; matrix products, arithmetic and copies ran while one was open for 2% of the time, Pallas kernels for 14%

profile of v7, /device:TPU:4, one launch (start us, length us, event | category | flops | bytes accessed | tf_op | source)
XLA Modules:
  0.0 100.7 jit_solution(16823684446265389464)
XLA Ops:
  0.0 1.9 %collective-permute-start = (bf16[16,2048]{1,0:T(8,128)(2,1)}, bf16[16,2048]{1,0:T(8,128)(2,1)S(1)}, u32[]{:S(2)}, u32[]{:S(2)}) collective-permute-start(bf16[16,2048]{1,0:T(8,128)(2,1)} %param.5), channel_id=1, source_target_pairs={{0,64},{64,0},{1,65},{65,1},{2,66},{66,2},{3,67},{67,3},{4,68},{68... | collective-permute-start | bytes 196616 | tf_op jit(solution)/shard_map/ppermute | solution.py:197
  1.9 0.9 pad.4
  2.8 0.6 collective-permute-done
  3.4 9.7 %collective-permute-start.2 = (bf16[16,4096]{1,0:T(8,128)(2,1)S(1)}, bf16[16,4096]{1,0:T(8,128)(2,1)S(1)}, u32[]{:S(2)}, u32[]{:S(2)}) collective-permute-start(bf16[16,4096]{1,0:T(8,128)(2,1)S(1)} %constant_dynamic-update-slice_fusion.7), channel_id=1, source_target_pairs={{4,0},{5,1},{6,2},{7,3},{0,4},{1,5},{2,6},{3,7},{68,8},{69,9},{70,... | collective-permute-start | bytes 393224 | tf_op jit(solution)/shard_map/ppermute | solution.py:67
  13.1 2.7 %collective-permute-start.1 = (bf16[16,4096]{1,0:T(8,128)(2,1)S(1)}, bf16[16,4096]{1,0:T(8,128)(2,1)S(1)}, u32[]{:S(2)}, u32[]{:S(2)}) collective-permute-start(bf16[16,4096]{1,0:T(8,128)(2,1)S(1)} %constant_dynamic-update-slice_fusion.7), channel_id=1, source_target_pairs={{0,0},{1,1},{2,2},{3,3},{4,4},{5,5},{6,6},{7,7},{64,8},{65,9},{66,... | collective-permute-start | bytes 393224 | tf_op jit(solution)/shard_map/ppermute | solution.py:67
  15.8 7.8 %collective-permute-start.8 = (bf16[2048,1024]{1,0:T(8,128)(2,1)}, bf16[2048,1024]{1,0:T(8,128)(2,1)}, u32[]{:S(2)}, u32[]{:S(2)}) collective-permute-start(bf16[2048,1024]{1,0:T(8,128)(2,1)} %own_ref), channel_id=1, source_target_pairs={{0,64},{64,0},{1,65},{65,1},{2,66},{66,2},{3,67},{67,3},{4,68},{68... | collective-permute-start | bytes 12582920 | tf_op jit(solution)/shard_map/ppermute | solution.py:201
  23.7 2.5 %shard_map.55.row_ref = s32[64]{0:T(128)} custom-call(s32[1]{0:T(128)} %bitcast.y_ref, s32[16384]{0:T(1024)} %label_ref.1, s32[8,8]{1,0:T(8,128)} %map_ref.1), custom_call_target="tpu_custom_call" | custom-call | flops 99999997952 | tf_op jit(solution)/shard_map/pallas_call | solution.py:29
  26.2 0.7 dynamic_slice.3
  26.8 0.0 collective-permute-done.2
  26.8 0.0 collective-permute-done.1
  26.9 3.2 %collective-permute-start.3 = (bf16[32,4096]{1,0:T(8,128)(2,1)S(1)}, bf16[32,4096]{1,0:T(8,128)(2,1)S(1)}, u32[]{:S(2)}, u32[]{:S(2)}) collective-permute-start(bf16[32,4096]{1,0:T(8,128)(2,1)S(1)} %get-tuple-element.38), channel_id=1, source_target_pairs={{0,1},{1,2},{2,3},{3,4},{4,5},{5,6},{6,7},{7,8},{8,9},{9,10},{10,1... | collective-permute-start | bytes 786440 | tf_op jit(solution)/shard_map/ppermute | solution.py:46
  30.1 5.2 %collective-permute-start.6 = (bf16[32,4096]{1,0:T(8,128)(2,1)S(1)}, bf16[32,4096]{1,0:T(8,128)(2,1)S(1)}, u32[]{:S(2)}, u32[]{:S(2)}) collective-permute-start(bf16[32,4096]{1,0:T(8,128)(2,1)S(1)} %get-tuple-element.38), channel_id=1, source_target_pairs={{0,2},{1,3},{2,4},{3,5},{4,6},{5,7},{6,8},{7,9},{8,10},{9,11},{10,... | collective-permute-start | bytes 786440 | tf_op jit(solution)/shard_map/ppermute | solution.py:46
  35.3 3.2 %collective-permute-start.7 = (bf16[32,4096]{1,0:T(8,128)(2,1)S(1)}, bf16[32,4096]{1,0:T(8,128)(2,1)S(1)}, u32[]{:S(2)}, u32[]{:S(2)}) collective-permute-start(bf16[32,4096]{1,0:T(8,128)(2,1)S(1)} %get-tuple-element.38), channel_id=1, source_target_pairs={{0,15},{1,0},{2,1},{3,2},{4,3},{5,4},{6,5},{7,6},{8,7},{9,8},{10,9... | collective-permute-start | bytes 786440 | tf_op jit(solution)/shard_map/ppermute | solution.py:46
  38.5 0.0 collective-permute-done.3
  38.5 2.2 %collective-permute-start.4 = (bf16[64,4096]{1,0:T(8,128)(2,1)S(1)}, bf16[64,4096]{1,0:T(8,128)(2,1)S(1)}, u32[]{:S(2)}, u32[]{:S(2)}) collective-permute-start(bf16[64,4096]{1,0:T(8,128)(2,1)S(1)} %constant_dynamic-update-slice_fusion.2.far_ref), channel_id=1, source_target_pairs={{0,16},{16,32},{32,48},{48,0},{64,112},{80,64},{96,80},{112,96},{1... | collective-permute-start | bytes 1572872 | tf_op jit(solution)/shard_map/ppermute | solution.py:46
  40.7 3.7 %collective-permute-start.5 = (bf16[64,4096]{1,0:T(8,128)(2,1)S(1)}, bf16[64,4096]{1,0:T(8,128)(2,1)S(1)}, u32[]{:S(2)}, u32[]{:S(2)}) collective-permute-start(bf16[64,4096]{1,0:T(8,128)(2,1)S(1)} %constant_dynamic-update-slice_fusion.2.far_ref), channel_id=1, source_target_pairs={{0,48},{16,0},{32,16},{48,32},{64,80},{80,96},{96,112},{112,64},{1... | collective-permute-start | bytes 1572872 | tf_op jit(solution)/shard_map/ppermute | solution.py:46
  44.4 4.6 %collective-permute-done.6 = bf16[32,4096]{1,0:T(8,128)(2,1)S(1)} collective-permute-done((bf16[32,4096]{1,0:T(8,128)(2,1)S(1)}, bf16[32,4096]{1,0:T(8,128)(2,1)S(1)}, u32[]{:S(2)}, u32[]{:S(2)}) %collective-permute-start.6) | collective-permute-done | bytes 262176 | tf_op jit(solution)/shard_map/ppermute | solution.py:46
  49.0 0.0 collective-permute-done.7
  49.1 3.4 %collective-permute-start.11 = (bf16[64,4096]{1,0:T(8,128)(2,1)S(1)}, bf16[64,4096]{1,0:T(8,128)(2,1)S(1)}, u32[]{:S(2)}, u32[]{:S(2)}) collective-permute-start(bf16[64,4096]{1,0:T(8,128)(2,1)S(1)} %constant_dynamic-update-slice_fusion.5.near_ref), channel_id=1, source_target_pairs={{0,16},{16,32},{32,48},{48,0},{64,112},{80,64},{96,80},{112,96},{1... | collective-permute-start | bytes 1572872 | tf_op jit(solution)/shard_map/ppermute | solution.py:46
  52.4 2.5 %collective-permute-start.13 = (bf16[64,4096]{1,0:T(8,128)(2,1)S(1)}, bf16[64,4096]{1,0:T(8,128)(2,1)S(1)}, u32[]{:S(2)}, u32[]{:S(2)}) collective-permute-start(bf16[64,4096]{1,0:T(8,128)(2,1)S(1)} %constant_dynamic-update-slice_fusion.5.near_ref), channel_id=1, source_target_pairs={{0,48},{16,0},{32,16},{48,32},{64,80},{80,96},{96,112},{112,64},{1... | collective-permute-start | bytes 1572872 | tf_op jit(solution)/shard_map/ppermute | solution.py:46
  54.9 0.1 pad_add_fusion.place_ref
  55.0 0.0 collective-permute-done.8.other_ref
  55.0 5.7 %shard_map.56 = (bf16[4096,1024]{1,0:T(8,128)(2,1)S(1)}, f32[128,1024]{1,0:T(8,128)S(1)}) custom-call(s32[2]{0:T(128)S(1)} %pad_add_fusion.place_ref, s32[64]{0:T(128)} %shard_map.55.row_ref, s32[1,1024]{1,0:T(1,128)S(1)} %bitcast.4, bf16[2048,1024]{1,0:T(8,128)(2,1)} %own_ref, bf16[2048,1024]{1,0:T(8,128)(2,1)} %collective-permute-done.8.other_ref, ...), custom_call_target="tpu_custom_call" | custom-call | flops 1073741824 | bytes 16777216 | tf_op jit(solution)/shard_map/pallas_call | solution.py:147
  60.8 0.0 collective-permute-done.4.far_ref
  60.8 0.0 collective-permute-done.5.far_ref
  60.8 3.4 %collective-permute-start.9 = (bf16[64,4096]{1,0:T(8,128)(2,1)S(1)}, bf16[64,4096]{1,0:T(8,128)(2,1)S(1)}, u32[]{:S(2)}, u32[]{:S(2)}) collective-permute-start(bf16[64,4096]{1,0:T(8,128)(2,1)S(1)} %collective-permute-done.4.far_ref), channel_id=1, source_target_pairs={{0,16},{16,32},{32,48},{48,0},{64,112},{80,64},{96,80},{112,96},{1... | collective-permute-start | bytes 1572872 | tf_op jit(solution)/shard_map/ppermute | solution.py:46
  64.2 5.1 %collective-permute-start.10 = (f32[128,1024]{1,0:T(8,128)S(1)}, f32[128,1024]{1,0:T(8,128)S(1)}, u32[]{:S(2)}, u32[]{:S(2)}) collective-permute-start(f32[128,1024]{1,0:T(8,128)S(1)} %get-tuple-element.29), channel_id=1, source_target_pairs={{0,0},{16,144},{32,416},{48,304},{64,320},{80,464},{96,224},{112,1... | collective-permute-start | bytes 1572872 | tf_op jit(solution)/shard_map/ppermute | solution.py:77
  69.3 0.0 collective-permute-done.11.near_ref
  69.3 5.0 %collective-permute-start.15 = (bf16[64,4096]{1,0:T(8,128)(2,1)S(1)}, bf16[64,4096]{1,0:T(8,128)(2,1)S(1)}, u32[]{:S(2)}, u32[]{:S(2)}) collective-permute-start(bf16[64,4096]{1,0:T(8,128)(2,1)S(1)} %collective-permute-done.11.near_ref), channel_id=1, source_target_pairs={{0,16},{16,32},{32,48},{48,0},{64,112},{80,64},{96,80},{112,96},{1... | collective-permute-start | bytes 1572872 | tf_op jit(solution)/shard_map/ppermute | solution.py:46
  74.3 1.8 %shard_map.57 = f32[128,1024]{1,0:T(8,128)S(1)} custom-call(s32[2]{0:T(128)S(1)} %pad_add_fusion.place_ref, bf16[64,4096]{1,0:T(8,128)(2,1)S(1)} %collective-permute-done.11.near_ref, bf16[64,4096]{1,0:T(8,128)(2,1)S(1)} %collective-permute-done.4.far_ref, bf16[4096,1024]{1,0:T(8,128)(2,1)S(1)} %get-tuple-element.32.held_ref), custom_call_target="tpu_custom_call" | custom-call | flops 1073741824 | bytes 8388608 | tf_op jit(solution)/shard_map/pallas_call | solution.py:181
  76.2 1.9 %collective-permute-start.12 = (f32[128,1024]{1,0:T(8,128)S(1)}, f32[128,1024]{1,0:T(8,128)S(1)}, u32[]{:S(2)}, u32[]{:S(2)}) collective-permute-start(f32[128,1024]{1,0:T(8,128)S(1)} %shard_map.57), channel_id=1, source_target_pairs={{0,256},{16,16},{32,160},{48,432},{64,448},{80,208},{96,96},{112,3... | collective-permute-start | bytes 1572872 | tf_op jit(solution)/shard_map/ppermute | solution.py:77
  78.1 0.0 collective-permute-done.13.near_ref
  78.1 1.8 %shard_map.58 = f32[128,1024]{1,0:T(8,128)S(1)} custom-call(s32[2]{0:T(128)S(1)} %pad_add_fusion.place_ref, bf16[64,4096]{1,0:T(8,128)(2,1)S(1)} %collective-permute-done.13.near_ref, bf16[64,4096]{1,0:T(8,128)(2,1)S(1)} %collective-permute-done.5.far_ref, bf16[4096,1024]{1,0:T(8,128)(2,1)S(1)} %get-tuple-element.32.held_ref), custom_call_target="tpu_custom_call" | custom-call | flops 1073741824 | bytes 8388608 | tf_op jit(solution)/shard_map/pallas_call | solution.py:181
  79.9 3.0 %collective-permute-start.14 = (f32[128,1024]{1,0:T(8,128)S(1)}, f32[128,1024]{1,0:T(8,128)S(1)}, u32[]{:S(2)}, u32[]{:S(2)}) collective-permute-start(f32[128,1024]{1,0:T(8,128)S(1)} %shard_map.58), channel_id=1, source_target_pairs={{0,128},{16,400},{32,288},{48,48},{64,64},{80,336},{96,480},{112,2... | collective-permute-start | bytes 1572872 | tf_op jit(solution)/shard_map/ppermute | solution.py:77
  83.0 0.0 collective-permute-done.9.far_ref
  83.0 0.0 collective-permute-done.10
  83.0 0.0 collective-permute-done.15.near_ref
  83.0 1.9 %shard_map.59 = f32[128,1024]{1,0:T(8,128)S(1)} custom-call(s32[2]{0:T(128)S(1)} %pad_add_fusion.place_ref, bf16[64,4096]{1,0:T(8,128)(2,1)S(1)} %collective-permute-done.15.near_ref, bf16[64,4096]{1,0:T(8,128)(2,1)S(1)} %collective-permute-done.9.far_ref, bf16[4096,1024]{1,0:T(8,128)(2,1)S(1)} %get-tuple-element.32.held_ref), custom_call_target="tpu_custom_call" | custom-call | flops 1073741824 | bytes 8388608 | tf_op jit(solution)/shard_map/pallas_call | solution.py:181
  84.9 0.7 collective-permute-start.16
  85.6 14.1 %collective-permute-done.12 = f32[128,1024]{1,0:T(8,128)S(1)} collective-permute-done((f32[128,1024]{1,0:T(8,128)S(1)}, f32[128,1024]{1,0:T(8,128)S(1)}, u32[]{:S(2)}, u32[]{:S(2)}) %collective-permute-start.12) | collective-permute-done | bytes 524320 | tf_op jit(solution)/shard_map/ppermute | solution.py:77
  99.7 0.0 collective-permute-done.14
  99.7 0.1 add_add_fusion
  99.8 0.0 collective-permute-done.16
  99.8 0.9 add.21
  (6 shorter events, 0.1 us)
Async XLA Ops:
  0.0 3.3 %collective-permute-start = (bf16[16,2048]{1,0:T(8,128)(2,1)}, bf16[16,2048]{1,0:T(8,128)(2,1)S(1)}, u32[]{:S(2)}, u32[]{:S(2)}) collective-permute-start(bf16[16,2048]{1,0:T(8,128)(2,1)} %param.5), channel_id=1, source_target_pairs={{0,64},{64,0},{1,65},{65,1},{2,66},{66,2},{3,67},{67,3},{4,68},{68... | collective-permute-start | bytes 196616 | tf_op jit(solution)/shard_map/ppermute | solution.py:197
  3.4 23.5 %collective-permute-start.2 = (bf16[16,4096]{1,0:T(8,128)(2,1)S(1)}, bf16[16,4096]{1,0:T(8,128)(2,1)S(1)}, u32[]{:S(2)}, u32[]{:S(2)}) collective-permute-start(bf16[16,4096]{1,0:T(8,128)(2,1)S(1)} %constant_dynamic-update-slice_fusion.7), channel_id=1, source_target_pairs={{4,0},{5,1},{6,2},{7,3},{0,4},{1,5},{2,6},{3,7},{68,8},{69,9},{70,... | collective-permute-start | bytes 393224 | tf_op jit(solution)/shard_map/ppermute | solution.py:67
  13.1 13.8 %collective-permute-start.1 = (bf16[16,4096]{1,0:T(8,128)(2,1)S(1)}, bf16[16,4096]{1,0:T(8,128)(2,1)S(1)}, u32[]{:S(2)}, u32[]{:S(2)}) collective-permute-start(bf16[16,4096]{1,0:T(8,128)(2,1)S(1)} %constant_dynamic-update-slice_fusion.7), channel_id=1, source_target_pairs={{0,0},{1,1},{2,2},{3,3},{4,4},{5,5},{6,6},{7,7},{64,8},{65,9},{66,... | collective-permute-start | bytes 393224 | tf_op jit(solution)/shard_map/ppermute | solution.py:67
  15.8 39.2 %collective-permute-start.8 = (bf16[2048,1024]{1,0:T(8,128)(2,1)}, bf16[2048,1024]{1,0:T(8,128)(2,1)}, u32[]{:S(2)}, u32[]{:S(2)}) collective-permute-start(bf16[2048,1024]{1,0:T(8,128)(2,1)} %own_ref), channel_id=1, source_target_pairs={{0,64},{64,0},{1,65},{65,1},{2,66},{66,2},{3,67},{67,3},{4,68},{68... | collective-permute-start | bytes 12582920 | tf_op jit(solution)/shard_map/ppermute | solution.py:201
  26.9 11.6 %collective-permute-start.3 = (bf16[32,4096]{1,0:T(8,128)(2,1)S(1)}, bf16[32,4096]{1,0:T(8,128)(2,1)S(1)}, u32[]{:S(2)}, u32[]{:S(2)}) collective-permute-start(bf16[32,4096]{1,0:T(8,128)(2,1)S(1)} %get-tuple-element.38), channel_id=1, source_target_pairs={{0,1},{1,2},{2,3},{3,4},{4,5},{5,6},{6,7},{7,8},{8,9},{9,10},{10,1... | collective-permute-start | bytes 786440 | tf_op jit(solution)/shard_map/ppermute | solution.py:46
  30.1 18.9 %collective-permute-start.6 = (bf16[32,4096]{1,0:T(8,128)(2,1)S(1)}, bf16[32,4096]{1,0:T(8,128)(2,1)S(1)}, u32[]{:S(2)}, u32[]{:S(2)}) collective-permute-start(bf16[32,4096]{1,0:T(8,128)(2,1)S(1)} %get-tuple-element.38), channel_id=1, source_target_pairs={{0,2},{1,3},{2,4},{3,5},{4,6},{5,7},{6,8},{7,9},{8,10},{9,11},{10,... | collective-permute-start | bytes 786440 | tf_op jit(solution)/shard_map/ppermute | solution.py:46
  35.3 13.8 %collective-permute-start.7 = (bf16[32,4096]{1,0:T(8,128)(2,1)S(1)}, bf16[32,4096]{1,0:T(8,128)(2,1)S(1)}, u32[]{:S(2)}, u32[]{:S(2)}) collective-permute-start(bf16[32,4096]{1,0:T(8,128)(2,1)S(1)} %get-tuple-element.38), channel_id=1, source_target_pairs={{0,15},{1,0},{2,1},{3,2},{4,3},{5,4},{6,5},{7,6},{8,7},{9,8},{10,9... | collective-permute-start | bytes 786440 | tf_op jit(solution)/shard_map/ppermute | solution.py:46
  38.5 22.2 %collective-permute-start.4 = (bf16[64,4096]{1,0:T(8,128)(2,1)S(1)}, bf16[64,4096]{1,0:T(8,128)(2,1)S(1)}, u32[]{:S(2)}, u32[]{:S(2)}) collective-permute-start(bf16[64,4096]{1,0:T(8,128)(2,1)S(1)} %constant_dynamic-update-slice_fusion.2.far_ref), channel_id=1, source_target_pairs={{0,16},{16,32},{32,48},{48,0},{64,112},{80,64},{96,80},{112,96},{1... | collective-permute-start | bytes 1572872 | tf_op jit(solution)/shard_map/ppermute | solution.py:46
  40.7 20.1 %collective-permute-start.5 = (bf16[64,4096]{1,0:T(8,128)(2,1)S(1)}, bf16[64,4096]{1,0:T(8,128)(2,1)S(1)}, u32[]{:S(2)}, u32[]{:S(2)}) collective-permute-start(bf16[64,4096]{1,0:T(8,128)(2,1)S(1)} %constant_dynamic-update-slice_fusion.2.far_ref), channel_id=1, source_target_pairs={{0,48},{16,0},{32,16},{48,32},{64,80},{80,96},{96,112},{112,64},{1... | collective-permute-start | bytes 1572872 | tf_op jit(solution)/shard_map/ppermute | solution.py:46
  49.1 20.2 %collective-permute-start.11 = (bf16[64,4096]{1,0:T(8,128)(2,1)S(1)}, bf16[64,4096]{1,0:T(8,128)(2,1)S(1)}, u32[]{:S(2)}, u32[]{:S(2)}) collective-permute-start(bf16[64,4096]{1,0:T(8,128)(2,1)S(1)} %constant_dynamic-update-slice_fusion.5.near_ref), channel_id=1, source_target_pairs={{0,16},{16,32},{32,48},{48,0},{64,112},{80,64},{96,80},{112,96},{1... | collective-permute-start | bytes 1572872 | tf_op jit(solution)/shard_map/ppermute | solution.py:46
  52.4 25.7 %collective-permute-start.13 = (bf16[64,4096]{1,0:T(8,128)(2,1)S(1)}, bf16[64,4096]{1,0:T(8,128)(2,1)S(1)}, u32[]{:S(2)}, u32[]{:S(2)}) collective-permute-start(bf16[64,4096]{1,0:T(8,128)(2,1)S(1)} %constant_dynamic-update-slice_fusion.5.near_ref), channel_id=1, source_target_pairs={{0,48},{16,0},{32,16},{48,32},{64,80},{80,96},{96,112},{112,64},{1... | collective-permute-start | bytes 1572872 | tf_op jit(solution)/shard_map/ppermute | solution.py:46
  60.8 22.2 %collective-permute-start.9 = (bf16[64,4096]{1,0:T(8,128)(2,1)S(1)}, bf16[64,4096]{1,0:T(8,128)(2,1)S(1)}, u32[]{:S(2)}, u32[]{:S(2)}) collective-permute-start(bf16[64,4096]{1,0:T(8,128)(2,1)S(1)} %collective-permute-done.4.far_ref), channel_id=1, source_target_pairs={{0,16},{16,32},{32,48},{48,0},{64,112},{80,64},{96,80},{112,96},{1... | collective-permute-start | bytes 1572872 | tf_op jit(solution)/shard_map/ppermute | solution.py:46
  64.2 18.8 %collective-permute-start.10 = (f32[128,1024]{1,0:T(8,128)S(1)}, f32[128,1024]{1,0:T(8,128)S(1)}, u32[]{:S(2)}, u32[]{:S(2)}) collective-permute-start(f32[128,1024]{1,0:T(8,128)S(1)} %get-tuple-element.29), channel_id=1, source_target_pairs={{0,0},{16,144},{32,416},{48,304},{64,320},{80,464},{96,224},{112,1... | collective-permute-start | bytes 1572872 | tf_op jit(solution)/shard_map/ppermute | solution.py:77
  69.3 13.7 %collective-permute-start.15 = (bf16[64,4096]{1,0:T(8,128)(2,1)S(1)}, bf16[64,4096]{1,0:T(8,128)(2,1)S(1)}, u32[]{:S(2)}, u32[]{:S(2)}) collective-permute-start(bf16[64,4096]{1,0:T(8,128)(2,1)S(1)} %collective-permute-done.11.near_ref), channel_id=1, source_target_pairs={{0,16},{16,32},{32,48},{48,0},{64,112},{80,64},{96,80},{112,96},{1... | collective-permute-start | bytes 1572872 | tf_op jit(solution)/shard_map/ppermute | solution.py:46
  76.2 23.5 %collective-permute-start.12 = (f32[128,1024]{1,0:T(8,128)S(1)}, f32[128,1024]{1,0:T(8,128)S(1)}, u32[]{:S(2)}, u32[]{:S(2)}) collective-permute-start(f32[128,1024]{1,0:T(8,128)S(1)} %shard_map.57), channel_id=1, source_target_pairs={{0,256},{16,16},{32,160},{48,432},{64,448},{80,208},{96,96},{112,3... | collective-permute-start | bytes 1572872 | tf_op jit(solution)/shard_map/ppermute | solution.py:77
  79.9 19.7 %collective-permute-start.14 = (f32[128,1024]{1,0:T(8,128)S(1)}, f32[128,1024]{1,0:T(8,128)S(1)}, u32[]{:S(2)}, u32[]{:S(2)}) collective-permute-start(f32[128,1024]{1,0:T(8,128)S(1)} %shard_map.58), channel_id=1, source_target_pairs={{0,128},{16,400},{32,288},{48,48},{64,64},{80,336},{96,480},{112,2... | collective-permute-start | bytes 1572872 | tf_op jit(solution)/shard_map/ppermute | solution.py:77
  84.9 14.9 %collective-permute-start.16 = (f32[128,1024]{1,0:T(8,128)S(1)}, f32[128,1024]{1,0:T(8,128)S(1)}, u32[]{:S(2)}, u32[]{:S(2)}) collective-permute-start(f32[128,1024]{1,0:T(8,128)S(1)} %shard_map.59), channel_id=1, source_target_pairs={{0,384},{16,272},{32,32},{48,176},{64,192},{80,80},{96,352},{112,4... | collective-permute-start | bytes 1572872 | tf_op jit(solution)/shard_map/ppermute | solution.py:77
